TPU v7x, 128 devices: a whole 4x4x4 slice. The times are simulated.
128 devices in a mesh: dp: 16 (over y, z), mp: 8 (over x, core).
Axes of the slice: x: 4, y: 4, z: 4, core: 2. Of those that a mesh axis runs over, the one named last changes fastest.
Arguments:
- activations: bfloat16 [16384, 4096], P('dp'), may hold values from -6 to 6
- gate_weight: bfloat16 [4096, 8192], P(None, 'mp'), may hold values from -0.09375 to 0.09375
- inner_weight: bfloat16 [4096, 8192], P(None, 'mp'), may hold values from -0.09375 to 0.09375
- state_proj: bfloat16 [4096, 256], replicated, may hold values from -0.09375 to 0.09375
- step_weight: bfloat16 [4096, 128], P(None, 'mp'), may hold values from -0.09375 to 0.09375
- inner_kernel: bfloat16 [4, 8192], P(None, 'mp'), may hold values from -3 to 3
- state_kernel: bfloat16 [4, 256], replicated, may hold values from -3 to 3
- step_bias: float32 [128], P('mp'), may hold values from -1.5 to 0.5
- decay_rate: float32 [128], P('mp'), may hold values from 0.002 to 0.1
- skip_scale: float32 [128], P('mp'), may hold values from 0.5 to 1.5
- norm_gain: bfloat16 [8192], P('mp'), may hold values from 0.099609375 to 1.8984375
- scan_cache: float32 [48, 128, 64, 128], P('dp', 'mp'), may hold values from -6 to 6
- window_cache: bfloat16 [48, 128, 192], P('dp', 'mp'), may hold values from -6 to 6
- state_history: bfloat16 [64, 3, 256], P('dp'), may hold values from -6 to 6
- hit_owner: int32 [64, 128], P('dp', 'mp'), may hold values from 0 to 15, as said below
- hit_slot: int32 [64, 128], P('dp', 'mp'), may hold values from 0 to 2
Outputs:
- normed: bfloat16 [16384, 8192], P('dp', 'mp')
- final_state: float32 [64, 128, 64, 128], P('dp', 'mp')
Inputs may be any that keep to these rules, and one draw needn't show every extreme that they name: Among the entries of hit_owner held by one device (its requests, its heads), no owner appears more than 8 times, and some owner appears exactly 8 times.
All inputs are finite; a program needn't handle non-finite values.
Results may differ from a plain program's by a relative error of at most 0.013.
Values sent between devices are 32-bit elements; how exact they have to be, the bound alone decides.
No kernel may reach another device: no remote copies, remote signals or barrier semaphores. Data moves between devices by JAX's collectives and lax.ppermute only.
A program may use at most 128 MiB of HBM per device.

v0:
```python
import functools

import jax
import jax.numpy as jnp
from jax import lax
from jax.experimental import pallas as pl
from jax.experimental.pallas import tpu as pltpu
from jax.sharding import PartitionSpec as P

EPSILON = 1e-05
CAP = 8
F32 = jnp.float32
BF16 = jnp.bfloat16
MIB = 1024 * 1024


def silu(v):
    half = 0.5 * v
    return half + half * jnp.tanh(half)


def full(shape, **kw):
    return pl.BlockSpec(shape, lambda *_: (0,) * len(shape), **kw)


def prep_kernel(owner_ref, slot_ref, wanted_ref, pos_ref, count_ref):
    owners = wanted_ref.shape[0]
    requests, heads = owner_ref.shape
    for o in range(owners):
        count_ref[o] = 0
        for k in range(CAP):
            wanted_ref[o, 0, k] = 0
    for r in range(requests):
        for h in range(heads):
            o = owner_ref[r, h]
            k = count_ref[o]
            count_ref[o] = k + 1
            wanted_ref[o, 0, k] = slot_ref[r, h] * heads + h
            pos_ref[r * heads + h] = o * CAP + k


def prep(hit_owner, hit_slot, owners):
    entries = hit_owner.size
    smem = pl.BlockSpec(memory_space=pltpu.SMEM)
    return pl.pallas_call(
        prep_kernel,
        out_shape=(
            jax.ShapeDtypeStruct((owners, 1, 128), jnp.int32),
            jax.ShapeDtypeStruct((entries,), jnp.int32),
        ),
        in_specs=[smem, smem],
        out_specs=(smem, smem),
        scratch_shapes=[pltpu.SMEM((owners,), jnp.int32)],
        name="prep",
    )(hit_owner, hit_slot)


def pick_kernel(codes_ref, cache_ref, out_ref):
    d = pl.program_id(0)
    for k in range(CAP):
        out_ref[0, k] = cache_ref[codes_ref[d, 0, k]]


def pick(codes, cache):
    owners = codes.shape[0]
    blocks, p, n = cache.shape
    return pl.pallas_call(
        pick_kernel,
        out_shape=jax.ShapeDtypeStruct((owners, CAP, p, n), F32),
        grid_spec=pltpu.PrefetchScalarGridSpec(
            num_scalar_prefetch=1,
            grid=(owners,),
            in_specs=[full((blocks, p, n), pipeline_mode=pl.Buffered(1))],
            out_specs=pl.BlockSpec((1, CAP, p, n), lambda d, c: (d, 0, 0, 0)),
        ),
        compiler_params=pltpu.CompilerParams(vmem_limit_bytes=8 * MIB),
        cost_estimate=pl.CostEstimate(flops=0, bytes_accessed=6 * MIB, transcendentals=0),
        name="pick",
    )(codes, cache)


TILE = 256


def project_kernel(steps, act_ref, wi_ref, wg_ref, ws_ref, wd_ref, inner_ref, gate_ref, state_ref, step_ref):
    j = pl.program_id(0)
    rows = act_ref.shape[0]
    chunk = 256

    def run(w_ref, out_ref):
        @pl.loop(0, rows // chunk)
        def _(m):
            at = pl.ds(pl.multiple_of(m * chunk, chunk), chunk)
            out_ref[at, :] = jnp.dot(act_ref[at, :], w_ref[...], preferred_element_type=F32).astype(out_ref.dtype)

    @pl.when(j == 0)
    def _():
        run(ws_ref, state_ref)
        run(wd_ref, step_ref)

    @pl.when((j > 0) & (j <= steps))
    def _():
        run(wi_ref, inner_ref)

    @pl.when(j > steps)
    def _():
        run(wg_ref, gate_ref)


def project(act, wi, wg, ws, wd):
    rows, depth = act.shape
    width = wi.shape[1]
    steps = width // TILE

    def at_inner(j):
        return (0, jnp.clip(j - 1, 0, steps - 1))

    def at_gate(j):
        return (0, jnp.clip(j - 1 - steps, 0, steps - 1))

    flops = 2 * rows * depth * (2 * width + ws.shape[1] + wd.shape[1])
    return pl.pallas_call(
        functools.partial(project_kernel, steps),
        out_shape=(
            jax.ShapeDtypeStruct((rows, width), BF16),
            jax.ShapeDtypeStruct((rows, width), BF16),
            jax.ShapeDtypeStruct((rows, ws.shape[1]), BF16),
            jax.ShapeDtypeStruct((rows, wd.shape[1]), F32),
        ),
        grid=(1 + 2 * steps,),
        in_specs=[
            full((rows, depth), pipeline_mode=pl.Buffered(1)),
            pl.BlockSpec((depth, TILE), at_inner),
            pl.BlockSpec((depth, TILE), at_gate),
            full(ws.shape, pipeline_mode=pl.Buffered(1)),
            full(wd.shape, pipeline_mode=pl.Buffered(1)),
        ],
        out_specs=(
            pl.BlockSpec((rows, TILE), at_inner),
            pl.BlockSpec((rows, TILE), at_gate),
            full((rows, ws.shape[1])),
            full((rows, wd.shape[1])),
        ),
        compiler_params=pltpu.CompilerParams(vmem_limit_bytes=36 * MIB),
        cost_estimate=pl.CostEstimate(flops=flops, bytes_accessed=32 * MIB, transcendentals=0),
        name="project",
    )(act, wi, wg, ws, wd)


def ssd_kernel(
    inner_ref,
    gate_ref,
    state_ref,
    step_ref,
    win_ref,
    hist_ref,
    ik_ref,
    sk_ref,
    bias_ref,
    decay_ref,
    skip_ref,
    az_ref,
    ez_ref,
    c_ref,
    f1_ref,
    el_ref,
    u_ref,
    v_ref,
):
    seq, width = inner_ref.shape
    heads = step_ref.shape[1]
    p = width // heads
    taps = ik_ref.shape[0]
    n = state_ref.shape[1] // 2
    lead = 8 - (taps - 1)
    half = seq // 2

    v_ref[lead:8, :] = hist_ref[0].astype(F32)
    v_ref[8:, :] = state_ref[...].astype(F32)
    sk = sk_ref[...].astype(F32)
    run = jnp.zeros((seq, 2 * n), F32)
    for k in range(taps):
        run = run + sk[k : k + 1] * v_ref[lead + k : lead + k + seq, :]
    conv = silu(run).astype(BF16)
    b = conv[:, :n]
    c = conv[:, n:]
    c_ref[...] = c

    raw = step_ref[...] + bias_ref[...]
    dt = jnp.maximum(raw, 0.0) + jnp.log1p(jnp.exp(-jnp.abs(raw)))
    dt = jnp.concatenate([dt, jnp.zeros((seq, 128 - heads), F32)], axis=1)
    decay = jnp.concatenate([decay_ref[...], jnp.zeros((1, 128 - heads), F32)], axis=1)
    t_at = lax.broadcasted_iota(jnp.int32, (seq, seq), 0)
    s_at = lax.broadcasted_iota(jnp.int32, (seq, seq), 1)
    causal = s_at <= t_at
    cum = jnp.dot(
        causal.astype(F32), -decay * dt, preferred_element_type=F32, precision=lax.Precision.HIGHEST
    )
    cum_t = cum.T
    dt_t = dt.T
    last = cum[seq - 1 : seq]
    spread = (
        lax.broadcasted_iota(jnp.int32, (128, width), 1) // p
        == lax.broadcasted_iota(jnp.int32, (128, width), 0)
    )
    spread = spread.astype(F32).astype(BF16)
    grown = jnp.exp(cum)
    tail = jnp.exp(last - cum) * dt
    el_ref[0] = jnp.broadcast_to(jnp.exp(cum_t[:heads, seq - 1 : seq]), (heads, n))

    scores = lax.dot_general(c, b, (((1,), (1,)), ((), ())), preferred_element_type=F32)
    scores = jnp.where(causal, scores, 0.0)
    top = scores[:half, :half]
    bottom = scores[half:]

    u_ref[lead:8, :] = win_ref[0]
    u_ref[8:, :] = inner_ref[...].astype(F32)
    lane = lax.broadcasted_iota(jnp.int32, (1, 128), 1)
    for q in range(width // 128):
        cols = slice(q * 128, q * 128 + 128)
        ik = ik_ref[:, cols].astype(F32)
        run = jnp.zeros((seq, 128), F32)
        for k in range(taps):
            run = run + ik[k : k + 1] * u_ref[lead + k : lead + k + seq, cols]
        x = silu(run).astype(BF16)
        xf = x.astype(F32)
        y_top = jnp.zeros((half, 128), F32)
        y_bottom = jnp.zeros((seq - half, 128), F32)
        for s in range(128 // p):
            h = q * (128 // p) + s
            own = (lane >= s * p) & (lane < (s + 1) * p)
            xs = jnp.where(own, xf, 0.0).astype(BF16)
            col = cum[:, h : h + 1]
            row = cum_t[h : h + 1]
            dr = dt_t[h : h + 1]
            w_top = jnp.exp(jnp.minimum(col[:half] - row[:, :half], 0.0)) * (top * dr[:, :half])
            w_bottom = jnp.exp(jnp.minimum(col[half:] - row, 0.0)) * (bottom * dr)
            y_top = y_top + jnp.dot(w_top.astype(BF16), xs[:half], preferred_element_type=F32)
            y_bottom = y_bottom + jnp.dot(w_bottom.astype(BF16), xs, preferred_element_type=F32)
        y = jnp.concatenate([y_top, y_bottom], axis=0) + skip_ref[:, cols] * xf
        z = silu(gate_ref[:, cols].astype(F32))
        az_ref[:, cols] = (y * z).astype(BF16)
        ez = jnp.dot(grown.astype(BF16), spread[:, cols], preferred_element_type=F32) * z
        ez_ref[:, cols] = ez.astype(BF16)
        tw = jnp.dot(tail.astype(BF16), spread[:, cols], preferred_element_type=F32)
        xt = (xf * tw).astype(BF16)
        f1_ref[0, cols, :] = lax.dot_general(
            xt, b, (((0,), (0,)), ((), ())), preferred_element_type=F32
        )


def ssd(inner, gate, state, step, window, history, ik, sk, bias, decay, skip):
    tokens, width = inner.shape
    requests = history.shape[0]
    seq = tokens // requests
    heads = step.shape[1]
    n2 = state.shape[1]
    n = n2 // 2
    rows = lambda w: pl.BlockSpec((seq, w), lambda r: (r, 0))
    per = lambda *s: pl.BlockSpec((1,) + s, lambda r: (r,) + (0,) * len(s))
    return pl.pallas_call(
        ssd_kernel,
        out_shape=(
            jax.ShapeDtypeStruct((tokens, width), BF16),
            jax.ShapeDtypeStruct((tokens, width), BF16),
            jax.ShapeDtypeStruct((tokens, n), BF16),
            jax.ShapeDtypeStruct((requests, width, n), F32),
            jax.ShapeDtypeStruct((requests, heads, n), F32),
        ),
        grid=(requests,),
        in_specs=[
            rows(width),
            rows(width),
            rows(n2),
            rows(heads),
            per(*window.shape[1:]),
            per(*history.shape[1:]),
            full(ik.shape),
            full(sk.shape),
            full(bias.shape),
            full(decay.shape),
            full(skip.shape),
        ],
        out_specs=(rows(width), rows(width), rows(n), per(width, n), per(heads, n)),
        scratch_shapes=[pltpu.VMEM((seq + 8, width), F32), pltpu.VMEM((seq + 8, n2), F32)],
        compiler_params=pltpu.CompilerParams(vmem_limit_bytes=32 * MIB),
        cost_estimate=pl.CostEstimate(
            flops=2 * tokens * width * seq * 2, bytes_accessed=14 * MIB, transcendentals=tokens * seq * heads
        ),
        name="ssd",
    )(inner, gate, state, step, window, history, ik, sk, bias, decay, skip)


def tail_kernel(pos_ref, back_ref, az_ref, ez_ref, c_ref, f1_ref, el_ref, g_ref, sq_ref, final_ref, s_ref):
    r = pl.program_id(0)
    heads, n = el_ref.shape[1:]
    p = back_ref.shape[1]
    seq, width = az_ref.shape
    for h in range(heads):
        block = back_ref[pos_ref[r * heads + h]]
        at = slice(h * p, h * p + p)
        final_ref[0, h] = el_ref[0, h : h + 1] * block + f1_ref[0, at]
        s_ref[at] = block.astype(BF16)
    c = c_ref[...]
    total = jnp.zeros((seq, 128), F32)
    for q in range(width // 256):
        cols = slice(q * 256, q * 256 + 256)
        seen = lax.dot_general(c, s_ref[cols], (((1,), (1,)), ((), ())), preferred_element_type=F32)
        g = az_ref[:, cols].astype(F32) + ez_ref[:, cols].astype(F32) * seen
        g_ref[:, cols] = g.astype(BF16)
        g2 = g * g
        total = total + g2[:, :128] + g2[:, 128:]

    @pl.when(r == 0)
    def _():
        sq_ref[...] = jnp.zeros_like(sq_ref)

    sq_ref[pl.ds(r, 1), :] = jnp.sum(total.T, axis=0, keepdims=True)


def tail(pos, back, az, ez, c, f1, el):
    requests, heads, n = el.shape
    tokens, width = az.shape
    p = back.shape[1]
    seq = tokens // requests
    rows = lambda w: pl.BlockSpec((seq, w), lambda r, _: (r, 0))
    per = lambda *s: pl.BlockSpec((1,) + s, lambda r, _: (r,) + (0,) * len(s))
    return pl.pallas_call(
        tail_kernel,
        out_shape=(
            jax.ShapeDtypeStruct((tokens, width), BF16),
            jax.ShapeDtypeStruct((8, seq), F32),
            jax.ShapeDtypeStruct((requests, heads, p, n), F32),
        ),
        grid_spec=pltpu.PrefetchScalarGridSpec(
            num_scalar_prefetch=1,
            grid=(requests,),
            in_specs=[
                full(back.shape, pipeline_mode=pl.Buffered(1)),
                rows(width),
                rows(width),
                rows(n),
                per(width, n),
                per(heads, n),
            ],
            out_specs=(rows(width), full((8, seq)), per(heads, p, n)),
            scratch_shapes=[pltpu.VMEM((width, n), BF16)],
        ),
        compiler_params=pltpu.CompilerParams(vmem_limit_bytes=24 * MIB),
        cost_estimate=pl.CostEstimate(
            flops=2 * tokens * width * n, bytes_accessed=14 * MIB, transcendentals=0
        ),
        name="tail",
    )(pos, back, az, ez, c, f1, el)


def norm_kernel(channels, g_ref, s0_ref, s1_ref, s2_ref, s3_ref, gain_ref, out_ref):
    r = pl.program_id(0)
    at = pl.ds(r, 1)
    seq, width = g_ref.shape
    square = s0_ref[at] + s1_ref[at] + s2_ref[at] + s3_ref[at]
    scale = lax.rsqrt(square / channels + EPSILON)
    scale = jnp.broadcast_to(scale, (128, seq)).T
    gain = gain_ref[...].astype(F32)
    for q in range(width // 128):
        cols = slice(q * 128, q * 128 + 128)
        out_ref[:, cols] = (g_ref[:, cols].astype(F32) * scale * gain[:, cols]).astype(BF16)


def normalise(g, parts, gain, channels):
    tokens, width = g.shape
    seq = parts[0].shape[1]
    rows = pl.BlockSpec((seq, width), lambda r: (r, 0))
    return pl.pallas_call(
        functools.partial(norm_kernel, channels),
        out_shape=jax.ShapeDtypeStruct((tokens, width), BF16),
        grid=(tokens // seq,),
        in_specs=[rows] + [full(parts[0].shape)] * 4 + [full(gain.shape)],
        out_specs=rows,
        compiler_params=pltpu.CompilerParams(vmem_limit_bytes=8 * MIB),
        cost_estimate=pl.CostEstimate(flops=2 * tokens * width, bytes_accessed=4 * MIB, transcendentals=0),
        name="normalise",
    )(g, *parts, gain)


def local(
    activations,
    gate_weight,
    inner_weight,
    state_proj,
    step_weight,
    inner_kernel,
    state_kernel,
    step_bias,
    decay_rate,
    skip_scale,
    norm_gain,
    scan_cache,
    window_cache,
    state_history,
    hit_owner,
    hit_slot,
):
    owners = lax.axis_size("dp")
    groups = lax.axis_size("mp")
    requests, heads = hit_owner.shape
    slots, _, p, n = scan_cache.shape
    width = inner_weight.shape[1]
    lead = inner_kernel.shape[0] - 1

    wanted, pos = prep(hit_owner, hit_slot, owners)
    codes = lax.all_to_all(wanted, "dp", split_axis=0, concat_axis=0, tiled=True)
    windows = lax.all_gather(window_cache.astype(F32), "dp", tiled=True)
    sent = pick(codes, scan_cache.reshape(slots * heads, p, n))
    back = lax.all_to_all(sent, "dp", split_axis=0, concat_axis=0, tiled=True)

    window = windows[hit_owner * slots + hit_slot, jnp.arange(heads)[None]]
    window = window.reshape(requests, heads, lead, p).transpose(0, 2, 1, 3).reshape(requests, lead, width)
    inner, gate, state, step = project(activations, inner_weight, gate_weight, state_proj, step_weight)
    az, ez, c, f1, el = ssd(
        inner,
        gate,
        state,
        step,
        window,
        state_history,
        inner_kernel,
        state_kernel,
        step_bias[None],
        decay_rate[None],
        jnp.repeat(skip_scale, p)[None],
    )
    g, square, final = tail(pos, back.reshape(owners * CAP, p, n), az, ez, c, f1, el)
    pair = [(i, i ^ 1) for i in range(groups)]
    square = square + lax.ppermute(square, "mp", pair)
    parts = [square] + [
        lax.ppermute(square, "mp", [(i, (i + 2 * s) % groups) for i in range(groups)])
        for s in range(1, groups // 2)
    ]
    normed = normalise(g, parts, norm_gain[None], width * groups)
    return normed, final


def solution(mesh):
    placed = (
        P("dp", None),
        P(None, "mp"),
        P(None, "mp"),
        P(),
        P(None, "mp"),
        P(None, "mp"),
        P(),
        P("mp"),
        P("mp"),
        P("mp"),
        P("mp"),
        P("dp", "mp", None, None),
        P("dp", "mp", None),
        P("dp", None, None),
        P("dp", "mp"),
        P("dp", "mp"),
    )
    return jax.shard_map(
        local,
        mesh=mesh,
        in_specs=placed,
        out_specs=(P("dp", "mp"), P("dp", "mp", None, None)),
        check_vma=False,
    )
```

profile of v0, /device:TPU:0, one launch (start us, length us, event | category | flops | bytes accessed | tf_op | source)
XLA Modules:
  0.0 171.7 jit_solution(8639733573574802605)
XLA Ops:
  0.6 1.8 %prep.1 = (s32[16,1,128]{2,1,0:T(1,128)}, s32[64]{0:T(128)}) custom-call(s32[4,16]{1,0:T(4,128)} %owner_ref.1, s32[4,16]{1,0:T(4,128)} %slot_ref.1), custom_call_target="tpu_custom_call" | custom-call | tf_op jit(solution)/shard_map/prep/pallas_call | solution.py:45
  2.4 15.6 %all_to_all.10.codes_ref = s32[16,1,128]{2,1,0:T(1,128)S(1)} all-to-all(s32[16,1,128]{2,1,0:T(1,128)} %get-tuple-element.17), channel_id=1, replica_groups=mesh['dp'=16,'mp'=8] {'dp'}, dimensions={0} | all-to-all | bytes 16384 | tf_op jit(solution)/shard_map/all_to_all | solution.py:412
  18.1 1.4 copy-done.5
  19.5 1.2 pick.1
  20.7 2.0 %copy-done = f32[16,8,64,128]{3,2,1,0:T(8,128)} copy-done((f32[16,8,64,128]{3,2,1,0:T(8,128)}, f32[16,8,64,128]{3,2,1,0:T(8,128)S(1)}, u32[]{:S(2)}) %copy-start) | copy-done | bytes 4194328
  22.7 4.7 %all-to-all-start.1 = ((f32[16,8,64,128]{3,2,1,0:T(8,128)}), f32[16,8,64,128]{3,2,1,0:T(8,128)}, u32[]{:S(2)}, u32[]{:S(2)}) async-start(f32[16,8,64,128]{3,2,1,0:T(8,128)} %copy-done), calls=%async_computation.1 | async-start | bytes 8388608 | tf_op jit(solution)/shard_map/all_to_all | solution.py:415
  27.4 0.0 copy-start.19
  27.4 0.5 copy.25.wd_ref
  28.0 0.1 reshape.23
  28.0 68.6 %all_gather.3 = f32[48,16,192]{2,1,0:T(8,128)S(1)} all-gather(f32[3,16,192]{2,1,0:T(8,128)S(1)} %convert_element_type.3), channel_id=1, replica_groups=mesh['dp'=16,'mp'=8] {'dp'}, dimensions={0}, use_global_device_ids=true | all-gather | bytes 626688 | tf_op jit(solution)/shard_map/all_gather | solution.py:413
  96.6 0.9 gather_fusion
  97.5 0.1 reshape.21
  97.7 0.1 reshape.35.win_ref
  97.8 0.1 broadcast_in_dim.25
  97.9 0.1 broadcast_in_dim_reshape.3.skip_ref
  97.9 0.0 copy-start.7
  98.0 3.4 %copy-done.7 = bf16[1024,4096]{1,0:T(8,128)(2,1)S(1)} copy-done((bf16[1024,4096]{1,0:T(8,128)(2,1)S(1)}, bf16[1024,4096]{1,0:T(8,128)(2,1)}, u32[]{:S(2)}) %copy-start.7) | copy-done | bytes 8388632
  101.3 1.6 copy-done.8
  102.9 31.6 %project.1 = (bf16[1024,1024]{1,0:T(8,128)(2,1)S(1)}, bf16[1024,1024]{1,0:T(8,128)(2,1)S(1)}, bf16[1024,256]{1,0:T(8,128)(2,1)S(1)}, f32[1024,16]{1,0:T(8,128)S(1)}) custom-call(bf16[1024,4096]{1,0:T(8,128)(2,1)S(1)} %copy-done.7, bf16[4096,1024]{1,0:T(8,128)(2,1)} %wi_ref.1, bf16[4096,1024]{1,0:T(8,128)(2,1)} %wg_ref.1, bf16[4096,256]{1,0:T(8,128)(2,1)S(1)} %copy-done.8, ...), custom_call_target="tpu_custom_call" | custom-call | flops 19461570560 | bytes 33554432 | tf_op jit(solution)/shard_map/project/pallas_call | solution.py:122
  134.6 14.3 %ssd.1 = (bf16[1024,1024]{1,0:T(8,128)(2,1)S(1)}, bf16[1024,1024]{1,0:T(8,128)(2,1)S(1)}, bf16[1024,128]{1,0:T(8,128)(2,1)S(1)}, f32[4,1024,128]{2,1,0:T(8,128)S(1)}, f32[4,16,128]{2,1,0:T(8,128)S(1)}) custom-call(bf16[1024,1024]{1,0:T(8,128)(2,1)S(1)} %get-tuple-element.18.inner_ref, bf16[1024,1024]{1,0:T(8,128)(2,1)S(1)} %get-tuple-element.19.gate_ref, ...), custom_call_target="tpu_custom_call" | custom-call | flops 1073741824 | bytes 14680064 | tf_op jit(solution)/shard_map/ssd/pallas_call | solution.py:261
  148.9 1.3 copy-done.1
  150.2 1.3 copy-done.3
  151.5 1.6 copy-done.2
  153.1 1.6 copy-done.4
  154.7 5.7 %tail.1 = (bf16[1024,1024]{1,0:T(8,128)(2,1)S(1)}, f32[8,256]{1,0:T(8,128)S(1)}, f32[4,16,64,128]{3,2,1,0:T(8,128)}) custom-call(s32[64]{0:T(128)S(1)} %copy-done.6, f32[128,64,128]{2,1,0:T(8,128)} %bitcast.1.back_ref, bf16[1024,1024]{1,0:T(8,128)(2,1)S(1)} %get-tuple-element.22.az_ref, bf16[1024,1024]{1,0:T(8,128)(2,1)S(1)} %copy-done.2, ...), custom_call_target="tpu_custom_call" | custom-call | flops 268435456 | bytes 14680064 | tf_op jit(solution)/shard_map/tail/pallas_call | solution.py:328
  160.4 1.2 collective-permute-done
  161.6 1.5 collective-permute-start.1
  163.1 2.7 %collective-permute-start.2 = (f32[8,256]{1,0:T(8,128)S(1)}, f32[8,256]{1,0:T(8,128)S(1)}, u32[]{:S(2)}, u32[]{:S(2)}) collective-permute-start(f32[8,256]{1,0:T(8,128)S(1)} %add.16.s0_ref), channel_id=1, source_target_pairs={{0,4},{1,5},{2,6},{3,7},{4,0},{5,1},{6,2},{7,3},{8,12},{9,13},{10,... | collective-permute-start | bytes 24584 | tf_op jit(solution)/shard_map/ppermute | solution.py:437
  165.8 1.4 collective-permute-start.3
  167.3 1.0 collective-permute-done.2.s2_ref
  168.2 1.2 collective-permute-done.3.s3_ref
  169.5 2.3 %normalise.1 = bf16[1024,1024]{1,0:T(8,128)(2,1)} custom-call(bf16[1024,1024]{1,0:T(8,128)(2,1)S(1)} %get-tuple-element.27.g_ref, f32[8,256]{1,0:T(8,128)S(1)} %add.16.s0_ref, f32[8,256]{1,0:T(8,128)S(1)} %collective-permute-done.1.s1_ref, f32[8,256]{1,0:T(8,128)S(1)} %collective-permute-done.2.s2_ref, f32[8,256]{1,0:T(8,128)S(1)} %collective-permute-done.3.s3_ref, ...), custom_call_target="tpu_custom_call" | custom-call | flops 2097152 | bytes 4194304 | tf_op jit(solution)/shard_map/normalise/pallas_call | solution.py:374
  (39 shorter events, 0.1 us)
Async XLA Ops:
  18.1 1.4 copy-start.5
  20.7 2.0 %copy-start = (f32[16,8,64,128]{3,2,1,0:T(8,128)}, f32[16,8,64,128]{3,2,1,0:T(8,128)S(1)}, u32[]{:S(2)}) copy-start(f32[16,8,64,128]{3,2,1,0:T(8,128)S(1)} %pick.1) | copy-start | bytes 12582916
  22.7 4.7 %copy-start.13 = (bf16[4096,16]{0,1:T(8,128)(2,1)S(1)}, bf16[4096,16]{0,1:T(8,128)(2,1)}, u32[]{:S(2)}) copy-start(bf16[4096,16]{0,1:T(8,128)(2,1)} %param.20) | copy-start | bytes 393220
  22.7 5.2 %copy-start.14 = (bf16[3,16,192]{2,1,0:T(8,128)(2,1)S(1)}, bf16[3,16,192]{2,1,0:T(8,128)(2,1)}, u32[]{:S(2)}) copy-start(bf16[3,16,192]{2,1,0:T(8,128)(2,1)} %param.28) | copy-start | bytes 55300
  22.7 5.2 %copy-start.15 = (s32[4,16]{1,0:T(4,128)S(1)}, s32[4,16]{1,0:T(4,128)}, u32[]{:S(2)}) copy-start(s32[4,16]{1,0:T(4,128)} %owner_ref.1) | copy-start | bytes 772
  22.7 5.2 %copy-start.16 = (s32[4,16]{1,0:T(4,128)S(1)}, s32[4,16]{1,0:T(4,128)}, u32[]{:S(2)}) copy-start(s32[4,16]{1,0:T(4,128)} %slot_ref.1) | copy-start | bytes 772
  22.7 128.8 %all-to-all-start.1 = ((f32[16,8,64,128]{3,2,1,0:T(8,128)}), f32[16,8,64,128]{3,2,1,0:T(8,128)}, u32[]{:S(2)}, u32[]{:S(2)}) async-start(f32[16,8,64,128]{3,2,1,0:T(8,128)} %copy-done), calls=%async_computation.1 | async-start | bytes 8388608 | tf_op jit(solution)/shard_map/all_to_all | solution.py:415
  27.4 70.4 %copy-start.19 = (f32[16]{0:T(128)S(1)}, f32[16]{0:T(128)}, u32[]{:S(2)}) copy-start(f32[16]{0:T(128)} %param.25) | copy-start | bytes 196
  27.4 70.5 %copy-start.17 = (bf16[4,3,256]{2,0,1:T(4,128)(2,1)S(1)}, bf16[4,3,256]{2,0,1:T(4,128)(2,1)}, u32[]{:S(2)}) copy-start(bf16[4,3,256]{2,0,1:T(4,128)(2,1)} %param.29) | copy-start | bytes 18436
  97.9 3.4 %copy-start.7 = (bf16[1024,4096]{1,0:T(8,128)(2,1)S(1)}, bf16[1024,4096]{1,0:T(8,128)(2,1)}, u32[]{:S(2)}) copy-start(bf16[1024,4096]{1,0:T(8,128)(2,1)} %act_ref.1) | copy-start | bytes 25165828
  101.3 1.6 copy-start.8
  102.9 31.6 %copy-start.9 = (bf16[4,1024]{1,0:T(4,128)(2,1)S(1)}, bf16[4,1024]{1,0:T(4,128)(2,1)}, u32[]{:S(2)}) copy-start(bf16[4,1024]{1,0:T(4,128)(2,1)} %ik_ref.1) | copy-start | bytes 24580
  102.9 31.6 %copy-start.10 = (bf16[4,256]{1,0:T(4,128)(2,1)S(1)}, bf16[4,256]{1,0:T(4,128)(2,1)}, u32[]{:S(2)}) copy-start(bf16[4,256]{1,0:T(4,128)(2,1)} %sk_ref.1) | copy-start | bytes 6148
  102.9 31.6 %copy-start.11 = (f32[16]{0:T(128)S(1)}, f32[16]{0:T(128)}, u32[]{:S(2)}) copy-start(f32[16]{0:T(128)} %param.23) | copy-start | bytes 196
  102.9 31.6 %copy-start.12 = (f32[16]{0:T(128)S(1)}, f32[16]{0:T(128)}, u32[]{:S(2)}) copy-start(f32[16]{0:T(128)} %param.24) | copy-start | bytes 196
  134.6 16.9 %copy-start.6 = (s32[64]{0:T(128)S(1)}, s32[64]{0:T(128)}, u32[]{:S(2)}) copy-start(s32[64]{0:T(128)} %get-tuple-element.16.pos_ref) | copy-start | bytes 772
  148.9 1.3 copy-start.1
  150.2 1.3 copy-start.3
  151.5 1.6 copy-start.2
  153.1 1.6 copy-start.4
  154.7 12.6 %copy-start.18 = (bf16[1024]{0:T(1024)(128)(2,1)S(1)}, bf16[1024]{0:T(1024)(128)(2,1)}, u32[]{:S(2)}) copy-start(bf16[1024]{0:T(1024)(128)(2,1)} %param.26) | copy-start | bytes 6148
  160.4 1.2 collective-permute-start
  161.6 5.7 %collective-permute-start.1 = (f32[8,256]{1,0:T(8,128)S(1)}, f32[8,256]{1,0:T(8,128)S(1)}, u32[]{:S(2)}, u32[]{:S(2)}) collective-permute-start(f32[8,256]{1,0:T(8,128)S(1)} %add.16.s0_ref), channel_id=1, source_target_pairs={{0,2},{1,3},{2,4},{3,5},{4,6},{5,7},{6,0},{7,1},{8,10},{9,11},{10,... | collective-permute-start | bytes 24584 | tf_op jit(solution)/shard_map/ppermute | solution.py:437
  163.1 5.2 %collective-permute-start.2 = (f32[8,256]{1,0:T(8,128)S(1)}, f32[8,256]{1,0:T(8,128)S(1)}, u32[]{:S(2)}, u32[]{:S(2)}) collective-permute-start(f32[8,256]{1,0:T(8,128)S(1)} %add.16.s0_ref), channel_id=1, source_target_pairs={{0,4},{1,5},{2,6},{3,7},{4,0},{5,1},{6,2},{7,3},{8,12},{9,13},{10,... | collective-permute-start | bytes 24584 | tf_op jit(solution)/shard_map/ppermute | solution.py:437
  165.8 3.7 %collective-permute-start.3 = (f32[8,256]{1,0:T(8,128)S(1)}, f32[8,256]{1,0:T(8,128)S(1)}, u32[]{:S(2)}, u32[]{:S(2)}) collective-permute-start(f32[8,256]{1,0:T(8,128)S(1)} %add.16.s0_ref), channel_id=1, source_target_pairs={{0,6},{1,7},{2,0},{3,1},{4,2},{5,3},{6,4},{7,5},{8,14},{9,15},{10,... | collective-permute-start | bytes 24584 | tf_op jit(solution)/shard_map/ppermute | solution.py:437
where the time goes:
time: 172 us
  blocking collectives  84.2 us (49%)
  Pallas kernels  56.8 us (33%)
  local copies, waits for them, and re-layouts  16.1 us (9%)
  starting transfers between devices  10.3 us (6%)
  waiting for transfers between devices  3.37 us (2%)
    all_gather x1, blocking collectives, local(): windows = lax.all_gather(window_cache.astype(F32), 'dp', tiled=True)  68.6 us
    pallas_call x1, Pallas kernels, project(): pl.pallas_call(functools.partial(project_kernel, steps), out_shape=(jax.S...  31.6 us
    all_to_all x1, blocking collectives, local(): lax.all_to_all(wanted, 'dp', split_axis=0, concat_axis=0, tiled=True)  15.6 us
    unnamed x42, local copies, waits for them, and re-layouts  14.7 us
    pallas_call x1, Pallas kernels, ssd(): pl.pallas_call(ssd_kernel, out_shape=(jax.ShapeDtypeStruct((tokens, width...  14.3 us
    pallas_call x1, Pallas kernels, tail(): pl.pallas_call(tail_kernel, out_shape=(jax.ShapeDtypeStruct((tokens, widt...  5.73 us
    ppermute x3, starting transfers between devices, local(): lax.ppermute(square, 'mp', [(i, (i + 2 * s) % groups) for i in range(grou...  5.66 us
    all_to_all x1, starting transfers between devices, local(): back = lax.all_to_all(sent, 'dp', split_axis=0, concat_axis=0, tiled=True)  4.68 us
  transfers between devices with their start and end apart: 5, of which 3 were waited for; matrix products, arithmetic and copies ran while one was open for 1% of the time, Pallas kernels for 27%

commit v1 on v0

--- a/solution.py
+++ b/solution.py
@@ -55,28 +55,59 @@
     )(hit_owner, hit_slot)
 
 
-def pick_kernel(codes_ref, cache_ref, out_ref):
-    d = pl.program_id(0)
-    for k in range(CAP):
-        out_ref[0, k] = cache_ref[codes_ref[d, 0, k]]
-
-
-def pick(codes, cache):
+def pick_kernel(codes_ref, cache_ref, window_ref, out_ref, wa_ref, wb_ref, rows_ref, sem):
+    owners = out_ref.shape[0]
+    p = cache_ref.shape[1]
+    half = window_ref.shape[1] // 3
+    cached = CAP * p
+
+    @pl.loop(0, owners)
+    def _(d):
+        for k in range(CAP):
+            pltpu.make_async_copy(
+                cache_ref.at[codes_ref[d, 0, k]], out_ref.at[d, k * p : k * p + p], sem
+            ).start()
+
+    w = window_ref[...].astype(F32)
+    first = w[:, : 2 * half]
+    second = jnp.concatenate([w[:, 2 * half :], jnp.zeros((w.shape[0], half), F32)], axis=1)
+    odd = lax.broadcasted_iota(jnp.int32, first.shape, 0) % 2 == 1
+    wa_ref[...] = jnp.where(odd, pltpu.roll(first, half, 1), first)
+    wb_ref[...] = jnp.where(odd, pltpu.roll(second, half, 1), second)
+
+    @pl.loop(0, owners)
+    def _(d):
+        for k in range(CAP):
+            at = pl.ds(codes_ref[d, 0, k], 1)
+            rows_ref[d, 2 * k : 2 * k + 1] = wa_ref[at]
+            rows_ref[d, 2 * k + 1 : 2 * k + 2] = wb_ref[at]
+
+    pltpu.make_async_copy(rows_ref, out_ref.at[:, cached:], sem).start()
+    pltpu.make_async_copy(out_ref, out_ref, sem).wait()
+
+
+def pick(codes, cache, window):
     owners = codes.shape[0]
     blocks, p, n = cache.shape
     return pl.pallas_call(
         pick_kernel,
-        out_shape=jax.ShapeDtypeStruct((owners, CAP, p, n), F32),
-        grid_spec=pltpu.PrefetchScalarGridSpec(
-            num_scalar_prefetch=1,
-            grid=(owners,),
-            in_specs=[full((blocks, p, n), pipeline_mode=pl.Buffered(1))],
-            out_specs=pl.BlockSpec((1, CAP, p, n), lambda d, c: (d, 0, 0, 0)),
-        ),
-        compiler_params=pltpu.CompilerParams(vmem_limit_bytes=8 * MIB),
-        cost_estimate=pl.CostEstimate(flops=0, bytes_accessed=6 * MIB, transcendentals=0),
+        out_shape=jax.ShapeDtypeStruct((owners, CAP * p + 2 * CAP, n), F32),
+        in_specs=[
+            pl.BlockSpec(memory_space=pltpu.SMEM),
+            pl.BlockSpec(memory_space=pl.ANY),
+            pl.BlockSpec(memory_space=pltpu.VMEM),
+        ],
+        out_specs=pl.BlockSpec(memory_space=pl.ANY),
+        scratch_shapes=[
+            pltpu.VMEM((blocks, n), F32),
+            pltpu.VMEM((blocks, n), F32),
+            pltpu.VMEM((owners, 2 * CAP, n), F32),
+            pltpu.SemaphoreType.DMA,
+        ],
+        compiler_params=pltpu.CompilerParams(vmem_limit_bytes=60 * MIB),
+        cost_estimate=pl.CostEstimate(flops=0, bytes_accessed=8 * MIB, transcendentals=0),
         name="pick",
-    )(codes, cache)
+    )(codes, cache, window)
 
 
 TILE = 256
@@ -85,7 +116,7 @@
 def project_kernel(steps, act_ref, wi_ref, wg_ref, ws_ref, wd_ref, inner_ref, gate_ref, state_ref, step_ref):
     j = pl.program_id(0)
     rows = act_ref.shape[0]
-    chunk = 256
+    chunk = 1024
 
     def run(w_ref, out_ref):
         @pl.loop(0, rows // chunk)
@@ -152,7 +183,6 @@
     gate_ref,
     state_ref,
     step_ref,
-    win_ref,
     hist_ref,
     ik_ref,
     sk_ref,
@@ -162,8 +192,10 @@
     az_ref,
     ez_ref,
     c_ref,
+    b_ref,
     f1_ref,
     el_ref,
+    first_ref,
     u_ref,
     v_ref,
 ):
@@ -171,8 +203,9 @@
     heads = step_ref.shape[1]
     p = width // heads
     taps = ik_ref.shape[0]
+    lag = taps - 1
     n = state_ref.shape[1] // 2
-    lead = 8 - (taps - 1)
+    lead = 8 - lag
     half = seq // 2
 
     v_ref[lead:8, :] = hist_ref[0].astype(F32)
@@ -185,6 +218,7 @@
     b = conv[:, :n]
     c = conv[:, n:]
     c_ref[...] = c
+    b_ref[0] = b[:16].astype(F32)[:8]
 
     raw = step_ref[...] + bias_ref[...]
     dt = jnp.maximum(raw, 0.0) + jnp.log1p(jnp.exp(-jnp.abs(raw)))
@@ -198,22 +232,43 @@
     )
     cum_t = cum.T
     dt_t = dt.T
+    begin = cum[lag - 1 : lag]
     last = cum[seq - 1 : seq]
     spread = (
         lax.broadcasted_iota(jnp.int32, (128, width), 1) // p
         == lax.broadcasted_iota(jnp.int32, (128, width), 0)
     )
     spread = spread.astype(F32).astype(BF16)
-    grown = jnp.exp(cum)
-    tail = jnp.exp(last - cum) * dt
-    el_ref[0] = jnp.broadcast_to(jnp.exp(cum_t[:heads, seq - 1 : seq]), (heads, n))
+    early = lax.broadcasted_iota(jnp.int32, (seq, 128), 0) < lag
+    grown = jnp.exp(jnp.where(early, cum, jnp.minimum(cum - begin, 0.0))).astype(BF16)
+    tail = jnp.exp(jnp.minimum(last - cum, 0.0)) * dt
+    begin_t = cum_t[:heads, lag - 1 : lag]
+    last_t = cum_t[:heads, seq - 1 : seq]
+    el_ref[0, :heads] = jnp.broadcast_to(jnp.exp(jnp.minimum(last_t - begin_t, 0.0)), (heads, n))
+    el_ref[0, heads:] = jnp.broadcast_to(jnp.exp(begin_t), (heads, n))
 
     scores = lax.dot_general(c, b, (((1,), (1,)), ((), ())), preferred_element_type=F32)
     scores = jnp.where(causal, scores, 0.0)
     top = scores[:half, :half]
     bottom = scores[half:]
 
-    u_ref[lead:8, :] = win_ref[0]
+    row8 = lax.broadcasted_iota(jnp.int32, (8, 128), 0)
+    cum8 = cum[:8]
+    dt8 = dt[:8]
+    small = [jnp.where(row8 < lag, jnp.exp(jnp.minimum(begin - cum8, 0.0)) * dt8, 0.0).astype(BF16)]
+    for j in range(lag):
+        rows = []
+        for t in range(8):
+            if j <= t < lag:
+                s = t - j
+                gap = jnp.exp(jnp.minimum(cum[t : t + 1] - cum[s : s + 1], 0.0))
+                rows.append(gap * scores[t : t + 1, s : s + 1] * dt[s : s + 1])
+            else:
+                rows.append(jnp.zeros((1, 128), F32))
+        small.append(jnp.concatenate(rows, axis=0).astype(BF16))
+    small = jnp.concatenate([m.astype(F32) for m in small], axis=0).astype(BF16)
+
+    u_ref[:8, :] = jnp.zeros((8, width), F32)
     u_ref[8:, :] = inner_ref[...].astype(F32)
     lane = lax.broadcasted_iota(jnp.int32, (1, 128), 1)
     for q in range(width // 128):
@@ -222,7 +277,7 @@
         run = jnp.zeros((seq, 128), F32)
         for k in range(taps):
             run = run + ik[k : k + 1] * u_ref[lead + k : lead + k + seq, cols]
-        x = silu(run).astype(BF16)
+        x = jnp.where(early, 0.0, silu(run)).astype(BF16)
         xf = x.astype(F32)
         y_top = jnp.zeros((half, 128), F32)
         y_bottom = jnp.zeros((seq - half, 128), F32)
@@ -237,25 +292,34 @@
             w_bottom = jnp.exp(jnp.minimum(col[half:] - row, 0.0)) * (bottom * dr)
             y_top = y_top + jnp.dot(w_top.astype(BF16), xs[:half], preferred_element_type=F32)
             y_bottom = y_bottom + jnp.dot(w_bottom.astype(BF16), xs, preferred_element_type=F32)
-        y = jnp.concatenate([y_top, y_bottom], axis=0) + skip_ref[:, cols] * xf
+        skip = skip_ref[:, cols]
+        y = jnp.concatenate([y_top, y_bottom], axis=0) + skip * xf
         z = silu(gate_ref[:, cols].astype(F32))
         az_ref[:, cols] = (y * z).astype(BF16)
-        ez = jnp.dot(grown.astype(BF16), spread[:, cols], preferred_element_type=F32) * z
+        ez = jnp.dot(grown, spread[:, cols], preferred_element_type=F32) * z
         ez_ref[:, cols] = ez.astype(BF16)
         tw = jnp.dot(tail.astype(BF16), spread[:, cols], preferred_element_type=F32)
         xt = (xf * tw).astype(BF16)
         f1_ref[0, cols, :] = lax.dot_general(
             xt, b, (((0,), (0,)), ((), ())), preferred_element_type=F32
         )
-
-
-def ssd(inner, gate, state, step, window, history, ik, sk, bias, decay, skip):
+        wide = jnp.dot(small, spread[:, cols], preferred_element_type=F32)
+        first_ref[0, 0:8, cols] = run[:8]
+        first_ref[0, 8:16, cols] = wide[:8]
+        z8 = z[:8]
+        first_ref[0, 16:24, cols] = jnp.where(row8 < lag, (wide[8:16] + skip) * z8, 0.0)
+        for j in range(1, lag):
+            first_ref[0, 16 + 8 * j : 24 + 8 * j, cols] = wide[8 + 8 * j : 16 + 8 * j] * z8
+
+
+def ssd(inner, gate, state, step, history, ik, sk, bias, decay, skip):
     tokens, width = inner.shape
     requests = history.shape[0]
     seq = tokens // requests
     heads = step.shape[1]
     n2 = state.shape[1]
     n = n2 // 2
+    lag = ik.shape[0] - 1
     rows = lambda w: pl.BlockSpec((seq, w), lambda r: (r, 0))
     per = lambda *s: pl.BlockSpec((1,) + s, lambda r: (r,) + (0,) * len(s))
     return pl.pallas_call(
@@ -264,8 +328,10 @@
             jax.ShapeDtypeStruct((tokens, width), BF16),
             jax.ShapeDtypeStruct((tokens, width), BF16),
             jax.ShapeDtypeStruct((tokens, n), BF16),
+            jax.ShapeDtypeStruct((requests, 8, n), F32),
             jax.ShapeDtypeStruct((requests, width, n), F32),
-            jax.ShapeDtypeStruct((requests, heads, n), F32),
+            jax.ShapeDtypeStruct((requests, 2 * heads, n), F32),
+            jax.ShapeDtypeStruct((requests, 16 + 8 * lag, width), F32),
         ),
         grid=(requests,),
         in_specs=[
@@ -273,7 +339,6 @@
             rows(width),
             rows(n2),
             rows(heads),
-            per(*window.shape[1:]),
             per(*history.shape[1:]),
             full(ik.shape),
             full(sk.shape),
@@ -281,48 +346,152 @@
             full(decay.shape),
             full(skip.shape),
         ],
-        out_specs=(rows(width), rows(width), rows(n), per(width, n), per(heads, n)),
+        out_specs=(
+            rows(width),
+            rows(width),
+            rows(n),
+            per(8, n),
+            per(width, n),
+            per(2 * heads, n),
+            per(16 + 8 * lag, width),
+        ),
         scratch_shapes=[pltpu.VMEM((seq + 8, width), F32), pltpu.VMEM((seq + 8, n2), F32)],
-        compiler_params=pltpu.CompilerParams(vmem_limit_bytes=32 * MIB),
+        compiler_params=pltpu.CompilerParams(vmem_limit_bytes=24 * MIB),
         cost_estimate=pl.CostEstimate(
             flops=2 * tokens * width * seq * 2, bytes_accessed=14 * MIB, transcendentals=tokens * seq * heads
         ),
         name="ssd",
-    )(inner, gate, state, step, window, history, ik, sk, bias, decay, skip)
-
-
-def tail_kernel(pos_ref, back_ref, az_ref, ez_ref, c_ref, f1_ref, el_ref, g_ref, sq_ref, final_ref, s_ref):
+    )(inner, gate, state, step, history, ik, sk, bias, decay, skip)
+
+
+def tail_kernel(
+    pos_ref,
+    back_ref,
+    az_ref,
+    ez_ref,
+    c_ref,
+    b_ref,
+    f1_ref,
+    el_ref,
+    first_ref,
+    ik_ref,
+    g_ref,
+    sq_ref,
+    final_ref,
+    held_ref,
+    rows_ref,
+    s_ref,
+    raw_ref,
+    win_ref,
+    mix_ref,
+    x_ref,
+    sem,
+    row_sem,
+):
     r = pl.program_id(0)
-    heads, n = el_ref.shape[1:]
-    p = back_ref.shape[1]
+    requests = pl.num_programs(0)
+    heads = el_ref.shape[1] // 2
+    p = held_ref.shape[1]
     seq, width = az_ref.shape
+    lag = ik_ref.shape[0] - 1
+    cached = CAP * p
+
+    def fetch(q):
+        for h in range(heads):
+            e = q * heads + h
+            at = pos_ref[e]
+            pltpu.make_async_copy(
+                back_ref.at[at // CAP, pl.ds(pl.multiple_of((at % CAP) * p, p), p)],
+                held_ref.at[e],
+                sem.at[q],
+            ).start()
+
+    row_copy = pltpu.make_async_copy(back_ref.at[:, cached:], rows_ref, row_sem)
+
+    @pl.when(r == 0)
+    def _():
+        row_copy.start()
+        fetch(0)
+        sq_ref[...] = jnp.zeros_like(sq_ref)
+        win_ref[...] = jnp.zeros_like(win_ref)
+        x_ref[...] = jnp.zeros_like(x_ref)
+        row_copy.wait()
+
+    @pl.when(r + 1 < requests)
+    def _():
+        fetch(r + 1)
+
+    low = lax.broadcasted_iota(jnp.int32, (1, 128), 1) < p
+    flat = rows_ref.reshape(rows_ref.shape[0] * rows_ref.shape[1], 128)
+    for q in range(heads // 2):
+        cols = slice(q * 128, q * 128 + 128)
+        even = 2 * pos_ref[r * heads + 2 * q]
+        odd = 2 * pos_ref[r * heads + 2 * q + 1]
+        a0, a1 = flat[pl.ds(even, 1)], flat[pl.ds(odd, 1)]
+        b0, b1 = flat[pl.ds(even + 1, 1)], flat[pl.ds(odd + 1, 1)]
+        win_ref[0:1, cols] = jnp.where(low, a0, a1)
+        win_ref[2:3, cols] = jnp.where(low, b0, b1)
+        mix_ref[q : q + 1] = jnp.where(low, a1, a0)
+    mix = pltpu.roll(mix_ref[...], p, 1)
+    for q in range(heads // 2):
+        win_ref[1:2, q * 128 : q * 128 + 128] = mix[q : q + 1]
+
+    ik = ik_ref[...].astype(F32)
+    run = first_ref[0, 0:8]
+    for k in range(lag):
+        run = run + ik[k : k + 1] * win_ref[k : k + 8]
+    row8 = lax.broadcasted_iota(jnp.int32, (8, width), 0)
+    x = jnp.where(row8 < lag, silu(run), 0.0).astype(BF16).astype(F32)
+    x_ref[8:16] = x
+    extra = first_ref[0, 16:24] * x
+    for j in range(1, lag):
+        extra = extra + first_ref[0, 16 + 8 * j : 24 + 8 * j] * x_ref[8 - j : 16 - j]
+    grow = (x * first_ref[0, 8:16]).T.astype(BF16)
+    add = jnp.dot(grow, b_ref[0].astype(BF16), preferred_element_type=F32)
+
+    pltpu.make_async_copy(
+        held_ref.at[pl.ds(r * heads, heads)], held_ref.at[pl.ds(r * heads, heads)], sem.at[r]
+    ).wait()
     for h in range(heads):
-        block = back_ref[pos_ref[r * heads + h]]
         at = slice(h * p, h * p + p)
+        block = held_ref[r * heads + h]
+        raw_ref[at] = block.astype(BF16)
+        block = el_ref[0, heads + h : heads + h + 1] * block + add[at]
+        s_ref[at] = block.astype(BF16)
         final_ref[0, h] = el_ref[0, h : h + 1] * block + f1_ref[0, at]
-        s_ref[at] = block.astype(BF16)
+
     c = c_ref[...]
-    total = jnp.zeros((seq, 128), F32)
+    total = jnp.zeros((seq - 16, 128), F32)
+    total16 = jnp.zeros((16, 128), F32)
+    row16 = lax.broadcasted_iota(jnp.int32, (16, 256), 0)
+    nt = (((1,), (1,)), ((), ()))
     for q in range(width // 256):
         cols = slice(q * 256, q * 256 + 256)
-        seen = lax.dot_general(c, s_ref[cols], (((1,), (1,)), ((), ())), preferred_element_type=F32)
-        g = az_ref[:, cols].astype(F32) + ez_ref[:, cols].astype(F32) * seen
-        g_ref[:, cols] = g.astype(BF16)
-        g2 = g * g
-        total = total + g2[:, :128] + g2[:, 128:]
-
-    @pl.when(r == 0)
-    def _():
-        sq_ref[...] = jnp.zeros_like(sq_ref)
-
+        seen = lax.dot_general(c, s_ref[cols], nt, preferred_element_type=F32)
+        seen16 = lax.dot_general(c[:16], raw_ref[cols], nt, preferred_element_type=F32)
+        seen16 = jnp.where(row16 < lag, seen16, seen[:16])
+        az = az_ref[:, cols].astype(F32)
+        ez = ez_ref[:, cols].astype(F32)
+        g = az[16:] + ez[16:] * seen[16:]
+        g16 = az[:16] + ez[:16] * seen16
+        g16 = g16 + jnp.concatenate([extra[:, cols], jnp.zeros((8, 256), F32)], axis=0)
+        g_ref[:16, cols] = g16.astype(BF16)
+        g_ref[16:, cols] = g.astype(BF16)
+        g = g * g
+        g16 = g16 * g16
+        total = total + g[:, :128] + g[:, 128:]
+        total16 = total16 + g16[:, :128] + g16[:, 128:]
+    total = jnp.concatenate([total16, total], axis=0)
     sq_ref[pl.ds(r, 1), :] = jnp.sum(total.T, axis=0, keepdims=True)
 
 
-def tail(pos, back, az, ez, c, f1, el):
-    requests, heads, n = el.shape
+def tail(pos, back, az, ez, c, b, f1, el, first, ik):
+    requests, heads2, n = el.shape
+    heads = heads2 // 2
     tokens, width = az.shape
-    p = back.shape[1]
+    p = width // heads
     seq = tokens // requests
+    owners = back.shape[0]
     rows = lambda w: pl.BlockSpec((seq, w), lambda r, _: (r, 0))
     per = lambda *s: pl.BlockSpec((1,) + s, lambda r, _: (r,) + (0,) * len(s))
     return pl.pallas_call(
@@ -336,22 +505,35 @@
             num_scalar_prefetch=1,
             grid=(requests,),
             in_specs=[
-                full(back.shape, pipeline_mode=pl.Buffered(1)),
+                pl.BlockSpec(memory_space=pl.ANY),
                 rows(width),
                 rows(width),
                 rows(n),
+                per(*b.shape[1:]),
                 per(width, n),
-                per(heads, n),
+                per(heads2, n),
+                per(*first.shape[1:]),
+                full(ik.shape),
             ],
             out_specs=(rows(width), full((8, seq)), per(heads, p, n)),
-            scratch_shapes=[pltpu.VMEM((width, n), BF16)],
+            scratch_shapes=[
+                pltpu.VMEM((requests * heads, p, n), F32),
+                pltpu.VMEM((owners, 2 * CAP, n), F32),
+                pltpu.VMEM((width, n), BF16),
+                pltpu.VMEM((width, n), BF16),
+                pltpu.VMEM((16, width), F32),
+                pltpu.VMEM((8, 128), F32),
+                pltpu.VMEM((16, width), F32),
+                pltpu.SemaphoreType.DMA((requests,)),
+                pltpu.SemaphoreType.DMA,
+            ],
         ),
         compiler_params=pltpu.CompilerParams(vmem_limit_bytes=24 * MIB),
         cost_estimate=pl.CostEstimate(
             flops=2 * tokens * width * n, bytes_accessed=14 * MIB, transcendentals=0
         ),
         name="tail",
-    )(pos, back, az, ez, c, f1, el)
+    )(pos, back, az, ez, c, b, f1, el, first, ik)
 
 
 def norm_kernel(channels, g_ref, s0_ref, s1_ref, s2_ref, s3_ref, gain_ref, out_ref):
@@ -406,23 +588,19 @@
     requests, heads = hit_owner.shape
     slots, _, p, n = scan_cache.shape
     width = inner_weight.shape[1]
-    lead = inner_kernel.shape[0] - 1
+    blocks = slots * heads
 
     wanted, pos = prep(hit_owner, hit_slot, owners)
     codes = lax.all_to_all(wanted, "dp", split_axis=0, concat_axis=0, tiled=True)
-    windows = lax.all_gather(window_cache.astype(F32), "dp", tiled=True)
-    sent = pick(codes, scan_cache.reshape(slots * heads, p, n))
+    sent = pick(codes, scan_cache.reshape(blocks, p, n), window_cache.reshape(blocks, -1))
     back = lax.all_to_all(sent, "dp", split_axis=0, concat_axis=0, tiled=True)
 
-    window = windows[hit_owner * slots + hit_slot, jnp.arange(heads)[None]]
-    window = window.reshape(requests, heads, lead, p).transpose(0, 2, 1, 3).reshape(requests, lead, width)
     inner, gate, state, step = project(activations, inner_weight, gate_weight, state_proj, step_weight)
-    az, ez, c, f1, el = ssd(
+    az, ez, c, b, f1, el, first = ssd(
         inner,
         gate,
         state,
         step,
-        window,
         state_history,
         inner_kernel,
         state_kernel,
@@ -430,7 +608,7 @@
         decay_rate[None],
         jnp.repeat(skip_scale, p)[None],
     )
-    g, square, final = tail(pos, back.reshape(owners * CAP, p, n), az, ez, c, f1, el)
+    g, square, final = tail(pos, back, az, ez, c, b, f1, el, first, inner_kernel)
     pair = [(i, i ^ 1) for i in range(groups)]
     square = square + lax.ppermute(square, "mp", pair)
     parts = [square] + [

time: 172 us -> 230 us (1.34)
  Pallas kernels: 56.8 us -> 182 us
  blocking collectives: 84.2 us -> 15.7 us
  waiting for transfers between devices: 3.37 us -> 9.48 us
  local copies, waits for them, and re-layouts: 16.1 us -> 11.5 us
    pallas_call x1, Pallas kernels: 1.17 us -> 129 us  [pick(): pl.pallas_call(pick_kernel, out_shape=jax.ShapeDtypeStruct((owners, CAP *...]
    all_gather x1 -> x0, blocking collectives: 68.6 us -> none  [local(): windows = lax.all_gather(window_cache.astype(F32), 'dp', tiled=True)]
    all_to_all x1, waiting for transfers between devices: 0.01 us -> 6.11 us  [local(): back = lax.all_to_all(sent, 'dp', split_axis=0, concat_axis=0, tiled=True)]
    pallas_call x1, Pallas kernels: 31.6 us -> 26.4 us  [project(): pl.pallas_call(functools.partial(project_kernel, steps), out_shape=(jax.S...]
    unnamed x42 -> x32, local copies, waits for them, and re-layouts: 14.7 us -> 11.3 us
  transfers between devices with their start and end apart: 5 -> 5, of which waited for: 3 -> 4; matrix products, arithmetic and copies ran while one was open for 1% -> 0% of each run, Pallas kernels for 27% -> 18%
where the time goes in v1:
time: 230 us
  Pallas kernels  182 us (79%)
  blocking collectives  15.7 us (7%)
  local copies, waits for them, and re-layouts  11.5 us (5%)
  starting transfers between devices  10.4 us (5%)
  waiting for transfers between devices  9.48 us (4%)
    pallas_call x1, Pallas kernels, pick(): pl.pallas_call(pick_kernel, out_shape=jax.ShapeDtypeStruct((owners, CAP *...  129 us
    pallas_call x1, Pallas kernels, project(): pl.pallas_call(functools.partial(project_kernel, steps), out_shape=(jax.S...  26.4 us
    all_to_all x1, blocking collectives, local(): lax.all_to_all(wanted, 'dp', split_axis=0, concat_axis=0, tiled=True)  15.7 us
    pallas_call x1, Pallas kernels, ssd(): pl.pallas_call(ssd_kernel, out_shape=(jax.ShapeDtypeStruct((tokens, width...  15.1 us
    unnamed x32, local copies, waits for them, and re-layouts  11.3 us
    pallas_call x1, Pallas kernels, tail(): pl.pallas_call(tail_kernel, out_shape=(jax.ShapeDtypeStruct((tokens, widt...  7.12 us
    all_to_all x1, waiting for transfers between devices, local(): back = lax.all_to_all(sent, 'dp', split_axis=0, concat_axis=0, tiled=True)  6.11 us
    ppermute x3, starting transfers between devices, local(): lax.ppermute(square, 'mp', [(i, (i + 2 * s) % groups) for i in range(grou...  5.65 us
  transfers between devices with their start and end apart: 5, of which 4 were waited for; matrix products, arithmetic and copies ran while one was open for 0% of the time, Pallas kernels for 18%

profile of v1, /device:TPU:0, one launch (start us, length us, event | category | flops | bytes accessed | tf_op | source)
XLA Modules:
  0.0 229.6 jit_solution(13255316621968755189)
XLA Ops:
  0.6 1.8 prep.1
  2.4 15.7 %all_to_all.10.codes_ref = s32[16,1,128]{2,1,0:T(1,128)} all-to-all(s32[16,1,128]{2,1,0:T(1,128)} %get-tuple-element.19), channel_id=1, replica_groups=mesh['dp'=16,'mp'=8] {'dp'}, dimensions={0} | all-to-all | bytes 16384 | tf_op jit(solution)/shard_map/all_to_all | solution.py:594
  18.2 129.0 %pick.1 = f32[16,528,128]{2,1,0:T(8,128)} custom-call(s32[16,1,128]{2,1,0:T(1,128)} %all_to_all.10.codes_ref, f32[48,64,128]{2,1,0:T(8,128)} %bitcast.6, bf16[48,192]{1,0:T(8,128)(2,1)} %bitcast.7), custom_call_target="tpu_custom_call" | custom-call | bytes 8388608 | tf_op jit(solution)/shard_map/pick/pallas_call | solution.py:92
  147.1 0.0 copy-start.11
  147.2 0.0 copy-start.14
  147.2 0.0 copy-start.12
  147.2 4.7 %all-to-all-start.1 = ((f32[16,528,128]{2,1,0:T(8,128)}), f32[16,528,128]{2,1,0:T(8,128)}, u32[]{:S(2)}, u32[]{:S(2)}) async-start(f32[16,528,128]{2,1,0:T(8,128)} %pick.1), calls=%async_computation.1 | async-start | bytes 8650752 | tf_op jit(solution)/shard_map/all_to_all | solution.py:596
  151.9 0.5 copy.18.wd_ref
  152.4 0.1 broadcast_in_dim.14
  152.5 0.1 broadcast_in_dim_reshape.3.skip_ref
  152.5 0.0 copy-done.12
  152.6 0.0 copy-start.6
  152.6 3.4 %copy-done.6 = bf16[1024,4096]{1,0:T(8,128)(2,1)S(1)} copy-done((bf16[1024,4096]{1,0:T(8,128)(2,1)S(1)}, bf16[1024,4096]{1,0:T(8,128)(2,1)}, u32[]{:S(2)}) %copy-start.6) | copy-done | bytes 8388632
  155.9 1.6 copy-done.7
  157.5 26.4 %project.1 = (bf16[1024,1024]{1,0:T(8,128)(2,1)S(1)}, bf16[1024,1024]{1,0:T(8,128)(2,1)S(1)}, bf16[1024,256]{1,0:T(8,128)(2,1)S(1)}, f32[1024,16]{1,0:T(8,128)S(1)}) custom-call(bf16[1024,4096]{1,0:T(8,128)(2,1)S(1)} %copy-done.6, bf16[4096,1024]{1,0:T(8,128)(2,1)} %wi_ref.1, bf16[4096,1024]{1,0:T(8,128)(2,1)} %wg_ref.1, bf16[4096,256]{1,0:T(8,128)(2,1)S(1)} %copy-done.7, ...), custom_call_target="tpu_custom_call" | custom-call | flops 19461570560 | bytes 33554432 | tf_op jit(solution)/shard_map/project/pallas_call | solution.py:153
  184.0 15.1 %ssd.1 = (bf16[1024,1024]{1,0:T(8,128)(2,1)S(1)}, bf16[1024,1024]{1,0:T(8,128)(2,1)S(1)}, bf16[1024,128]{1,0:T(8,128)(2,1)S(1)}, f32[4,8,128]{2,1,0:T(8,128)S(1)...) custom-call(bf16[1024,1024]{1,0:T(8,128)(2,1)S(1)} %get-tuple-element.20.inner_ref, ...), custom_call_target="tpu_custom_call" | custom-call | flops 1073741824 | bytes 14680064 | tf_op jit(solution)/shard_map/ssd/pallas_call | solution.py:325
  199.1 0.0 copy-start
  199.2 1.3 copy-done
  200.5 1.3 copy-done.2
  201.8 6.1 %all-to-all-done.1.back_ref = f32[16,528,128]{2,1,0:T(8,128)} async-done(((f32[16,528,128]{2,1,0:T(8,128)}), f32[16,528,128]{2,1,0:T(8,128)}, u32[]{:S(2)}, u32[]{:S(2)}) %all-to-all-start.1) | async-done | bytes 4325408 | tf_op jit(solution)/shard_map/all_to_all | solution.py:596
  207.9 1.6 copy-done.1
  209.5 1.6 copy-done.3
  211.1 7.1 %tail.1 = (bf16[1024,1024]{1,0:T(8,128)(2,1)S(1)}, f32[8,256]{1,0:T(8,128)S(1)}, f32[4,16,64,128]{3,2,1,0:T(8,128)}) custom-call(s32[64]{0:T(128)S(1)} %copy-done.5, f32[16,528,128]{2,1,0:T(8,128)} %all-to-all-done.1.back_ref, bf16[1024,1024]{1,0:T(8,128)(2,1)S(1)} %get-tuple-element.24.az_ref, bf16[1024,1024]{1,0:T(8,128)(2,1)S(1)} %copy-done.1, ...), custom_call_target="tpu_custom_call" | custom-call | flops 268435456 | bytes 14680064 | tf_op jit(solution)/shard_map/tail/pallas_call | solution.py:497
  218.2 0.1 collective-permute-start
  218.3 1.2 collective-permute-done
  219.5 1.5 collective-permute-start.1
  221.0 2.7 %collective-permute-start.2 = (f32[8,256]{1,0:T(8,128)S(1)}, f32[8,256]{1,0:T(8,128)S(1)}, u32[]{:S(2)}, u32[]{:S(2)}) collective-permute-start(f32[8,256]{1,0:T(8,128)S(1)} %add.3.s0_ref), channel_id=1, source_target_pairs={{0,4},{1,5},{2,6},{3,7},{4,0},{5,1},{6,2},{7,3},{8,12},{9,13},{10,... | collective-permute-start | bytes 24584 | tf_op jit(solution)/shard_map/ppermute | solution.py:615
  223.7 1.4 collective-permute-start.3
  225.1 0.0 collective-permute-done.1.s1_ref
  225.1 1.0 collective-permute-done.2.s2_ref
  226.1 1.2 collective-permute-done.3.s3_ref
  227.3 2.3 normalise.1
  (21 shorter events, 0.0 us)
Async XLA Ops:
  147.1 4.7 %copy-start.11 = (bf16[4096,16]{0,1:T(8,128)(2,1)S(1)}, bf16[4096,16]{0,1:T(8,128)(2,1)}, u32[]{:S(2)}) copy-start(bf16[4096,16]{0,1:T(8,128)(2,1)} %param.20) | copy-start | bytes 393220
  147.2 5.2 %copy-start.14 = (f32[16]{0:T(128)S(1)}, f32[16]{0:T(128)}, u32[]{:S(2)}) copy-start(f32[16]{0:T(128)} %param.25) | copy-start | bytes 196
  147.2 5.4 %copy-start.12 = (bf16[4,3,256]{2,0,1:T(4,128)(2,1)S(1)}, bf16[4,3,256]{2,0,1:T(4,128)(2,1)}, u32[]{:S(2)}) copy-start(bf16[4,3,256]{2,0,1:T(4,128)(2,1)} %param.29) | copy-start | bytes 18436
  147.2 60.7 %all-to-all-start.1 = ((f32[16,528,128]{2,1,0:T(8,128)}), f32[16,528,128]{2,1,0:T(8,128)}, u32[]{:S(2)}, u32[]{:S(2)}) async-start(f32[16,528,128]{2,1,0:T(8,128)} %pick.1), calls=%async_computation.1 | async-start | bytes 8650752 | tf_op jit(solution)/shard_map/all_to_all | solution.py:596
  152.6 3.4 %copy-start.6 = (bf16[1024,4096]{1,0:T(8,128)(2,1)S(1)}, bf16[1024,4096]{1,0:T(8,128)(2,1)}, u32[]{:S(2)}) copy-start(bf16[1024,4096]{1,0:T(8,128)(2,1)} %act_ref.1) | copy-start | bytes 25165828
  155.9 1.6 copy-start.7
  157.5 26.4 %copy-start.4 = (bf16[4,1024]{1,0:T(4,128)(2,1)S(1)}, bf16[4,1024]{1,0:T(4,128)(2,1)}, u32[]{:S(2)}) copy-start(bf16[4,1024]{1,0:T(4,128)(2,1)} %ik_ref.3) | copy-start | bytes 24580
  157.5 26.5 %copy-start.8 = (bf16[4,256]{1,0:T(4,128)(2,1)S(1)}, bf16[4,256]{1,0:T(4,128)(2,1)}, u32[]{:S(2)}) copy-start(bf16[4,256]{1,0:T(4,128)(2,1)} %sk_ref.1) | copy-start | bytes 6148
  157.5 26.5 %copy-start.9 = (f32[16]{0:T(128)S(1)}, f32[16]{0:T(128)}, u32[]{:S(2)}) copy-start(f32[16]{0:T(128)} %param.23) | copy-start | bytes 196
  157.5 26.5 %copy-start.10 = (f32[16]{0:T(128)S(1)}, f32[16]{0:T(128)}, u32[]{:S(2)}) copy-start(f32[16]{0:T(128)} %param.24) | copy-start | bytes 196
  184.0 23.9 %copy-start.5 = (s32[64]{0:T(128)S(1)}, s32[64]{0:T(128)}, u32[]{:S(2)}) copy-start(s32[64]{0:T(128)} %get-tuple-element.18.pos_ref) | copy-start | bytes 772
  199.1 1.3 copy-start
  200.5 1.3 copy-start.2
  207.9 1.6 copy-start.1
  209.5 1.6 copy-start.3
  211.1 14.0 %copy-start.13 = (bf16[1024]{0:T(1024)(128)(2,1)S(1)}, bf16[1024]{0:T(1024)(128)(2,1)}, u32[]{:S(2)}) copy-start(bf16[1024]{0:T(1024)(128)(2,1)} %param.26) | copy-start | bytes 6148
  218.2 1.3 collective-permute-start
  219.5 5.7 %collective-permute-start.1 = (f32[8,256]{1,0:T(8,128)S(1)}, f32[8,256]{1,0:T(8,128)S(1)}, u32[]{:S(2)}, u32[]{:S(2)}) collective-permute-start(f32[8,256]{1,0:T(8,128)S(1)} %add.3.s0_ref), channel_id=1, source_target_pairs={{0,2},{1,3},{2,4},{3,5},{4,6},{5,7},{6,0},{7,1},{8,10},{9,11},{10,... | collective-permute-start | bytes 24584 | tf_op jit(solution)/shard_map/ppermute | solution.py:615
  221.0 5.2 %collective-permute-start.2 = (f32[8,256]{1,0:T(8,128)S(1)}, f32[8,256]{1,0:T(8,128)S(1)}, u32[]{:S(2)}, u32[]{:S(2)}) collective-permute-start(f32[8,256]{1,0:T(8,128)S(1)} %add.3.s0_ref), channel_id=1, source_target_pairs={{0,4},{1,5},{2,6},{3,7},{4,0},{5,1},{6,2},{7,3},{8,12},{9,13},{10,... | collective-permute-start | bytes 24584 | tf_op jit(solution)/shard_map/ppermute | solution.py:615
  223.7 3.7 %collective-permute-start.3 = (f32[8,256]{1,0:T(8,128)S(1)}, f32[8,256]{1,0:T(8,128)S(1)}, u32[]{:S(2)}, u32[]{:S(2)}) collective-permute-start(f32[8,256]{1,0:T(8,128)S(1)} %add.3.s0_ref), channel_id=1, source_target_pairs={{0,6},{1,7},{2,0},{3,1},{4,2},{5,3},{6,4},{7,5},{8,14},{9,15},{10,... | collective-permute-start | bytes 24584 | tf_op jit(solution)/shard_map/ppermute | solution.py:615

commit v2 on v1

--- a/solution.py
+++ b/solution.py
@@ -94,7 +94,7 @@
         out_shape=jax.ShapeDtypeStruct((owners, CAP * p + 2 * CAP, n), F32),
         in_specs=[
             pl.BlockSpec(memory_space=pltpu.SMEM),
-            pl.BlockSpec(memory_space=pl.ANY),
+            pl.BlockSpec(memory_space=pltpu.VMEM),
             pl.BlockSpec(memory_space=pltpu.VMEM),
         ],
         out_specs=pl.BlockSpec(memory_space=pl.ANY),
@@ -356,12 +356,35 @@
             per(16 + 8 * lag, width),
         ),
         scratch_shapes=[pltpu.VMEM((seq + 8, width), F32), pltpu.VMEM((seq + 8, n2), F32)],
-        compiler_params=pltpu.CompilerParams(vmem_limit_bytes=24 * MIB),
+        compiler_params=pltpu.CompilerParams(vmem_limit_bytes=60 * MIB),
         cost_estimate=pl.CostEstimate(
             flops=2 * tokens * width * seq * 2, bytes_accessed=14 * MIB, transcendentals=tokens * seq * heads
         ),
         name="ssd",
     )(inner, gate, state, step, history, ik, sk, bias, decay, skip)
+
+
+def fetch_blocks(pos_ref, back_ref, held_ref, sem, r, heads):
+    p = held_ref.shape[1]
+    for h in range(heads):
+        e = r * heads + h
+        at = pos_ref[e]
+        pltpu.make_async_copy(
+            back_ref.at[at // CAP, pl.ds(pl.multiple_of((at % CAP) * p, p), p)],
+            held_ref.at[e],
+            sem.at[r],
+        ).start()
+
+
+def await_blocks(held_ref, sem, r, heads):
+    part = held_ref.at[pl.ds(r * heads, heads)]
+    pltpu.make_async_copy(part, part, sem.at[r]).wait()
+
+
+def first_sources(grow_ref, b_ref, r):
+    own = lax.broadcasted_iota(jnp.int32, b_ref.shape, 0) // 8 == r
+    b = jnp.where(own, b_ref[...], 0.0).astype(BF16)
+    return jnp.dot(grow_ref[...], b, preferred_element_type=F32)
 
 
 def tail_kernel(
@@ -371,13 +394,12 @@
     ez_ref,
     c_ref,
     b_ref,
-    f1_ref,
     el_ref,
     first_ref,
     ik_ref,
     g_ref,
     sq_ref,
-    final_ref,
+    grow_ref,
     held_ref,
     rows_ref,
     s_ref,
@@ -385,80 +407,68 @@
     win_ref,
     mix_ref,
     x_ref,
+    extra_ref,
     sem,
     row_sem,
 ):
     r = pl.program_id(0)
-    requests = pl.num_programs(0)
+    requests = first_ref.shape[0]
     heads = el_ref.shape[1] // 2
     p = held_ref.shape[1]
     seq, width = az_ref.shape
     lag = ik_ref.shape[0] - 1
     cached = CAP * p
-
-    def fetch(q):
-        for h in range(heads):
-            e = q * heads + h
-            at = pos_ref[e]
-            pltpu.make_async_copy(
-                back_ref.at[at // CAP, pl.ds(pl.multiple_of((at % CAP) * p, p), p)],
-                held_ref.at[e],
-                sem.at[q],
-            ).start()
-
     row_copy = pltpu.make_async_copy(back_ref.at[:, cached:], rows_ref, row_sem)
 
     @pl.when(r == 0)
     def _():
         row_copy.start()
-        fetch(0)
+        fetch_blocks(pos_ref, back_ref, held_ref, sem, 0, heads)
         sq_ref[...] = jnp.zeros_like(sq_ref)
         win_ref[...] = jnp.zeros_like(win_ref)
         x_ref[...] = jnp.zeros_like(x_ref)
         row_copy.wait()
+        low = lax.broadcasted_iota(jnp.int32, (1, 128), 1) < p
+        flat = rows_ref.reshape(rows_ref.shape[0] * rows_ref.shape[1], 128)
+        pairs = heads // 2
+        for i in range(requests):
+            for q in range(pairs):
+                cols = slice(q * 128, q * 128 + 128)
+                even = 2 * pos_ref[i * heads + 2 * q]
+                odd = 2 * pos_ref[i * heads + 2 * q + 1]
+                a0, a1 = flat[pl.ds(even, 1)], flat[pl.ds(odd, 1)]
+                b0, b1 = flat[pl.ds(even + 1, 1)], flat[pl.ds(odd + 1, 1)]
+                win_ref[i, 0:1, cols] = jnp.where(low, a0, a1)
+                win_ref[i, 2:3, cols] = jnp.where(low, b0, b1)
+                mix_ref[i * pairs + q : i * pairs + q + 1] = jnp.where(low, a1, a0)
+        mix = pltpu.roll(mix_ref[...], p, 1)
+        for i in range(requests):
+            for q in range(pairs):
+                win_ref[i, 1:2, q * 128 : q * 128 + 128] = mix[i * pairs + q : i * pairs + q + 1]
+        ik = ik_ref[...].astype(F32)
+        run = first_ref[:, 0:8]
+        for k in range(lag):
+            run = run + ik[k : k + 1][None] * win_ref[:, k : k + 8]
+        row8 = lax.broadcasted_iota(jnp.int32, run.shape, 1)
+        x = jnp.where(row8 < lag, silu(run), 0.0).astype(BF16).astype(F32)
+        x_ref[:, 8:16] = x
+        extra = first_ref[:, 16:24] * x
+        for j in range(1, lag):
+            extra = extra + first_ref[:, 16 + 8 * j : 24 + 8 * j] * x_ref[:, 8 - j : 16 - j]
+        extra_ref[...] = extra
+        grow_ref[...] = (x * first_ref[:, 8:16]).reshape(requests * 8, width).T.astype(BF16)
 
     @pl.when(r + 1 < requests)
     def _():
-        fetch(r + 1)
-
-    low = lax.broadcasted_iota(jnp.int32, (1, 128), 1) < p
-    flat = rows_ref.reshape(rows_ref.shape[0] * rows_ref.shape[1], 128)
-    for q in range(heads // 2):
-        cols = slice(q * 128, q * 128 + 128)
-        even = 2 * pos_ref[r * heads + 2 * q]
-        odd = 2 * pos_ref[r * heads + 2 * q + 1]
-        a0, a1 = flat[pl.ds(even, 1)], flat[pl.ds(odd, 1)]
-        b0, b1 = flat[pl.ds(even + 1, 1)], flat[pl.ds(odd + 1, 1)]
-        win_ref[0:1, cols] = jnp.where(low, a0, a1)
-        win_ref[2:3, cols] = jnp.where(low, b0, b1)
-        mix_ref[q : q + 1] = jnp.where(low, a1, a0)
-    mix = pltpu.roll(mix_ref[...], p, 1)
-    for q in range(heads // 2):
-        win_ref[1:2, q * 128 : q * 128 + 128] = mix[q : q + 1]
-
-    ik = ik_ref[...].astype(F32)
-    run = first_ref[0, 0:8]
-    for k in range(lag):
-        run = run + ik[k : k + 1] * win_ref[k : k + 8]
-    row8 = lax.broadcasted_iota(jnp.int32, (8, width), 0)
-    x = jnp.where(row8 < lag, silu(run), 0.0).astype(BF16).astype(F32)
-    x_ref[8:16] = x
-    extra = first_ref[0, 16:24] * x
-    for j in range(1, lag):
-        extra = extra + first_ref[0, 16 + 8 * j : 24 + 8 * j] * x_ref[8 - j : 16 - j]
-    grow = (x * first_ref[0, 8:16]).T.astype(BF16)
-    add = jnp.dot(grow, b_ref[0].astype(BF16), preferred_element_type=F32)
-
-    pltpu.make_async_copy(
-        held_ref.at[pl.ds(r * heads, heads)], held_ref.at[pl.ds(r * heads, heads)], sem.at[r]
-    ).wait()
+        fetch_blocks(pos_ref, back_ref, held_ref, sem, r + 1, heads)
+
+    add = first_sources(grow_ref, b_ref, r)
+    await_blocks(held_ref, sem, r, heads)
     for h in range(heads):
         at = slice(h * p, h * p + p)
         block = held_ref[r * heads + h]
         raw_ref[at] = block.astype(BF16)
-        block = el_ref[0, heads + h : heads + h + 1] * block + add[at]
-        s_ref[at] = block.astype(BF16)
-        final_ref[0, h] = el_ref[0, h : h + 1] * block + f1_ref[0, at]
+        s_ref[at] = (el_ref[0, heads + h : heads + h + 1] * block + add[at]).astype(BF16)
 
     c = c_ref[...]
     total = jnp.zeros((seq - 16, 128), F32)
@@ -474,7 +484,7 @@
         ez = ez_ref[:, cols].astype(F32)
         g = az[16:] + ez[16:] * seen[16:]
         g16 = az[:16] + ez[:16] * seen16
-        g16 = g16 + jnp.concatenate([extra[:, cols], jnp.zeros((8, 256), F32)], axis=0)
+        g16 = g16 + jnp.concatenate([extra_ref[r, :, cols], jnp.zeros((8, 256), F32)], axis=0)
         g_ref[:16, cols] = g16.astype(BF16)
         g_ref[16:, cols] = g.astype(BF16)
         g = g * g
@@ -485,7 +495,7 @@
     sq_ref[pl.ds(r, 1), :] = jnp.sum(total.T, axis=0, keepdims=True)
 
 
-def tail(pos, back, az, ez, c, b, f1, el, first, ik):
+def tail(pos, back, az, ez, c, b, el, first, ik):
     requests, heads2, n = el.shape
     heads = heads2 // 2
     tokens, width = az.shape
@@ -494,12 +504,13 @@
     owners = back.shape[0]
     rows = lambda w: pl.BlockSpec((seq, w), lambda r, _: (r, 0))
     per = lambda *s: pl.BlockSpec((1,) + s, lambda r, _: (r,) + (0,) * len(s))
+    once = lambda s: full(s, pipeline_mode=pl.Buffered(1))
     return pl.pallas_call(
         tail_kernel,
         out_shape=(
             jax.ShapeDtypeStruct((tokens, width), BF16),
             jax.ShapeDtypeStruct((8, seq), F32),
-            jax.ShapeDtypeStruct((requests, heads, p, n), F32),
+            jax.ShapeDtypeStruct((width, requests * 8), BF16),
         ),
         grid_spec=pltpu.PrefetchScalarGridSpec(
             num_scalar_prefetch=1,
@@ -509,31 +520,87 @@
                 rows(width),
                 rows(width),
                 rows(n),
-                per(*b.shape[1:]),
-                per(width, n),
+                once(b.shape),
                 per(heads2, n),
-                per(*first.shape[1:]),
-                full(ik.shape),
+                once(first.shape),
+                once(ik.shape),
             ],
-            out_specs=(rows(width), full((8, seq)), per(heads, p, n)),
+            out_specs=(rows(width), full((8, seq)), full((width, requests * 8))),
             scratch_shapes=[
                 pltpu.VMEM((requests * heads, p, n), F32),
                 pltpu.VMEM((owners, 2 * CAP, n), F32),
                 pltpu.VMEM((width, n), BF16),
                 pltpu.VMEM((width, n), BF16),
-                pltpu.VMEM((16, width), F32),
-                pltpu.VMEM((8, 128), F32),
-                pltpu.VMEM((16, width), F32),
+                pltpu.VMEM((requests, 16, width), F32),
+                pltpu.VMEM((requests * heads // 2, 128), F32),
+                pltpu.VMEM((requests, 16, width), F32),
+                pltpu.VMEM((requests, 8, width), F32),
                 pltpu.SemaphoreType.DMA((requests,)),
                 pltpu.SemaphoreType.DMA,
             ],
         ),
-        compiler_params=pltpu.CompilerParams(vmem_limit_bytes=24 * MIB),
+        compiler_params=pltpu.CompilerParams(vmem_limit_bytes=60 * MIB),
         cost_estimate=pl.CostEstimate(
-            flops=2 * tokens * width * n, bytes_accessed=14 * MIB, transcendentals=0
+            flops=2 * tokens * width * n, bytes_accessed=10 * MIB, transcendentals=0
         ),
         name="tail",
-    )(pos, back, az, ez, c, b, f1, el, first, ik)
+    )(pos, back, az, ez, c, b, el, first, ik)
+
+
+def final_kernel(pos_ref, back_ref, grow_ref, b_ref, el_ref, f1_ref, final_ref, held_ref, sem):
+    r = pl.program_id(0)
+    requests = pl.num_programs(0)
+    heads = el_ref.shape[1] // 2
+    p = held_ref.shape[1]
+
+    @pl.when(r == 0)
+    def _():
+        fetch_blocks(pos_ref, back_ref, held_ref, sem, 0, heads)
+
+    @pl.when(r + 1 < requests)
+    def _():
+        fetch_blocks(pos_ref, back_ref, held_ref, sem, r + 1, heads)
+
+    add = first_sources(grow_ref, b_ref, r)
+    await_blocks(held_ref, sem, r, heads)
+    for h in range(heads):
+        at = slice(h * p, h * p + p)
+        block = el_ref[0, heads + h : heads + h + 1] * held_ref[r * heads + h] + add[at]
+        final_ref[0, h] = el_ref[0, h : h + 1] * block + f1_ref[0, at]
+
+
+def finals(pos, back, grow, b, el, f1):
+    requests, heads2, n = el.shape
+    heads = heads2 // 2
+    width = f1.shape[1]
+    p = width // heads
+    per = lambda *s: pl.BlockSpec((1,) + s, lambda r, _: (r,) + (0,) * len(s))
+    once = lambda s: full(s, pipeline_mode=pl.Buffered(1))
+    return pl.pallas_call(
+        final_kernel,
+        out_shape=jax.ShapeDtypeStruct((requests, heads, p, n), F32),
+        grid_spec=pltpu.PrefetchScalarGridSpec(
+            num_scalar_prefetch=1,
+            grid=(requests,),
+            in_specs=[
+                pl.BlockSpec(memory_space=pl.ANY),
+                once(grow.shape),
+                once(b.shape),
+                per(heads2, n),
+                per(width, n),
+            ],
+            out_specs=per(heads, p, n),
+            scratch_shapes=[
+                pltpu.VMEM((requests * heads, p, n), F32),
+                pltpu.SemaphoreType.DMA((requests,)),
+            ],
+        ),
+        compiler_params=pltpu.CompilerParams(vmem_limit_bytes=60 * MIB),
+        cost_estimate=pl.CostEstimate(
+            flops=2 * requests * width * n * 32, bytes_accessed=6 * MIB, transcendentals=0
+        ),
+        name="finals",
+    )(pos, back, grow, b, el, f1)
 
 
 def norm_kernel(channels, g_ref, s0_ref, s1_ref, s2_ref, s3_ref, gain_ref, out_ref):
@@ -559,7 +626,7 @@
         grid=(tokens // seq,),
         in_specs=[rows] + [full(parts[0].shape)] * 4 + [full(gain.shape)],
         out_specs=rows,
-        compiler_params=pltpu.CompilerParams(vmem_limit_bytes=8 * MIB),
+        compiler_params=pltpu.CompilerParams(vmem_limit_bytes=60 * MIB),
         cost_estimate=pl.CostEstimate(flops=2 * tokens * width, bytes_accessed=4 * MIB, transcendentals=0),
         name="normalise",
     )(g, *parts, gain)
@@ -608,7 +675,9 @@
         decay_rate[None],
         jnp.repeat(skip_scale, p)[None],
     )
-    g, square, final = tail(pos, back, az, ez, c, b, f1, el, first, inner_kernel)
+    b = b.reshape(-1, n)
+    g, square, grow = tail(pos, back, az, ez, c, b, el, first, inner_kernel)
+    final = finals(pos, back, grow, b, el, f1)
     pair = [(i, i ^ 1) for i in range(groups)]
     square = square + lax.ppermute(square, "mp", pair)
     parts = [square] + [

time: 230 us -> 112 us (0.49)
  Pallas kernels: 182 us -> 68.4 us
  waiting for transfers between devices: 9.48 us -> 3.97 us
    pallas_call x1, Pallas kernels: 129 us -> 3.5 us  [pick(): pl.pallas_call(pick_kernel, out_shape=jax.ShapeDtypeStruct((owners, CAP *...]
    pallas_call x0 -> x1, Pallas kernels: none -> 6.07 us  [finals(): pl.pallas_call(final_kernel, out_shape=jax.ShapeDtypeStruct((requests, he...]
    all_to_all x1, waiting for transfers between devices: 6.11 us -> 2.59 us  [local(): back = lax.all_to_all(sent, 'dp', split_axis=0, concat_axis=0, tiled=True)]
    pallas_call x1, Pallas kernels: 15.1 us -> 17.7 us  [ssd(): pl.pallas_call(ssd_kernel, out_shape=(jax.ShapeDtypeStruct((tokens, width...]
    unnamed x32 -> x30, local copies, waits for them, and re-layouts: 11.3 us -> 9.35 us
  transfers between devices with their start and end apart: 5 -> 5, of which waited for: 4 -> 2; matrix products, arithmetic and copies ran while one was open for 0% -> 2% of each run, Pallas kernels for 18% -> 45%
where the time goes in v2:
time: 112 us; the launch traced here: 111 us
  Pallas kernels  68.4 us (61%)
  blocking collectives  15.6 us (14%)
  local copies, waits for them, and re-layouts  10.7 us (10%)
  starting transfers between devices  10.4 us (9%)
  waiting for transfers between devices  3.97 us (4%)
    pallas_call x1, Pallas kernels, project(): pl.pallas_call(functools.partial(project_kernel, steps), out_shape=(jax.S...  26.3 us
    pallas_call x1, Pallas kernels, ssd(): pl.pallas_call(ssd_kernel, out_shape=(jax.ShapeDtypeStruct((tokens, width...  17.7 us
    all_to_all x1, blocking collectives, local(): lax.all_to_all(wanted, 'dp', split_axis=0, concat_axis=0, tiled=True)  15.6 us
    unnamed x30, local copies, waits for them, and re-layouts  9.35 us
    pallas_call x1, Pallas kernels, tail(): pl.pallas_call(tail_kernel, out_shape=(jax.ShapeDtypeStruct((tokens, widt...  8.87 us
    pallas_call x1, Pallas kernels, finals(): pl.pallas_call(final_kernel, out_shape=jax.ShapeDtypeStruct((requests, he...  6.07 us
    ppermute x3, starting transfers between devices, local(): lax.ppermute(square, 'mp', [(i, (i + 2 * s) % groups) for i in range(grou...  5.66 us
    all_to_all x1, starting transfers between devices, local(): back = lax.all_to_all(sent, 'dp', split_axis=0, concat_axis=0, tiled=True)  4.68 us
  transfers between devices with their start and end apart: 5, of which 2 were waited for; matrix products, arithmetic and copies ran while one was open for 2% of the time, Pallas kernels for 45%

profile of v2, /device:TPU:0, one launch (start us, length us, event | category | flops | bytes accessed | tf_op | source)
XLA Modules:
  0.0 110.6 jit_solution(7815426842613173196)
XLA Ops:
  0.6 1.8 %prep.1 = (s32[16,1,128]{2,1,0:T(1,128)}, s32[64]{0:T(128)}) custom-call(s32[4,16]{1,0:T(4,128)} %owner_ref.1, s32[4,16]{1,0:T(4,128)} %slot_ref.1), custom_call_target="tpu_custom_call" | custom-call | tf_op jit(solution)/shard_map/prep/pallas_call | solution.py:45
  2.4 15.6 %all_to_all.10.codes_ref = s32[16,1,128]{2,1,0:T(1,128)} all-to-all(s32[16,1,128]{2,1,0:T(1,128)} %get-tuple-element.19), channel_id=1, replica_groups=mesh['dp'=16,'mp'=8] {'dp'}, dimensions={0} | all-to-all | bytes 16384 | tf_op jit(solution)/shard_map/all_to_all | solution.py:661
  18.0 3.5 %pick.1 = f32[16,528,128]{2,1,0:T(8,128)} custom-call(s32[16,1,128]{2,1,0:T(1,128)} %all_to_all.10.codes_ref, f32[48,64,128]{2,1,0:T(8,128)} %bitcast.5, bf16[48,192]{1,0:T(8,128)(2,1)} %bitcast.8), custom_call_target="tpu_custom_call" | custom-call | bytes 8388608 | tf_op jit(solution)/shard_map/pick/pallas_call | solution.py:92
  21.5 0.0 copy-start.13
  21.6 0.0 copy-start.11
  21.6 4.7 %all-to-all-start.1 = ((f32[16,528,128]{2,1,0:T(8,128)}), f32[16,528,128]{2,1,0:T(8,128)}, u32[]{:S(2)}, u32[]{:S(2)}) async-start(f32[16,528,128]{2,1,0:T(8,128)} %pick.1), calls=%async_computation.1 | async-start | bytes 8650752 | tf_op jit(solution)/shard_map/all_to_all | solution.py:663
  26.3 0.5 copy.18.wd_ref
  26.8 0.1 broadcast_in_dim.14
  26.8 0.7 broadcast_in_dim_reshape.3.skip_ref
  27.5 0.6 copy.19.hist_ref
  28.1 3.4 %copy-done = bf16[1024,4096]{1,0:T(8,128)(2,1)S(1)} copy-done((bf16[1024,4096]{1,0:T(8,128)(2,1)S(1)}, bf16[1024,4096]{1,0:T(8,128)(2,1)}, u32[]{:S(2)}) %copy-start) | copy-done | bytes 8388632
  31.5 26.3 %project.1 = (bf16[1024,1024]{1,0:T(8,128)(2,1)S(1)}, bf16[1024,1024]{1,0:T(8,128)(2,1)S(1)}, bf16[1024,256]{1,0:T(8,128)(2,1)S(1)}, f32[1024,16]{1,0:T(8,128)S(1)}) custom-call(bf16[1024,4096]{1,0:T(8,128)(2,1)S(1)} %copy-done, bf16[4096,1024]{1,0:T(8,128)(2,1)} %wi_ref.1, bf16[4096,1024]{1,0:T(8,128)(2,1)} %wg_ref.1, bf16[4096,256]{1,0:T(8,128)(2,1)S(1)} %copy-done.1, ...), custom_call_target="tpu_custom_call" | custom-call | flops 19461570560 | bytes 33554432 | tf_op jit(solution)/shard_map/project/pallas_call | solution.py:153
  57.8 0.0 copy-start.2
  57.8 1.3 %copy-done.2 = bf16[1024,1024]{1,0:T(8,128)(2,1)} copy-done((bf16[1024,1024]{1,0:T(8,128)(2,1)}, bf16[1024,1024]{1,0:T(8,128)(2,1)S(1)}, u32[]{:S(2)}) %copy-start.2) | copy-done | bytes 2097176
  59.1 1.3 %copy-done.3 = bf16[1024,1024]{1,0:T(8,128)(2,1)} copy-done((bf16[1024,1024]{1,0:T(8,128)(2,1)}, bf16[1024,1024]{1,0:T(8,128)(2,1)S(1)}, u32[]{:S(2)}) %copy-start.3) | copy-done | bytes 2097176
  60.4 0.8 copy-done.4
  61.3 0.8 copy-done.5
  62.1 17.7 %ssd.1 = (bf16[1024,1024]{1,0:T(8,128)(2,1)}, bf16[1024,1024]{1,0:T(8,128)(2,1)}, bf16[1024,128]{1,0:T(8,128)(2,1)}, f32[4,8,128]{2,1,0:T(8,128)}, f32[4,1024,12...) custom-call(bf16[1024,1024]{1,0:T(8,128)(2,1)} %copy-done.2, bf16[1024,1024]{1,0:T(8,128)(2,1)} %copy-done.3, ...), custom_call_target="tpu_custom_call" | custom-call | flops 1073741824 | bytes 14680064 | tf_op jit(solution)/shard_map/ssd/pallas_call | solution.py:325
  79.8 2.6 %all-to-all-done.1.back_ref = f32[16,528,128]{2,1,0:T(8,128)} async-done(((f32[16,528,128]{2,1,0:T(8,128)}), f32[16,528,128]{2,1,0:T(8,128)}, u32[]{:S(2)}, u32[]{:S(2)}) %all-to-all-start.1) | async-done | bytes 4325408 | tf_op jit(solution)/shard_map/all_to_all | solution.py:663
  82.4 8.9 %tail.1 = (bf16[1024,1024]{1,0:T(8,128)(2,1)}, f32[8,256]{1,0:T(8,128)}, bf16[1024,32]{1,0:T(8,128)(2,1)}) custom-call(s32[64]{0:T(128)} %get-tuple-element.18.pos_ref, f32[16,528,128]{2,1,0:T(8,128)} %all-to-all-done.1.back_ref, bf16[1024,1024]{1,0:T(8,128)(2,1)} %get-tuple-element.24.az_ref, bf16[1024,1024]{1,0:T(8,128)(2,1)} %get-tuple-element.25.ez_ref, ...), custom_call_target="tpu_custom_call" | custom-call | flops 268435456 | bytes 10485760 | tf_op jit(solution)/shard_map/tail/pallas_call | solution.py:508
  91.3 0.1 collective-permute-start
  91.4 1.4 %collective-permute-done = f32[8,256]{1,0:T(8,128)S(1)} collective-permute-done((f32[8,256]{1,0:T(8,128)}, f32[8,256]{1,0:T(8,128)S(1)}, u32[]{:S(2)}, u32[]{:S(2)}) %collective-permute-start) | collective-permute-done | bytes 8224 | tf_op jit(solution)/shard_map/ppermute | solution.py:682
  92.7 0.7 add.3.s0_ref
  93.4 1.5 %collective-permute-start.1 = (f32[8,256]{1,0:T(8,128)S(1)}, f32[8,256]{1,0:T(8,128)S(1)}, u32[]{:S(2)}, u32[]{:S(2)}) collective-permute-start(f32[8,256]{1,0:T(8,128)S(1)} %add.3.s0_ref), channel_id=1, source_target_pairs={{0,2},{1,3},{2,4},{3,5},{4,6},{5,7},{6,0},{7,1},{8,10},{9,11},{10,... | collective-permute-start | bytes 24584 | tf_op jit(solution)/shard_map/ppermute | solution.py:684
  94.9 2.7 %collective-permute-start.2 = (f32[8,256]{1,0:T(8,128)S(1)}, f32[8,256]{1,0:T(8,128)S(1)}, u32[]{:S(2)}, u32[]{:S(2)}) collective-permute-start(f32[8,256]{1,0:T(8,128)S(1)} %add.3.s0_ref), channel_id=1, source_target_pairs={{0,4},{1,5},{2,6},{3,7},{4,0},{5,1},{6,2},{7,3},{8,12},{9,13},{10,... | collective-permute-start | bytes 24584 | tf_op jit(solution)/shard_map/ppermute | solution.py:684
  97.6 1.4 %collective-permute-start.3 = (f32[8,256]{1,0:T(8,128)S(1)}, f32[8,256]{1,0:T(8,128)S(1)}, u32[]{:S(2)}, u32[]{:S(2)}) collective-permute-start(f32[8,256]{1,0:T(8,128)S(1)} %add.3.s0_ref), channel_id=1, source_target_pairs={{0,6},{1,7},{2,0},{3,1},{4,2},{5,3},{6,4},{7,5},{8,14},{9,15},{10,... | collective-permute-start | bytes 24584 | tf_op jit(solution)/shard_map/ppermute | solution.py:684
  99.1 0.6 broadcast_in_dim.15.gain_ref
  99.7 6.1 %finals.1 = f32[4,16,64,128]{3,2,1,0:T(8,128)} custom-call(s32[64]{0:T(128)} %get-tuple-element.18.pos_ref, f32[16,528,128]{2,1,0:T(8,128)} %all-to-all-done.1.back_ref, bf16[1024,32]{1,0:T(8,128)(2,1)} %get-tuple-element.32.grow_ref, f32[32,128]{1,0:T(8,128)} %bitcast.7, f32[4,32,128]{2,1,0:T(8,128)} %get-tuple-element.28.el_ref, ...), custom_call_target="tpu_custom_call" | custom-call | flops 33554432 | bytes 6291456 | tf_op jit(solution)/shard_map/finals/pallas_call | solution.py:579
  105.8 0.5 copy-done.8
  106.4 0.0 copy-done.9
  106.4 0.0 copy-done.10
  106.4 4.2 %normalise.1 = bf16[1024,1024]{1,0:T(8,128)(2,1)} custom-call(bf16[1024,1024]{1,0:T(8,128)(2,1)} %get-tuple-element.30.g_ref, f32[8,256]{1,0:T(8,128)} %copy-done.7, f32[8,256]{1,0:T(8,128)} %copy-done.8, f32[8,256]{1,0:T(8,128)} %copy-done.9, f32[8,256]{1,0:T(8,128)} %copy-done.10, bf16[1,1024]{1,0:T(2,128)(2,1)} %broadcast_in_dim.15.gain_ref), custom_call_target="tpu_custom_call" | custom-call | flops 2097152 | bytes 4194304 | tf_op jit(solution)/shard_map/normalise/pallas_call | solution.py:623
  (20 shorter events, 0.0 us)
Async XLA Ops:
  21.5 4.7 %copy-start.6 = (bf16[4096,16]{0,1:T(8,128)(2,1)S(1)}, bf16[4096,16]{0,1:T(8,128)(2,1)}, u32[]{:S(2)}) copy-start(bf16[4096,16]{0,1:T(8,128)(2,1)} %param.20) | copy-start | bytes 393220
  21.5 5.2 %copy-start.13 = (f32[16]{0:T(128)S(1)}, f32[16]{0:T(128)}, u32[]{:S(2)}) copy-start(f32[16]{0:T(128)} %param.25) | copy-start | bytes 196
  21.6 6.0 %copy-start.11 = (bf16[4,3,256]{2,0,1:T(4,128)(2,1)S(1)}, bf16[4,3,256]{2,0,1:T(4,128)(2,1)}, u32[]{:S(2)}) copy-start(bf16[4,3,256]{2,0,1:T(4,128)(2,1)} %param.29) | copy-start | bytes 18436
  21.6 6.5 %copy-start.1 = (bf16[4096,256]{1,0:T(8,128)(2,1)S(1)}, bf16[4096,256]{1,0:T(8,128)(2,1)}, u32[]{:S(2)}) copy-start(bf16[4096,256]{1,0:T(8,128)(2,1)} %ws_ref.1) | copy-start | bytes 6291460
  21.6 60.8 %all-to-all-start.1 = ((f32[16,528,128]{2,1,0:T(8,128)}), f32[16,528,128]{2,1,0:T(8,128)}, u32[]{:S(2)}, u32[]{:S(2)}) async-start(f32[16,528,128]{2,1,0:T(8,128)} %pick.1), calls=%async_computation.1 | async-start | bytes 8650752 | tf_op jit(solution)/shard_map/all_to_all | solution.py:663
  28.1 3.4 %copy-start = (bf16[1024,4096]{1,0:T(8,128)(2,1)S(1)}, bf16[1024,4096]{1,0:T(8,128)(2,1)}, u32[]{:S(2)}) copy-start(bf16[1024,4096]{1,0:T(8,128)(2,1)} %act_ref.1) | copy-start | bytes 25165828
  57.8 1.3 %copy-start.2 = (bf16[1024,1024]{1,0:T(8,128)(2,1)}, bf16[1024,1024]{1,0:T(8,128)(2,1)S(1)}, u32[]{:S(2)}) copy-start(bf16[1024,1024]{1,0:T(8,128)(2,1)S(1)} %get-tuple-element.20.inner_ref) | copy-start | bytes 6291460
  59.1 1.3 %copy-start.3 = (bf16[1024,1024]{1,0:T(8,128)(2,1)}, bf16[1024,1024]{1,0:T(8,128)(2,1)S(1)}, u32[]{:S(2)}) copy-start(bf16[1024,1024]{1,0:T(8,128)(2,1)S(1)} %get-tuple-element.21.gate_ref) | copy-start | bytes 6291460
  60.4 0.8 copy-start.4
  61.3 0.8 copy-start.5
  82.4 16.7 %copy-start.12 = (bf16[1024]{0:T(1024)(128)(2,1)S(1)}, bf16[1024]{0:T(1024)(128)(2,1)}, u32[]{:S(2)}) copy-start(bf16[1024]{0:T(1024)(128)(2,1)} %param.26) | copy-start | bytes 6148
  91.3 1.5 %collective-permute-start = (f32[8,256]{1,0:T(8,128)}, f32[8,256]{1,0:T(8,128)S(1)}, u32[]{:S(2)}, u32[]{:S(2)}) collective-permute-start(f32[8,256]{1,0:T(8,128)} %get-tuple-element.31), channel_id=1, source_target_pairs={{0,1},{1,0},{2,3},{3,2},{4,5},{5,4},{6,7},{7,6},{8,9},{9,8},{10,11... | collective-permute-start | bytes 24584 | tf_op jit(solution)/shard_map/ppermute | solution.py:682
  93.4 12.3 %copy-start.7 = (f32[8,256]{1,0:T(8,128)}, f32[8,256]{1,0:T(8,128)S(1)}, u32[]{:S(2)}) copy-start(f32[8,256]{1,0:T(8,128)S(1)} %add.3.s0_ref) | copy-start | bytes 24580
  93.4 12.3 %collective-permute-start.1 = (f32[8,256]{1,0:T(8,128)S(1)}, f32[8,256]{1,0:T(8,128)S(1)}, u32[]{:S(2)}, u32[]{:S(2)}) collective-permute-start(f32[8,256]{1,0:T(8,128)S(1)} %add.3.s0_ref), channel_id=1, source_target_pairs={{0,2},{1,3},{2,4},{3,5},{4,6},{5,7},{6,0},{7,1},{8,10},{9,11},{10,... | collective-permute-start | bytes 24584 | tf_op jit(solution)/shard_map/ppermute | solution.py:684
  94.9 10.9 %collective-permute-start.2 = (f32[8,256]{1,0:T(8,128)S(1)}, f32[8,256]{1,0:T(8,128)S(1)}, u32[]{:S(2)}, u32[]{:S(2)}) collective-permute-start(f32[8,256]{1,0:T(8,128)S(1)} %add.3.s0_ref), channel_id=1, source_target_pairs={{0,4},{1,5},{2,6},{3,7},{4,0},{5,1},{6,2},{7,3},{8,12},{9,13},{10,... | collective-permute-start | bytes 24584 | tf_op jit(solution)/shard_map/ppermute | solution.py:684
  97.6 8.2 %collective-permute-start.3 = (f32[8,256]{1,0:T(8,128)S(1)}, f32[8,256]{1,0:T(8,128)S(1)}, u32[]{:S(2)}, u32[]{:S(2)}) collective-permute-start(f32[8,256]{1,0:T(8,128)S(1)} %add.3.s0_ref), channel_id=1, source_target_pairs={{0,6},{1,7},{2,0},{3,1},{4,2},{5,3},{6,4},{7,5},{8,14},{9,15},{10,... | collective-permute-start | bytes 24584 | tf_op jit(solution)/shard_map/ppermute | solution.py:684
  105.8 0.6 copy-start.8
  105.8 0.6 copy-start.9
  105.8 0.6 copy-start.10

commit v3 on v1

--- a/solution.py
+++ b/solution.py
@@ -94,7 +94,7 @@
         out_shape=jax.ShapeDtypeStruct((owners, CAP * p + 2 * CAP, n), F32),
         in_specs=[
             pl.BlockSpec(memory_space=pltpu.SMEM),
-            pl.BlockSpec(memory_space=pl.ANY),
+            pl.BlockSpec(memory_space=pltpu.VMEM),
             pl.BlockSpec(memory_space=pltpu.VMEM),
         ],
         out_specs=pl.BlockSpec(memory_space=pl.ANY),
@@ -172,7 +172,7 @@
             full((rows, ws.shape[1])),
             full((rows, wd.shape[1])),
         ),
-        compiler_params=pltpu.CompilerParams(vmem_limit_bytes=36 * MIB),
+        compiler_params=pltpu.CompilerParams(vmem_limit_bytes=60 * MIB),
         cost_estimate=pl.CostEstimate(flops=flops, bytes_accessed=32 * MIB, transcendentals=0),
         name="project",
     )(act, wi, wg, ws, wd)
@@ -192,9 +192,8 @@
     az_ref,
     ez_ref,
     c_ref,
-    b_ref,
     f1_ref,
-    el_ref,
+    small_ref,
     first_ref,
     u_ref,
     v_ref,
@@ -218,7 +217,7 @@
     b = conv[:, :n]
     c = conv[:, n:]
     c_ref[...] = c
-    b_ref[0] = b[:16].astype(F32)[:8]
+    small_ref[0, 2 * heads :] = b[:16].astype(F32)[:8]
 
     raw = step_ref[...] + bias_ref[...]
     dt = jnp.maximum(raw, 0.0) + jnp.log1p(jnp.exp(-jnp.abs(raw)))
@@ -244,8 +243,8 @@
     tail = jnp.exp(jnp.minimum(last - cum, 0.0)) * dt
     begin_t = cum_t[:heads, lag - 1 : lag]
     last_t = cum_t[:heads, seq - 1 : seq]
-    el_ref[0, :heads] = jnp.broadcast_to(jnp.exp(jnp.minimum(last_t - begin_t, 0.0)), (heads, n))
-    el_ref[0, heads:] = jnp.broadcast_to(jnp.exp(begin_t), (heads, n))
+    small_ref[0, :heads] = jnp.broadcast_to(jnp.exp(jnp.minimum(last_t - begin_t, 0.0)), (heads, n))
+    small_ref[0, heads : 2 * heads] = jnp.broadcast_to(jnp.exp(begin_t), (heads, n))
 
     scores = lax.dot_general(c, b, (((1,), (1,)), ((), ())), preferred_element_type=F32)
     scores = jnp.where(causal, scores, 0.0)
@@ -305,6 +304,7 @@
         )
         wide = jnp.dot(small, spread[:, cols], preferred_element_type=F32)
         first_ref[0, 0:8, cols] = run[:8]
+        first_ref[0, 16 + 8 * lag : 16 + 8 * lag + taps, cols] = ik
         first_ref[0, 8:16, cols] = wide[:8]
         z8 = z[:8]
         first_ref[0, 16:24, cols] = jnp.where(row8 < lag, (wide[8:16] + skip) * z8, 0.0)
@@ -328,10 +328,9 @@
             jax.ShapeDtypeStruct((tokens, width), BF16),
             jax.ShapeDtypeStruct((tokens, width), BF16),
             jax.ShapeDtypeStruct((tokens, n), BF16),
-            jax.ShapeDtypeStruct((requests, 8, n), F32),
             jax.ShapeDtypeStruct((requests, width, n), F32),
-            jax.ShapeDtypeStruct((requests, 2 * heads, n), F32),
-            jax.ShapeDtypeStruct((requests, 16 + 8 * lag, width), F32),
+            jax.ShapeDtypeStruct((requests, 2 * heads + 8, n), F32),
+            jax.ShapeDtypeStruct((requests, 24 + 8 * lag, width), F32),
         ),
         grid=(requests,),
         in_specs=[
@@ -350,215 +349,306 @@
             rows(width),
             rows(width),
             rows(n),
-            per(8, n),
             per(width, n),
-            per(2 * heads, n),
-            per(16 + 8 * lag, width),
+            per(2 * heads + 8, n),
+            per(24 + 8 * lag, width),
         ),
         scratch_shapes=[pltpu.VMEM((seq + 8, width), F32), pltpu.VMEM((seq + 8, n2), F32)],
-        compiler_params=pltpu.CompilerParams(vmem_limit_bytes=24 * MIB),
+        compiler_params=pltpu.CompilerParams(vmem_limit_bytes=60 * MIB),
         cost_estimate=pl.CostEstimate(
             flops=2 * tokens * width * seq * 2, bytes_accessed=14 * MIB, transcendentals=tokens * seq * heads
         ),
         name="ssd",
     )(inner, gate, state, step, history, ik, sk, bias, decay, skip)
+
+
+def first_sources(grow_ref, small_ref, r):
+    requests = small_ref.shape[0]
+    b = small_ref[r, small_ref.shape[1] - 8 :]
+    zero = jnp.zeros_like(b)
+    b = jnp.concatenate([b if i == r else zero for i in range(requests)], axis=0).astype(BF16)
+    return jnp.dot(grow_ref[...], b, preferred_element_type=F32)
 
 
 def tail_kernel(
     pos_ref,
     back_ref,
+    az_hbm,
+    ez_hbm,
+    c_hbm,
+    small_hbm,
+    first_hbm,
+    g_ref,
+    sq_ref,
+    grow_ref,
+    held_ref,
     az_ref,
     ez_ref,
     c_ref,
-    b_ref,
-    f1_ref,
-    el_ref,
+    small_ref,
     first_ref,
-    ik_ref,
-    g_ref,
-    sq_ref,
-    final_ref,
-    held_ref,
     rows_ref,
     s_ref,
     raw_ref,
     win_ref,
     mix_ref,
     x_ref,
+    extra_ref,
     sem,
-    row_sem,
+    az_sem,
+    ez_sem,
+    c_sem,
+    once_sem,
 ):
-    r = pl.program_id(0)
-    requests = pl.num_programs(0)
-    heads = el_ref.shape[1] // 2
+    requests = first_ref.shape[0]
+    heads = (small_ref.shape[1] - 8) // 2
     p = held_ref.shape[1]
-    seq, width = az_ref.shape
-    lag = ik_ref.shape[0] - 1
-    cached = CAP * p
-
-    def fetch(q):
+    tokens, width = g_ref.shape
+    seq = tokens // requests
+    lag = (first_ref.shape[1] - 24) // 8
+    pairs = heads // 2
+
+    def rows_of(r):
+        return slice(r * seq, r * seq + seq)
+
+    def copies(r):
+        return (
+            pltpu.make_async_copy(az_hbm.at[rows_of(r)], az_ref.at[rows_of(r)], az_sem.at[r]),
+            pltpu.make_async_copy(ez_hbm.at[rows_of(r)], ez_ref.at[rows_of(r)], ez_sem.at[r]),
+            pltpu.make_async_copy(c_hbm.at[rows_of(r)], c_ref.at[rows_of(r)], c_sem.at[r]),
+        )
+
+    def fetch(r):
         for h in range(heads):
-            e = q * heads + h
+            e = r * heads + h
             at = pos_ref[e]
             pltpu.make_async_copy(
                 back_ref.at[at // CAP, pl.ds(pl.multiple_of((at % CAP) * p, p), p)],
                 held_ref.at[e],
-                sem.at[q],
+                sem.at[r],
             ).start()
-
-    row_copy = pltpu.make_async_copy(back_ref.at[:, cached:], rows_ref, row_sem)
-
-    @pl.when(r == 0)
-    def _():
-        row_copy.start()
-        fetch(0)
-        sq_ref[...] = jnp.zeros_like(sq_ref)
-        win_ref[...] = jnp.zeros_like(win_ref)
-        x_ref[...] = jnp.zeros_like(x_ref)
-        row_copy.wait()
-
-    @pl.when(r + 1 < requests)
-    def _():
-        fetch(r + 1)
+        for copy in copies(r):
+            copy.start()
+
+    once = (
+        pltpu.make_async_copy(back_ref.at[:, CAP * p :], rows_ref, once_sem.at[0]),
+        pltpu.make_async_copy(first_hbm, first_ref, once_sem.at[1]),
+        pltpu.make_async_copy(small_hbm, small_ref, once_sem.at[2]),
+    )
+    for copy in once:
+        copy.start()
+    fetch(0)
+    fetch(1)
+    win_ref[...] = jnp.zeros_like(win_ref)
+    x_ref[...] = jnp.zeros_like(x_ref)
+    once[0].wait()
 
     low = lax.broadcasted_iota(jnp.int32, (1, 128), 1) < p
     flat = rows_ref.reshape(rows_ref.shape[0] * rows_ref.shape[1], 128)
-    for q in range(heads // 2):
-        cols = slice(q * 128, q * 128 + 128)
-        even = 2 * pos_ref[r * heads + 2 * q]
-        odd = 2 * pos_ref[r * heads + 2 * q + 1]
-        a0, a1 = flat[pl.ds(even, 1)], flat[pl.ds(odd, 1)]
-        b0, b1 = flat[pl.ds(even + 1, 1)], flat[pl.ds(odd + 1, 1)]
-        win_ref[0:1, cols] = jnp.where(low, a0, a1)
-        win_ref[2:3, cols] = jnp.where(low, b0, b1)
-        mix_ref[q : q + 1] = jnp.where(low, a1, a0)
+    for i in range(requests):
+        for q in range(pairs):
+            cols = slice(q * 128, q * 128 + 128)
+            even = 2 * pos_ref[i * heads + 2 * q]
+            odd = 2 * pos_ref[i * heads + 2 * q + 1]
+            a0, a1 = flat[pl.ds(even, 1)], flat[pl.ds(odd, 1)]
+            b0, b1 = flat[pl.ds(even + 1, 1)], flat[pl.ds(odd + 1, 1)]
+            win_ref[i, 0:1, cols] = jnp.where(low, a0, a1)
+            win_ref[i, 2:3, cols] = jnp.where(low, b0, b1)
+            mix_ref[i * pairs + q : i * pairs + q + 1] = jnp.where(low, a1, a0)
     mix = pltpu.roll(mix_ref[...], p, 1)
-    for q in range(heads // 2):
-        win_ref[1:2, q * 128 : q * 128 + 128] = mix[q : q + 1]
-
-    ik = ik_ref[...].astype(F32)
-    run = first_ref[0, 0:8]
+    for i in range(requests):
+        for q in range(pairs):
+            win_ref[i, 1:2, q * 128 : q * 128 + 128] = mix[i * pairs + q : i * pairs + q + 1]
+
+    once[1].wait()
+    run = first_ref[:, 0:8]
     for k in range(lag):
-        run = run + ik[k : k + 1] * win_ref[k : k + 8]
-    row8 = lax.broadcasted_iota(jnp.int32, (8, width), 0)
+        at = 16 + 8 * lag + k
+        run = run + first_ref[:, at : at + 1] * win_ref[:, k : k + 8]
+    row8 = lax.broadcasted_iota(jnp.int32, run.shape, 1)
     x = jnp.where(row8 < lag, silu(run), 0.0).astype(BF16).astype(F32)
-    x_ref[8:16] = x
-    extra = first_ref[0, 16:24] * x
+    x_ref[:, 8:16] = x
+    extra = first_ref[:, 16:24] * x
     for j in range(1, lag):
-        extra = extra + first_ref[0, 16 + 8 * j : 24 + 8 * j] * x_ref[8 - j : 16 - j]
-    grow = (x * first_ref[0, 8:16]).T.astype(BF16)
-    add = jnp.dot(grow, b_ref[0].astype(BF16), preferred_element_type=F32)
-
-    pltpu.make_async_copy(
-        held_ref.at[pl.ds(r * heads, heads)], held_ref.at[pl.ds(r * heads, heads)], sem.at[r]
-    ).wait()
-    for h in range(heads):
-        at = slice(h * p, h * p + p)
-        block = held_ref[r * heads + h]
-        raw_ref[at] = block.astype(BF16)
-        block = el_ref[0, heads + h : heads + h + 1] * block + add[at]
-        s_ref[at] = block.astype(BF16)
-        final_ref[0, h] = el_ref[0, h : h + 1] * block + f1_ref[0, at]
-
-    c = c_ref[...]
-    total = jnp.zeros((seq - 16, 128), F32)
-    total16 = jnp.zeros((16, 128), F32)
+        extra = extra + first_ref[:, 16 + 8 * j : 24 + 8 * j] * x_ref[:, 8 - j : 16 - j]
+    extra_ref[...] = extra
+    grow_ref[...] = (x * first_ref[:, 8:16]).reshape(requests * 8, width).T.astype(BF16)
+
+    for r in range(2, requests):
+        fetch(r)
+
+    once[2].wait()
     row16 = lax.broadcasted_iota(jnp.int32, (16, 256), 0)
     nt = (((1,), (1,)), ((), ()))
-    for q in range(width // 256):
-        cols = slice(q * 256, q * 256 + 256)
-        seen = lax.dot_general(c, s_ref[cols], nt, preferred_element_type=F32)
-        seen16 = lax.dot_general(c[:16], raw_ref[cols], nt, preferred_element_type=F32)
-        seen16 = jnp.where(row16 < lag, seen16, seen[:16])
-        az = az_ref[:, cols].astype(F32)
-        ez = ez_ref[:, cols].astype(F32)
-        g = az[16:] + ez[16:] * seen[16:]
-        g16 = az[:16] + ez[:16] * seen16
-        g16 = g16 + jnp.concatenate([extra[:, cols], jnp.zeros((8, 256), F32)], axis=0)
-        g_ref[:16, cols] = g16.astype(BF16)
-        g_ref[16:, cols] = g.astype(BF16)
-        g = g * g
-        g16 = g16 * g16
-        total = total + g[:, :128] + g[:, 128:]
-        total16 = total16 + g16[:, :128] + g16[:, 128:]
-    total = jnp.concatenate([total16, total], axis=0)
-    sq_ref[pl.ds(r, 1), :] = jnp.sum(total.T, axis=0, keepdims=True)
-
-
-def tail(pos, back, az, ez, c, b, f1, el, first, ik):
-    requests, heads2, n = el.shape
-    heads = heads2 // 2
+    squares = []
+    for r in range(requests):
+        rows = rows_of(r)
+        add = first_sources(grow_ref, small_ref, r)
+        part = held_ref.at[r * heads : r * heads + heads]
+        pltpu.make_async_copy(part, part, sem.at[r]).wait()
+        for h in range(heads):
+            at = slice(h * p, h * p + p)
+            block = held_ref[r * heads + h]
+            raw_ref[r % 2, at] = block.astype(BF16)
+            s_ref[r % 2, at] = (small_ref[r, heads + h : heads + h + 1] * block + add[at]).astype(BF16)
+        for copy in copies(r):
+            copy.wait()
+        c = c_ref[rows]
+        total = jnp.zeros((seq - 16, 128), F32)
+        total16 = jnp.zeros((16, 128), F32)
+        for q in range(width // 256):
+            cols = slice(q * 256, q * 256 + 256)
+            seen = lax.dot_general(c, s_ref[r % 2, cols], nt, preferred_element_type=F32)
+            seen16 = lax.dot_general(c[:16], raw_ref[r % 2, cols], nt, preferred_element_type=F32)
+            seen16 = jnp.where(row16 < lag, seen16, seen[:16])
+            az = az_ref[rows, cols].astype(F32)
+            ez = ez_ref[rows, cols].astype(F32)
+            g = az[16:] + ez[16:] * seen[16:]
+            g16 = az[:16] + ez[:16] * seen16
+            g16 = g16 + jnp.concatenate([extra_ref[r, :, cols], jnp.zeros((8, 256), F32)], axis=0)
+            g_ref[r * seq : r * seq + 16, cols] = g16.astype(BF16)
+            g_ref[r * seq + 16 : r * seq + seq, cols] = g.astype(BF16)
+            g = g * g
+            g16 = g16 * g16
+            total = total + g[:, :128] + g[:, 128:]
+            total16 = total16 + g16[:, :128] + g16[:, 128:]
+        total = jnp.concatenate([total16, total], axis=0)
+        squares.append(jnp.sum(total.T, axis=0, keepdims=True))
+    squares.append(jnp.zeros((8 - requests, seq), F32))
+    sq_ref[...] = jnp.concatenate(squares, axis=0)
+
+
+def in_hbm(*arrays):
+    return [pltpu.with_memory_space_constraint(v, pltpu.HBM) for v in arrays]
+
+
+def tail(pos, back, az, ez, c, small, first):
+    requests, packed, n = small.shape
+    heads = (packed - 8) // 2
     tokens, width = az.shape
     p = width // heads
     seq = tokens // requests
     owners = back.shape[0]
-    rows = lambda w: pl.BlockSpec((seq, w), lambda r, _: (r, 0))
-    per = lambda *s: pl.BlockSpec((1,) + s, lambda r, _: (r,) + (0,) * len(s))
+    vmem = pl.BlockSpec(memory_space=pltpu.VMEM)
+    hbm = pl.BlockSpec(memory_space=pltpu.HBM)
     return pl.pallas_call(
         tail_kernel,
         out_shape=(
-            jax.ShapeDtypeStruct((tokens, width), BF16),
-            jax.ShapeDtypeStruct((8, seq), F32),
-            jax.ShapeDtypeStruct((requests, heads, p, n), F32),
-        ),
-        grid_spec=pltpu.PrefetchScalarGridSpec(
-            num_scalar_prefetch=1,
-            grid=(requests,),
-            in_specs=[
-                pl.BlockSpec(memory_space=pl.ANY),
-                rows(width),
-                rows(width),
-                rows(n),
-                per(*b.shape[1:]),
-                per(width, n),
-                per(heads2, n),
-                per(*first.shape[1:]),
-                full(ik.shape),
-            ],
-            out_specs=(rows(width), full((8, seq)), per(heads, p, n)),
-            scratch_shapes=[
-                pltpu.VMEM((requests * heads, p, n), F32),
-                pltpu.VMEM((owners, 2 * CAP, n), F32),
-                pltpu.VMEM((width, n), BF16),
-                pltpu.VMEM((width, n), BF16),
-                pltpu.VMEM((16, width), F32),
-                pltpu.VMEM((8, 128), F32),
-                pltpu.VMEM((16, width), F32),
-                pltpu.SemaphoreType.DMA((requests,)),
-                pltpu.SemaphoreType.DMA,
-            ],
-        ),
+            pltpu.VMEM((tokens, width), BF16),
+            pltpu.VMEM((8, seq), F32),
+            pltpu.VMEM((width, requests * 8), BF16),
+            pltpu.VMEM((requests * heads, p, n), F32),
+        ),
+        in_specs=[pl.BlockSpec(memory_space=pltpu.SMEM)] + [hbm] * 6,
+        out_specs=(vmem,) * 4,
+        scratch_shapes=[
+            pltpu.VMEM((tokens, width), BF16),
+            pltpu.VMEM((tokens, width), BF16),
+            pltpu.VMEM((tokens, n), BF16),
+            pltpu.VMEM(small.shape, F32),
+            pltpu.VMEM(first.shape, F32),
+            pltpu.VMEM((owners, 2 * CAP, n), F32),
+            pltpu.VMEM((2, width, n), BF16),
+            pltpu.VMEM((2, width, n), BF16),
+            pltpu.VMEM((requests, 16, width), F32),
+            pltpu.VMEM((requests * heads // 2, 128), F32),
+            pltpu.VMEM((requests, 16, width), F32),
+            pltpu.VMEM((requests, 8, width), F32),
+            pltpu.SemaphoreType.DMA((requests,)),
+            pltpu.SemaphoreType.DMA((requests,)),
+            pltpu.SemaphoreType.DMA((requests,)),
+            pltpu.SemaphoreType.DMA((requests,)),
+            pltpu.SemaphoreType.DMA((3,)),
+        ],
         compiler_params=pltpu.CompilerParams(vmem_limit_bytes=24 * MIB),
         cost_estimate=pl.CostEstimate(
-            flops=2 * tokens * width * n, bytes_accessed=14 * MIB, transcendentals=0
+            flops=2 * tokens * width * n, bytes_accessed=10 * MIB, transcendentals=0
         ),
         name="tail",
-    )(pos, back, az, ez, c, b, f1, el, first, ik)
-
-
-def norm_kernel(channels, g_ref, s0_ref, s1_ref, s2_ref, s3_ref, gain_ref, out_ref):
-    r = pl.program_id(0)
-    at = pl.ds(r, 1)
-    seq, width = g_ref.shape
-    square = s0_ref[at] + s1_ref[at] + s2_ref[at] + s3_ref[at]
+    )(pos, *in_hbm(back, az, ez, c, small, first))
+
+
+def final_kernel(held_ref, grow_ref, small_ref, f1_hbm, out_ref, f1_ref, made_ref, f1_sem, sem):
+    requests, heads, p = out_ref.shape[:3]
+
+    def part(r):
+        return pltpu.make_async_copy(f1_hbm.at[r], f1_ref.at[r], f1_sem.at[r])
+
+    for r in range(requests):
+        part(r).start()
+
+    def copy(r):
+        return pltpu.make_async_copy(made_ref.at[r], out_ref.at[r], sem.at[r])
+
+    for r in range(requests):
+        add = first_sources(grow_ref, small_ref, r)
+        part(r).wait()
+        for h in range(heads):
+            at = slice(h * p, h * p + p)
+            block = small_ref[r, heads + h : heads + h + 1] * held_ref[r * heads + h] + add[at]
+            made_ref[r, h] = small_ref[r, h : h + 1] * block + f1_ref[r, at]
+        copy(r).start()
+    for r in range(requests):
+        copy(r).wait()
+
+
+def finals(held, grow, small, f1):
+    requests, width, n = f1.shape
+    heads = (small.shape[1] - 8) // 2
+    p = width // heads
+    vmem = pl.BlockSpec(memory_space=pltpu.VMEM)
+    return pl.pallas_call(
+        final_kernel,
+        out_shape=jax.ShapeDtypeStruct((requests, heads, p, n), F32),
+        in_specs=[vmem] * 3 + [pl.BlockSpec(memory_space=pltpu.HBM)],
+        out_specs=pl.BlockSpec(memory_space=pltpu.HBM),
+        scratch_shapes=[
+            pltpu.VMEM((requests, width, n), F32),
+            pltpu.VMEM((requests, heads, p, n), F32),
+            pltpu.SemaphoreType.DMA((requests,)),
+            pltpu.SemaphoreType.DMA((requests,)),
+        ],
+        compiler_params=pltpu.CompilerParams(vmem_limit_bytes=16 * MIB),
+        cost_estimate=pl.CostEstimate(
+            flops=2 * requests * width * n * 32, bytes_accessed=6 * MIB, transcendentals=0
+        ),
+        name="finals",
+    )(held, grow, small, *in_hbm(f1))
+
+
+def norm_kernel(channels, g_ref, s0_ref, s1_ref, s2_ref, s3_ref, gain_ref, out_ref, made_ref, sem):
+    tokens, width = g_ref.shape
+    seq = s0_ref.shape[1]
+    step = 128
+    gain = gain_ref[...].astype(F32)
+    square = s0_ref[...] + s1_ref[...] + s2_ref[...] + s3_ref[...]
     scale = lax.rsqrt(square / channels + EPSILON)
-    scale = jnp.broadcast_to(scale, (128, seq)).T
-    gain = gain_ref[...].astype(F32)
-    for q in range(width // 128):
-        cols = slice(q * 128, q * 128 + 128)
-        out_ref[:, cols] = (g_ref[:, cols].astype(F32) * scale * gain[:, cols]).astype(BF16)
+
+    def copy(i):
+        rows = slice(i * step, i * step + step)
+        return pltpu.make_async_copy(made_ref.at[rows], out_ref.at[rows], sem.at[i])
+
+    for i in range(tokens // step):
+        rows = slice(i * step, i * step + step)
+        r, at = i * step // seq, i * step % seq
+        wide = jnp.broadcast_to(scale[r : r + 1, at : at + step], (128, step)).T
+        for q in range(width // 128):
+            cols = slice(q * 128, q * 128 + 128)
+            made_ref[rows, cols] = (g_ref[rows, cols].astype(F32) * wide * gain[:, cols]).astype(BF16)
+        copy(i).start()
+    for i in range(tokens // step):
+        copy(i).wait()
 
 
 def normalise(g, parts, gain, channels):
     tokens, width = g.shape
-    seq = parts[0].shape[1]
-    rows = pl.BlockSpec((seq, width), lambda r: (r, 0))
+    vmem = pl.BlockSpec(memory_space=pltpu.VMEM)
     return pl.pallas_call(
         functools.partial(norm_kernel, channels),
         out_shape=jax.ShapeDtypeStruct((tokens, width), BF16),
-        grid=(tokens // seq,),
-        in_specs=[rows] + [full(parts[0].shape)] * 4 + [full(gain.shape)],
-        out_specs=rows,
+        in_specs=[vmem] * 6,
+        out_specs=pl.BlockSpec(memory_space=pltpu.HBM),
+        scratch_shapes=[pltpu.VMEM((tokens, width), BF16), pltpu.SemaphoreType.DMA((tokens // 128,))],
         compiler_params=pltpu.CompilerParams(vmem_limit_bytes=8 * MIB),
         cost_estimate=pl.CostEstimate(flops=2 * tokens * width, bytes_accessed=4 * MIB, transcendentals=0),
         name="normalise",
@@ -596,7 +686,7 @@
     back = lax.all_to_all(sent, "dp", split_axis=0, concat_axis=0, tiled=True)
 
     inner, gate, state, step = project(activations, inner_weight, gate_weight, state_proj, step_weight)
-    az, ez, c, b, f1, el, first = ssd(
+    az, ez, c, f1, small, first = ssd(
         inner,
         gate,
         state,
@@ -608,7 +698,8 @@
         decay_rate[None],
         jnp.repeat(skip_scale, p)[None],
     )
-    g, square, final = tail(pos, back, az, ez, c, b, f1, el, first, inner_kernel)
+    g, square, grow, held = tail(pos, back, az, ez, c, small, first)
+    final = finals(held, grow, small, f1)
     pair = [(i, i ^ 1) for i in range(groups)]
     square = square + lax.ppermute(square, "mp", pair)
     parts = [square] + [

time: 230 us -> 99.8 us (0.43)
  Pallas kernels: 182 us -> 63.3 us
  local copies, waits for them, and re-layouts: 11.5 us -> 2.75 us
  waiting for transfers between devices: 9.48 us -> 6.28 us
    pallas_call x1, Pallas kernels: 129 us -> 3.5 us  [pick(): pl.pallas_call(pick_kernel, out_shape=jax.ShapeDtypeStruct((owners, CAP *...]
    unnamed x32 -> x14, local copies, waits for them, and re-layouts: 11.3 us -> 2.01 us
    pallas_call x1, Pallas kernels: 26.4 us -> 30.6 us  [project(): pl.pallas_call(functools.partial(project_kernel, steps), out_shape=(jax.S...]
    pallas_call x1, Pallas kernels: 15.1 us -> 17.7 us  [ssd(): pl.pallas_call(ssd_kernel, out_shape=(jax.ShapeDtypeStruct((tokens, width...]
    pallas_call x1 -> x2, Pallas kernels: 7.12 us -> 8.15 us  [the longest x1 5.29 us: tail(): pl.pallas_call(tail_kernel, out_shape=(pltpu.VMEM((tokens, width), BF16),...]
  transfers between devices with their start and end apart: 5 -> 5, of which waited for: 4 -> 2; matrix products, arithmetic and copies ran while one was open for 0% -> 3% of each run, Pallas kernels for 18% -> 52%
where the time goes in v3:
time: 99.8 us; the launch traced here: 99.2 us
  Pallas kernels  63.3 us (63%)
  blocking collectives  15.6 us (16%)
  starting transfers between devices  10.4 us (10%)
  waiting for transfers between devices  6.28 us (6%)
  local copies, waits for them, and re-layouts  2.75 us (3%)
    pallas_call x1, Pallas kernels, project(): pl.pallas_call(functools.partial(project_kernel, steps), out_shape=(jax.S...  30.6 us
    pallas_call x1, Pallas kernels, ssd(): pl.pallas_call(ssd_kernel, out_shape=(jax.ShapeDtypeStruct((tokens, width...  17.7 us
    all_to_all x1, blocking collectives, local(): lax.all_to_all(wanted, 'dp', split_axis=0, concat_axis=0, tiled=True)  15.6 us
    ppermute x3, starting transfers between devices, local(): lax.ppermute(square, 'mp', [(i, (i + 2 * s) % groups) for i in range(grou...  5.65 us
    pallas_call x1, Pallas kernels, tail(): pl.pallas_call(tail_kernel, out_shape=(pltpu.VMEM((tokens, width), BF16),...  5.29 us
    all_to_all x1, waiting for transfers between devices, local(): back = lax.all_to_all(sent, 'dp', split_axis=0, concat_axis=0, tiled=True)  5.11 us
    all_to_all x1, starting transfers between devices, local(): back = lax.all_to_all(sent, 'dp', split_axis=0, concat_axis=0, tiled=True)  4.68 us
    pallas_call x1, Pallas kernels, pick(): pl.pallas_call(pick_kernel, out_shape=jax.ShapeDtypeStruct((owners, CAP *...  3.5 us
  transfers between devices with their start and end apart: 5, of which 2 were waited for; matrix products, arithmetic and copies ran while one was open for 3% of the time, Pallas kernels for 52%

profile of v3, /device:TPU:0, one launch (start us, length us, event | category | flops | bytes accessed | tf_op | source)
XLA Modules:
  0.0 99.2 jit_solution(7943279538870607352)
XLA Ops:
  0.6 1.8 %prep.1 = (s32[16,1,128]{2,1,0:T(1,128)}, s32[64]{0:T(128)}) custom-call(s32[4,16]{1,0:T(4,128)} %owner_ref.1, s32[4,16]{1,0:T(4,128)} %slot_ref.1), custom_call_target="tpu_custom_call" | custom-call | tf_op jit(solution)/shard_map/prep/pallas_call | solution.py:45
  2.4 15.6 %all_to_all.10.codes_ref = s32[16,1,128]{2,1,0:T(1,128)} all-to-all(s32[16,1,128]{2,1,0:T(1,128)} %get-tuple-element.19), channel_id=1, replica_groups=mesh['dp'=16,'mp'=8] {'dp'}, dimensions={0} | all-to-all | bytes 16384 | tf_op jit(solution)/shard_map/all_to_all | solution.py:684
  18.0 3.5 %pick.1 = f32[16,528,128]{2,1,0:T(8,128)} custom-call(s32[16,1,128]{2,1,0:T(1,128)} %all_to_all.10.codes_ref, f32[48,64,128]{2,1,0:T(8,128)} %bitcast.4, bf16[48,192]{1,0:T(8,128)(2,1)} %bitcast.5), custom_call_target="tpu_custom_call" | custom-call | bytes 8388608 | tf_op jit(solution)/shard_map/pick/pallas_call | solution.py:92
  21.5 0.0 copy-start.2
  21.5 0.0 copy-start.5
  21.6 0.0 copy-start.3
  21.6 4.7 %all-to-all-start.1 = ((f32[16,528,128]{2,1,0:T(8,128)}), f32[16,528,128]{2,1,0:T(8,128)}, u32[]{:S(2)}, u32[]{:S(2)}) async-start(f32[16,528,128]{2,1,0:T(8,128)} %pick.1), calls=%async_computation.1 | async-start | bytes 8650752 | tf_op jit(solution)/shard_map/all_to_all | solution.py:686
  26.3 0.0 copy-done.2
  26.3 1.4 %copy.18.wd_ref = bf16[4096,16]{1,0:T(8,128)(2,1)} copy(bf16[4096,16]{0,1:T(8,128)(2,1)S(1)} %copy-done.2) | data formatting | bytes 262144 | tf_op args[4]
  27.6 0.0 copy-done.5
  27.6 0.1 broadcast_in_dim.14
  27.7 0.7 broadcast_in_dim_reshape.3.skip_ref
  28.4 0.0 copy-done.3
  28.4 0.6 copy.19.hist_ref
  29.0 30.6 %project.1 = (bf16[1024,1024]{1,0:T(8,128)(2,1)}, bf16[1024,1024]{1,0:T(8,128)(2,1)}, bf16[1024,256]{1,0:T(8,128)(2,1)}, f32[1024,16]{1,0:T(8,128)}) custom-call(bf16[1024,4096]{1,0:T(8,128)(2,1)} %act_ref.1, bf16[4096,1024]{1,0:T(8,128)(2,1)} %wi_ref.1, bf16[4096,1024]{1,0:T(8,128)(2,1)} %wg_ref.1, bf16[4096,256]{1,0:T(8,128)(2,1)} %ws_ref.1, ...), custom_call_target="tpu_custom_call" | custom-call | flops 19461570560 | bytes 33554432 | tf_op jit(solution)/shard_map/project/pallas_call | solution.py:153
  59.5 0.0 copy-start.1
  59.5 17.7 %ssd.1 = (bf16[1024,1024]{1,0:T(8,128)(2,1)}, bf16[1024,1024]{1,0:T(8,128)(2,1)}, bf16[1024,128]{1,0:T(8,128)(2,1)}, f32[4,1024,128]{2,1,0:T(8,128)}, f32[4,40,128]{2,1,0:T(8,128)}, /*index=5*/f32[4,48,1024]{2,1,0:T(8,128)}) custom-call(bf16[1024,1024]{1,0:T(8,128)(2,1)} %get-tuple-element.20.inner_ref, bf16[1024,1024]{1,0:T(8,128)(2,1)} %get-tuple-element.21.gate_ref, ...), custom_call_target="tpu_custom_call" | custom-call | flops 1073741824 | bytes 14680064 | tf_op jit(solution)/shard_map/ssd/pallas_call | solution.py:325
  77.3 5.1 %all-to-all-done.1.back_ref = f32[16,528,128]{2,1,0:T(8,128)} async-done(((f32[16,528,128]{2,1,0:T(8,128)}), f32[16,528,128]{2,1,0:T(8,128)}, u32[]{:S(2)}, u32[]{:S(2)}) %all-to-all-start.1) | async-done | bytes 4325408 | tf_op jit(solution)/shard_map/all_to_all | solution.py:686
  82.4 0.0 copy-done.1
  82.4 5.3 %tail.1 = (bf16[1024,1024]{1,0:T(8,128)(2,1)S(1)}, f32[8,256]{1,0:T(8,128)S(1)}, bf16[1024,32]{1,0:T(8,128)(2,1)S(1)}, f32[64,64,128]{2,1,0:T(8,128)S(1)}) custom-call(s32[64]{0:T(128)S(1)} %copy-done.1, f32[16,528,128]{2,1,0:T(8,128)} %all-to-all-done.1.back_ref, bf16[1024,1024]{1,0:T(8,128)(2,1)} %get-tuple-element.24.az_hbm, ...), custom_call_target="tpu_custom_call" | custom-call | flops 268435456 | bytes 10485760 | tf_op jit(solution)/shard_map/tail/pallas_call | solution.py:534
  87.7 0.1 collective-permute-start
  87.8 1.2 %collective-permute-done = f32[8,256]{1,0:T(8,128)S(1)} collective-permute-done((f32[8,256]{1,0:T(8,128)S(1)}, f32[8,256]{1,0:T(8,128)S(1)}, u32[]{:S(2)}, u32[]{:S(2)}) %collective-permute-start) | collective-permute-done | bytes 8224 | tf_op jit(solution)/shard_map/ppermute | solution.py:704
  88.9 1.5 %collective-permute-start.1 = (f32[8,256]{1,0:T(8,128)S(1)}, f32[8,256]{1,0:T(8,128)S(1)}, u32[]{:S(2)}, u32[]{:S(2)}) collective-permute-start(f32[8,256]{1,0:T(8,128)S(1)} %add.3.s0_ref), channel_id=1, source_target_pairs={{0,2},{1,3},{2,4},{3,5},{4,6},{5,7},{6,0},{7,1},{8,10},{9,11},{10,... | collective-permute-start | bytes 24584 | tf_op jit(solution)/shard_map/ppermute | solution.py:706
  90.4 2.7 %collective-permute-start.2 = (f32[8,256]{1,0:T(8,128)S(1)}, f32[8,256]{1,0:T(8,128)S(1)}, u32[]{:S(2)}, u32[]{:S(2)}) collective-permute-start(f32[8,256]{1,0:T(8,128)S(1)} %add.3.s0_ref), channel_id=1, source_target_pairs={{0,4},{1,5},{2,6},{3,7},{4,0},{5,1},{6,2},{7,3},{8,12},{9,13},{10,... | collective-permute-start | bytes 24584 | tf_op jit(solution)/shard_map/ppermute | solution.py:706
  93.2 1.4 %collective-permute-start.3 = (f32[8,256]{1,0:T(8,128)S(1)}, f32[8,256]{1,0:T(8,128)S(1)}, u32[]{:S(2)}, u32[]{:S(2)}) collective-permute-start(f32[8,256]{1,0:T(8,128)S(1)} %add.3.s0_ref), channel_id=1, source_target_pairs={{0,6},{1,7},{2,0},{3,1},{4,2},{5,3},{6,4},{7,5},{8,14},{9,15},{10,... | collective-permute-start | bytes 24584 | tf_op jit(solution)/shard_map/ppermute | solution.py:706
  94.6 0.0 copy-done.4
  94.6 0.0 copy-done
  94.6 2.9 %finals.1 = f32[4,16,64,128]{3,2,1,0:T(8,128)} custom-call(f32[64,64,128]{2,1,0:T(8,128)S(1)} %get-tuple-element.31.held_ref, bf16[1024,32]{1,0:T(8,128)(2,1)S(1)} %get-tuple-element.32.grow_ref, f32[4,40,128]{2,1,0:T(8,128)S(1)} %copy-done, f32[4,1024,128]{2,1,0:T(8,128)} %get-tuple-element.33.f1_hbm), custom_call_target="tpu_custom_call" | custom-call | flops 33554432 | bytes 6291456 | tf_op jit(solution)/shard_map/finals/pallas_call | solution.py:600
  97.5 0.0 collective-permute-done.1.s1_ref
  97.5 0.0 collective-permute-done.2.s2_ref
  97.5 0.0 collective-permute-done.3.s3_ref
  97.5 1.6 %normalise.1 = bf16[1024,1024]{1,0:T(8,128)(2,1)} custom-call(bf16[1024,1024]{1,0:T(8,128)(2,1)S(1)} %get-tuple-element.29.g_ref, f32[8,256]{1,0:T(8,128)S(1)} %add.3.s0_ref, f32[8,256]{1,0:T(8,128)S(1)} %collective-permute-done.1.s1_ref, f32[8,256]{1,0:T(8,128)S(1)} %collective-permute-done.2.s2_ref, f32[8,256]{1,0:T(8,128)S(1)} %collective-permute-done.3.s3_ref, ...), custom_call_target="tpu_custom_call" | custom-call | flops 2097152 | bytes 4194304 | tf_op jit(solution)/shard_map/normalise/pallas_call | solution.py:646
  (4 shorter events, 0.0 us)
Async XLA Ops:
  21.5 4.7 %copy-start.2 = (bf16[4096,16]{0,1:T(8,128)(2,1)S(1)}, bf16[4096,16]{0,1:T(8,128)(2,1)}, u32[]{:S(2)}) copy-start(bf16[4096,16]{0,1:T(8,128)(2,1)} %param.20) | copy-start | bytes 393220
  21.5 6.1 %copy-start.5 = (f32[16]{0:T(128)S(1)}, f32[16]{0:T(128)}, u32[]{:S(2)}) copy-start(f32[16]{0:T(128)} %param.25) | copy-start | bytes 196
  21.6 6.8 %copy-start.3 = (bf16[4,3,256]{2,0,1:T(4,128)(2,1)S(1)}, bf16[4,3,256]{2,0,1:T(4,128)(2,1)}, u32[]{:S(2)}) copy-start(bf16[4,3,256]{2,0,1:T(4,128)(2,1)} %param.29) | copy-start | bytes 18436
  21.6 60.8 %all-to-all-start.1 = ((f32[16,528,128]{2,1,0:T(8,128)}), f32[16,528,128]{2,1,0:T(8,128)}, u32[]{:S(2)}, u32[]{:S(2)}) async-start(f32[16,528,128]{2,1,0:T(8,128)} %pick.1), calls=%async_computation.1 | async-start | bytes 8650752 | tf_op jit(solution)/shard_map/all_to_all | solution.py:686
  59.5 22.8 %copy-start.1 = (s32[64]{0:T(128)S(1)}, s32[64]{0:T(128)}, u32[]{:S(2)}) copy-start(s32[64]{0:T(128)} %get-tuple-element.18.pos_ref) | copy-start | bytes 772
  82.4 12.2 %copy-start.4 = (bf16[1024]{0:T(1024)(128)(2,1)S(1)}, bf16[1024]{0:T(1024)(128)(2,1)}, u32[]{:S(2)}) copy-start(bf16[1024]{0:T(1024)(128)(2,1)} %param.26) | copy-start | bytes 6148
  82.4 12.2 %copy-start = (f32[4,40,128]{2,1,0:T(8,128)S(1)}, f32[4,40,128]{2,1,0:T(8,128)}, u32[]{:S(2)}) copy-start(f32[4,40,128]{2,1,0:T(8,128)} %get-tuple-element.27.small_hbm.small_ref) | copy-start | bytes 245764
  87.7 1.3 %collective-permute-start = (f32[8,256]{1,0:T(8,128)S(1)}, f32[8,256]{1,0:T(8,128)S(1)}, u32[]{:S(2)}, u32[]{:S(2)}) collective-permute-start(f32[8,256]{1,0:T(8,128)S(1)} %get-tuple-element.30), channel_id=1, source_target_pairs={{0,1},{1,0},{2,3},{3,2},{4,5},{5,4},{6,7},{7,6},{8,9},{9,8},{10,11... | collective-permute-start | bytes 24584 | tf_op jit(solution)/shard_map/ppermute | solution.py:704
  88.9 8.5 %collective-permute-start.1 = (f32[8,256]{1,0:T(8,128)S(1)}, f32[8,256]{1,0:T(8,128)S(1)}, u32[]{:S(2)}, u32[]{:S(2)}) collective-permute-start(f32[8,256]{1,0:T(8,128)S(1)} %add.3.s0_ref), channel_id=1, source_target_pairs={{0,2},{1,3},{2,4},{3,5},{4,6},{5,7},{6,0},{7,1},{8,10},{9,11},{10,... | collective-permute-start | bytes 24584 | tf_op jit(solution)/shard_map/ppermute | solution.py:706
  90.4 7.1 %collective-permute-start.2 = (f32[8,256]{1,0:T(8,128)S(1)}, f32[8,256]{1,0:T(8,128)S(1)}, u32[]{:S(2)}, u32[]{:S(2)}) collective-permute-start(f32[8,256]{1,0:T(8,128)S(1)} %add.3.s0_ref), channel_id=1, source_target_pairs={{0,4},{1,5},{2,6},{3,7},{4,0},{5,1},{6,2},{7,3},{8,12},{9,13},{10,... | collective-permute-start | bytes 24584 | tf_op jit(solution)/shard_map/ppermute | solution.py:706
  93.2 4.3 %collective-permute-start.3 = (f32[8,256]{1,0:T(8,128)S(1)}, f32[8,256]{1,0:T(8,128)S(1)}, u32[]{:S(2)}, u32[]{:S(2)}) collective-permute-start(f32[8,256]{1,0:T(8,128)S(1)} %add.3.s0_ref), channel_id=1, source_target_pairs={{0,6},{1,7},{2,0},{3,1},{4,2},{5,3},{6,4},{7,5},{8,14},{9,15},{10,... | collective-permute-start | bytes 24584 | tf_op jit(solution)/shard_map/ppermute | solution.py:706

commit v4 on v3

--- a/solution.py
+++ b/solution.py
@@ -23,9 +23,28 @@
     return pl.BlockSpec(shape, lambda *_: (0,) * len(shape), **kw)
 
 
-def prep_kernel(owner_ref, slot_ref, wanted_ref, pos_ref, count_ref):
+def in_hbm(*arrays):
+    return [pltpu.with_memory_space_constraint(v, pltpu.HBM) for v in arrays]
+
+
+def in_vmem(*arrays):
+    return [pltpu.with_memory_space_constraint(v, pltpu.VMEM) for v in arrays]
+
+
+def prep_kernel(
+    owner_ref, slot_ref, cache_hbm, window_ref, wanted_ref, pos_ref, cache_ref, wa_ref, wb_ref, count_ref, sem
+):
     owners = wanted_ref.shape[0]
     requests, heads = owner_ref.shape
+    copy = pltpu.make_async_copy(cache_hbm, cache_ref, sem)
+    copy.start()
+    half = window_ref.shape[1] // 3
+    w = window_ref[...].astype(F32)
+    first = w[:, : 2 * half]
+    second = jnp.concatenate([w[:, 2 * half :], jnp.zeros((w.shape[0], half), F32)], axis=1)
+    odd = lax.broadcasted_iota(jnp.int32, first.shape, 0) % 2 == 1
+    wa_ref[...] = jnp.where(odd, pltpu.roll(first, half, 1), first)
+    wb_ref[...] = jnp.where(odd, pltpu.roll(second, half, 1), second)
     for o in range(owners):
         count_ref[o] = 0
         for k in range(CAP):
@@ -37,28 +56,34 @@
             count_ref[o] = k + 1
             wanted_ref[o, 0, k] = slot_ref[r, h] * heads + h
             pos_ref[r * heads + h] = o * CAP + k
-
-
-def prep(hit_owner, hit_slot, owners):
+    copy.wait()
+
+
+def prep(hit_owner, hit_slot, cache, window, owners):
     entries = hit_owner.size
     smem = pl.BlockSpec(memory_space=pltpu.SMEM)
+    vmem = pl.BlockSpec(memory_space=pltpu.VMEM)
+    blocks, p, n = cache.shape
     return pl.pallas_call(
         prep_kernel,
         out_shape=(
             jax.ShapeDtypeStruct((owners, 1, 128), jnp.int32),
             jax.ShapeDtypeStruct((entries,), jnp.int32),
-        ),
-        in_specs=[smem, smem],
-        out_specs=(smem, smem),
-        scratch_shapes=[pltpu.SMEM((owners,), jnp.int32)],
+            pltpu.VMEM((blocks, p, n), F32),
+            pltpu.VMEM((blocks, n), F32),
+            pltpu.VMEM((blocks, n), F32),
+        ),
+        in_specs=[smem, smem, pl.BlockSpec(memory_space=pltpu.HBM), vmem],
+        out_specs=(smem, smem, vmem, vmem, vmem),
+        scratch_shapes=[pltpu.SMEM((owners,), jnp.int32), pltpu.SemaphoreType.DMA],
+        compiler_params=pltpu.CompilerParams(vmem_limit_bytes=8 * MIB),
         name="prep",
-    )(hit_owner, hit_slot)
-
-
-def pick_kernel(codes_ref, cache_ref, window_ref, out_ref, wa_ref, wb_ref, rows_ref, sem):
+    )(*in_hbm(hit_owner, hit_slot, cache, window))
+
+
+def pick_kernel(codes_ref, cache_ref, wa_ref, wb_ref, out_ref, rows_ref, sem):
     owners = out_ref.shape[0]
     p = cache_ref.shape[1]
-    half = window_ref.shape[1] // 3
     cached = CAP * p
 
     @pl.loop(0, owners)
@@ -68,13 +93,6 @@
                 cache_ref.at[codes_ref[d, 0, k]], out_ref.at[d, k * p : k * p + p], sem
             ).start()
 
-    w = window_ref[...].astype(F32)
-    first = w[:, : 2 * half]
-    second = jnp.concatenate([w[:, 2 * half :], jnp.zeros((w.shape[0], half), F32)], axis=1)
-    odd = lax.broadcasted_iota(jnp.int32, first.shape, 0) % 2 == 1
-    wa_ref[...] = jnp.where(odd, pltpu.roll(first, half, 1), first)
-    wb_ref[...] = jnp.where(odd, pltpu.roll(second, half, 1), second)
-
     @pl.loop(0, owners)
     def _(d):
         for k in range(CAP):
@@ -86,28 +104,21 @@
     pltpu.make_async_copy(out_ref, out_ref, sem).wait()
 
 
-def pick(codes, cache, window):
+def pick(codes, cache, wa, wb):
     owners = codes.shape[0]
     blocks, p, n = cache.shape
+    vmem = pl.BlockSpec(memory_space=pltpu.VMEM)
+    hbm = pl.BlockSpec(memory_space=pltpu.HBM)
     return pl.pallas_call(
         pick_kernel,
-        out_shape=jax.ShapeDtypeStruct((owners, CAP * p + 2 * CAP, n), F32),
-        in_specs=[
-            pl.BlockSpec(memory_space=pltpu.SMEM),
-            pl.BlockSpec(memory_space=pltpu.VMEM),
-            pl.BlockSpec(memory_space=pltpu.VMEM),
-        ],
-        out_specs=pl.BlockSpec(memory_space=pl.ANY),
-        scratch_shapes=[
-            pltpu.VMEM((blocks, n), F32),
-            pltpu.VMEM((blocks, n), F32),
-            pltpu.VMEM((owners, 2 * CAP, n), F32),
-            pltpu.SemaphoreType.DMA,
-        ],
-        compiler_params=pltpu.CompilerParams(vmem_limit_bytes=60 * MIB),
+        out_shape=pltpu.HBM((owners, CAP * p + 2 * CAP, n), F32),
+        in_specs=[pl.BlockSpec(memory_space=pltpu.SMEM), vmem, vmem, vmem],
+        out_specs=hbm,
+        scratch_shapes=[pltpu.VMEM((owners, 2 * CAP, n), F32), pltpu.SemaphoreType.DMA],
+        compiler_params=pltpu.CompilerParams(vmem_limit_bytes=8 * MIB),
         cost_estimate=pl.CostEstimate(flops=0, bytes_accessed=8 * MIB, transcendentals=0),
         name="pick",
-    )(codes, cache, window)
+    )(codes, *in_vmem(cache, wa, wb))
 
 
 TILE = 256
@@ -216,7 +227,7 @@
     conv = silu(run).astype(BF16)
     b = conv[:, :n]
     c = conv[:, n:]
-    c_ref[...] = c
+    c_ref[:, :n] = c
     small_ref[0, 2 * heads :] = b[:16].astype(F32)[:8]
 
     raw = step_ref[...] + bias_ref[...]
@@ -248,6 +259,11 @@
 
     scores = lax.dot_general(c, b, (((1,), (1,)), ((), ())), preferred_element_type=F32)
     scores = jnp.where(causal, scores, 0.0)
+    own = scores[:, :n]
+    seen = (lax.broadcasted_iota(jnp.int32, own.shape, 1) < lag) & (
+        lax.broadcasted_iota(jnp.int32, own.shape, 0) >= lag
+    )
+    c_ref[:, n:] = pltpu.roll(jnp.where(seen, own, 0.0), 8 * pl.program_id(0), 1).astype(BF16)
     top = scores[:half, :half]
     bottom = scores[half:]
 
@@ -325,12 +341,12 @@
     return pl.pallas_call(
         ssd_kernel,
         out_shape=(
-            jax.ShapeDtypeStruct((tokens, width), BF16),
-            jax.ShapeDtypeStruct((tokens, width), BF16),
-            jax.ShapeDtypeStruct((tokens, n), BF16),
-            jax.ShapeDtypeStruct((requests, width, n), F32),
-            jax.ShapeDtypeStruct((requests, 2 * heads + 8, n), F32),
-            jax.ShapeDtypeStruct((requests, 24 + 8 * lag, width), F32),
+            pltpu.VMEM((tokens, width), BF16),
+            pltpu.HBM((tokens, width), BF16),
+            pltpu.VMEM((tokens, 2 * n), BF16),
+            pltpu.HBM((requests, width, n), F32),
+            pltpu.VMEM((requests, 2 * heads + 8, n), F32),
+            pltpu.VMEM((requests, 24 + 8 * lag, width), F32),
         ),
         grid=(requests,),
         in_specs=[
@@ -348,18 +364,18 @@
         out_specs=(
             rows(width),
             rows(width),
-            rows(n),
+            rows(2 * n),
             per(width, n),
             per(2 * heads + 8, n),
             per(24 + 8 * lag, width),
         ),
         scratch_shapes=[pltpu.VMEM((seq + 8, width), F32), pltpu.VMEM((seq + 8, n2), F32)],
-        compiler_params=pltpu.CompilerParams(vmem_limit_bytes=60 * MIB),
+        compiler_params=pltpu.CompilerParams(vmem_limit_bytes=40 * MIB),
         cost_estimate=pl.CostEstimate(
             flops=2 * tokens * width * seq * 2, bytes_accessed=14 * MIB, transcendentals=tokens * seq * heads
         ),
         name="ssd",
-    )(inner, gate, state, step, history, ik, sk, bias, decay, skip)
+    )(*in_hbm(inner, gate, state, step), history, ik, sk, bias, decay, skip)
 
 
 def first_sources(grow_ref, small_ref, r):
@@ -373,20 +389,18 @@
 def tail_kernel(
     pos_ref,
     back_ref,
-    az_hbm,
     ez_hbm,
-    c_hbm,
-    small_hbm,
-    first_hbm,
+    f1_hbm,
+    az_ref,
+    c_ref,
+    small_ref,
+    first_ref,
     g_ref,
     sq_ref,
     grow_ref,
     held_ref,
-    az_ref,
+    f1_ref,
     ez_ref,
-    c_ref,
-    small_ref,
-    first_ref,
     rows_ref,
     s_ref,
     raw_ref,
@@ -395,9 +409,7 @@
     x_ref,
     extra_ref,
     sem,
-    az_sem,
     ez_sem,
-    c_sem,
     once_sem,
 ):
     requests = first_ref.shape[0]
@@ -411,12 +423,8 @@
     def rows_of(r):
         return slice(r * seq, r * seq + seq)
 
-    def copies(r):
-        return (
-            pltpu.make_async_copy(az_hbm.at[rows_of(r)], az_ref.at[rows_of(r)], az_sem.at[r]),
-            pltpu.make_async_copy(ez_hbm.at[rows_of(r)], ez_ref.at[rows_of(r)], ez_sem.at[r]),
-            pltpu.make_async_copy(c_hbm.at[rows_of(r)], c_ref.at[rows_of(r)], c_sem.at[r]),
-        )
+    def ez_copy(r):
+        return pltpu.make_async_copy(ez_hbm.at[rows_of(r)], ez_ref.at[rows_of(r)], ez_sem.at[r])
 
     def fetch(r):
         for h in range(heads):
@@ -427,21 +435,16 @@
                 held_ref.at[e],
                 sem.at[r],
             ).start()
-        for copy in copies(r):
-            copy.start()
-
-    once = (
-        pltpu.make_async_copy(back_ref.at[:, CAP * p :], rows_ref, once_sem.at[0]),
-        pltpu.make_async_copy(first_hbm, first_ref, once_sem.at[1]),
-        pltpu.make_async_copy(small_hbm, small_ref, once_sem.at[2]),
-    )
-    for copy in once:
-        copy.start()
+        ez_copy(r).start()
+
+    row_copy = pltpu.make_async_copy(back_ref.at[:, CAP * p :], rows_ref, once_sem.at[0])
+    f1_copy = pltpu.make_async_copy(f1_hbm, f1_ref, once_sem.at[1])
+    row_copy.start()
     fetch(0)
     fetch(1)
     win_ref[...] = jnp.zeros_like(win_ref)
     x_ref[...] = jnp.zeros_like(x_ref)
-    once[0].wait()
+    row_copy.wait()
 
     low = lax.broadcasted_iota(jnp.int32, (1, 128), 1) < p
     flat = rows_ref.reshape(rows_ref.shape[0] * rows_ref.shape[1], 128)
@@ -460,7 +463,6 @@
         for q in range(pairs):
             win_ref[i, 1:2, q * 128 : q * 128 + 128] = mix[i * pairs + q : i * pairs + q + 1]
 
-    once[1].wait()
     run = first_ref[:, 0:8]
     for k in range(lag):
         at = 16 + 8 * lag + k
@@ -472,34 +474,37 @@
     for j in range(1, lag):
         extra = extra + first_ref[:, 16 + 8 * j : 24 + 8 * j] * x_ref[:, 8 - j : 16 - j]
     extra_ref[...] = extra
-    grow_ref[...] = (x * first_ref[:, 8:16]).reshape(requests * 8, width).T.astype(BF16)
+    grow = (x * first_ref[:, 8:16]).reshape(requests * 8, width).T
+    grow_ref[...] = grow.astype(BF16)
+    n = c_ref.shape[1] // 2
+    grow = jnp.concatenate([grow, jnp.zeros((width, n - requests * 8), F32)], axis=1).astype(BF16)
+    s_ref[0, :, n:] = grow
+    s_ref[1, :, n:] = grow
 
     for r in range(2, requests):
         fetch(r)
-
-    once[2].wait()
+    f1_copy.start()
+
     row16 = lax.broadcasted_iota(jnp.int32, (16, 256), 0)
     nt = (((1,), (1,)), ((), ()))
     squares = []
     for r in range(requests):
         rows = rows_of(r)
-        add = first_sources(grow_ref, small_ref, r)
         part = held_ref.at[r * heads : r * heads + heads]
         pltpu.make_async_copy(part, part, sem.at[r]).wait()
         for h in range(heads):
             at = slice(h * p, h * p + p)
             block = held_ref[r * heads + h]
             raw_ref[r % 2, at] = block.astype(BF16)
-            s_ref[r % 2, at] = (small_ref[r, heads + h : heads + h + 1] * block + add[at]).astype(BF16)
-        for copy in copies(r):
-            copy.wait()
+            s_ref[r % 2, at, :n] = (small_ref[r, heads + h : heads + h + 1] * block).astype(BF16)
+        ez_copy(r).wait()
         c = c_ref[rows]
         total = jnp.zeros((seq - 16, 128), F32)
         total16 = jnp.zeros((16, 128), F32)
         for q in range(width // 256):
             cols = slice(q * 256, q * 256 + 256)
             seen = lax.dot_general(c, s_ref[r % 2, cols], nt, preferred_element_type=F32)
-            seen16 = lax.dot_general(c[:16], raw_ref[r % 2, cols], nt, preferred_element_type=F32)
+            seen16 = lax.dot_general(c[:16, :n], raw_ref[r % 2, cols], nt, preferred_element_type=F32)
             seen16 = jnp.where(row16 < lag, seen16, seen[:16])
             az = az_ref[rows, cols].astype(F32)
             ez = ez_ref[rows, cols].astype(F32)
@@ -516,15 +521,13 @@
         squares.append(jnp.sum(total.T, axis=0, keepdims=True))
     squares.append(jnp.zeros((8 - requests, seq), F32))
     sq_ref[...] = jnp.concatenate(squares, axis=0)
-
-
-def in_hbm(*arrays):
-    return [pltpu.with_memory_space_constraint(v, pltpu.HBM) for v in arrays]
-
-
-def tail(pos, back, az, ez, c, small, first):
+    f1_copy.wait()
+
+
+def tail(pos, back, ez, f1, az, c, small, first):
     requests, packed, n = small.shape
     heads = (packed - 8) // 2
+    assert requests * 8 <= n
     tokens, width = az.shape
     p = width // heads
     seq = tokens // requests
@@ -538,17 +541,14 @@
             pltpu.VMEM((8, seq), F32),
             pltpu.VMEM((width, requests * 8), BF16),
             pltpu.VMEM((requests * heads, p, n), F32),
-        ),
-        in_specs=[pl.BlockSpec(memory_space=pltpu.SMEM)] + [hbm] * 6,
-        out_specs=(vmem,) * 4,
+            pltpu.VMEM(f1.shape, F32),
+        ),
+        in_specs=[pl.BlockSpec(memory_space=pltpu.SMEM)] + [hbm] * 3 + [vmem] * 4,
+        out_specs=(vmem,) * 5,
         scratch_shapes=[
             pltpu.VMEM((tokens, width), BF16),
-            pltpu.VMEM((tokens, width), BF16),
-            pltpu.VMEM((tokens, n), BF16),
-            pltpu.VMEM(small.shape, F32),
-            pltpu.VMEM(first.shape, F32),
             pltpu.VMEM((owners, 2 * CAP, n), F32),
-            pltpu.VMEM((2, width, n), BF16),
+            pltpu.VMEM((2, width, 2 * n), BF16),
             pltpu.VMEM((2, width, n), BF16),
             pltpu.VMEM((requests, 16, width), F32),
             pltpu.VMEM((requests * heads // 2, 128), F32),
@@ -556,33 +556,24 @@
             pltpu.VMEM((requests, 8, width), F32),
             pltpu.SemaphoreType.DMA((requests,)),
             pltpu.SemaphoreType.DMA((requests,)),
-            pltpu.SemaphoreType.DMA((requests,)),
-            pltpu.SemaphoreType.DMA((requests,)),
-            pltpu.SemaphoreType.DMA((3,)),
+            pltpu.SemaphoreType.DMA((2,)),
         ],
         compiler_params=pltpu.CompilerParams(vmem_limit_bytes=24 * MIB),
         cost_estimate=pl.CostEstimate(
             flops=2 * tokens * width * n, bytes_accessed=10 * MIB, transcendentals=0
         ),
         name="tail",
-    )(pos, *in_hbm(back, az, ez, c, small, first))
-
-
-def final_kernel(held_ref, grow_ref, small_ref, f1_hbm, out_ref, f1_ref, made_ref, f1_sem, sem):
+    )(pos, *in_hbm(back, ez, f1), *in_vmem(az, c, small, first))
+
+
+def final_kernel(held_ref, grow_ref, small_ref, f1_ref, out_ref, made_ref, sem):
     requests, heads, p = out_ref.shape[:3]
-
-    def part(r):
-        return pltpu.make_async_copy(f1_hbm.at[r], f1_ref.at[r], f1_sem.at[r])
-
-    for r in range(requests):
-        part(r).start()
 
     def copy(r):
         return pltpu.make_async_copy(made_ref.at[r], out_ref.at[r], sem.at[r])
 
     for r in range(requests):
         add = first_sources(grow_ref, small_ref, r)
-        part(r).wait()
         for h in range(heads):
             at = slice(h * p, h * p + p)
             block = small_ref[r, heads + h : heads + h + 1] * held_ref[r * heads + h] + add[at]
@@ -600,12 +591,10 @@
     return pl.pallas_call(
         final_kernel,
         out_shape=jax.ShapeDtypeStruct((requests, heads, p, n), F32),
-        in_specs=[vmem] * 3 + [pl.BlockSpec(memory_space=pltpu.HBM)],
+        in_specs=[vmem] * 4,
         out_specs=pl.BlockSpec(memory_space=pltpu.HBM),
         scratch_shapes=[
-            pltpu.VMEM((requests, width, n), F32),
             pltpu.VMEM((requests, heads, p, n), F32),
-            pltpu.SemaphoreType.DMA((requests,)),
             pltpu.SemaphoreType.DMA((requests,)),
         ],
         compiler_params=pltpu.CompilerParams(vmem_limit_bytes=16 * MIB),
@@ -613,7 +602,7 @@
             flops=2 * requests * width * n * 32, bytes_accessed=6 * MIB, transcendentals=0
         ),
         name="finals",
-    )(held, grow, small, *in_hbm(f1))
+    )(*in_vmem(held, grow, small, f1))
 
 
 def norm_kernel(channels, g_ref, s0_ref, s1_ref, s2_ref, s3_ref, gain_ref, out_ref, made_ref, sem):
@@ -680,9 +669,10 @@
     width = inner_weight.shape[1]
     blocks = slots * heads
 
-    wanted, pos = prep(hit_owner, hit_slot, owners)
+    cache = scan_cache.reshape(blocks, p, n)
+    wanted, pos, cache, wa, wb = prep(hit_owner, hit_slot, cache, window_cache.reshape(blocks, -1), owners)
     codes = lax.all_to_all(wanted, "dp", split_axis=0, concat_axis=0, tiled=True)
-    sent = pick(codes, scan_cache.reshape(blocks, p, n), window_cache.reshape(blocks, -1))
+    sent = pick(codes, cache, wa, wb)
     back = lax.all_to_all(sent, "dp", split_axis=0, concat_axis=0, tiled=True)
 
     inner, gate, state, step = project(activations, inner_weight, gate_weight, state_proj, step_weight)
@@ -698,7 +688,7 @@
         decay_rate[None],
         jnp.repeat(skip_scale, p)[None],
     )
-    g, square, grow, held = tail(pos, back, az, ez, c, small, first)
+    g, square, grow, held, f1 = tail(pos, back, ez, f1, az, c, small, first)
     final = finals(held, grow, small, f1)
     pair = [(i, i ^ 1) for i in range(groups)]
     square = square + lax.ppermute(square, "mp", pair)

time: 99.8 us -> 98.9 us (level)
  waiting for transfers between devices: 6.28 us -> 8.41 us
  Pallas kernels: 63.3 us -> 61.8 us
  local copies, waits for them, and re-layouts: 2.75 us -> 1.58 us
    all_to_all x1, waiting for transfers between devices: 5.11 us -> 6.75 us  [local(): back = lax.all_to_all(sent, 'dp', split_axis=0, concat_axis=0, tiled=True)]
    pallas_call x2, Pallas kernels: 21.2 us -> 20 us  [the longest x1 17.3 us: ssd(): pl.pallas_call(ssd_kernel, out_shape=(pltpu.VMEM((tokens, width), BF16),...]
    pallas_call x1, Pallas kernels: 2.86 us -> 1.69 us  [finals(): pl.pallas_call(final_kernel, out_shape=jax.ShapeDtypeStruct((requests, he...]
    pallas_call x1, Pallas kernels: 1.81 us -> 2.9 us  [prep(): pl.pallas_call(prep_kernel, out_shape=(jax.ShapeDtypeStruct((owners, 1, 1...]
    unnamed x14 -> x18, local copies, waits for them, and re-layouts: 2.01 us -> 1.43 us
  transfers between devices with their start and end apart: 5 -> 5, of which waited for: 2 -> 3; matrix products, arithmetic and copies ran while one was open for 3% -> 2% of each run, Pallas kernels for 52% -> 50%
where the time goes in v4:
time: 98.9 us; the launch traced here: 98.5 us
  Pallas kernels  61.8 us (62%)
  blocking collectives  15.5 us (16%)
  starting transfers between devices  10.4 us (11%)
  waiting for transfers between devices  8.41 us (9%)
  local copies, waits for them, and re-layouts  1.58 us (2%)
    pallas_call x1, Pallas kernels, project(): pl.pallas_call(functools.partial(project_kernel, steps), out_shape=(jax.S...  30.5 us
    pallas_call x1, Pallas kernels, ssd(): pl.pallas_call(ssd_kernel, out_shape=(pltpu.VMEM((tokens, width), BF16),...  17.3 us
    all_to_all x1, blocking collectives, local(): lax.all_to_all(wanted, 'dp', split_axis=0, concat_axis=0, tiled=True)  15.5 us
    all_to_all x1, waiting for transfers between devices, local(): back = lax.all_to_all(sent, 'dp', split_axis=0, concat_axis=0, tiled=True)  6.75 us
    ppermute x3, starting transfers between devices, local(): lax.ppermute(square, 'mp', [(i, (i + 2 * s) % groups) for i in range(grou...  5.65 us
    pallas_call x1, Pallas kernels, tail(): pl.pallas_call(tail_kernel, out_shape=(pltpu.VMEM((tokens, width), BF16),...  5.06 us
    all_to_all x1, starting transfers between devices, local(): back = lax.all_to_all(sent, 'dp', split_axis=0, concat_axis=0, tiled=True)  4.68 us
    pallas_call x1, Pallas kernels, prep(): pl.pallas_call(prep_kernel, out_shape=(jax.ShapeDtypeStruct((owners, 1, 1...  2.9 us
  transfers between devices with their start and end apart: 5, of which 3 were waited for; matrix products, arithmetic and copies ran while one was open for 2% of the time, Pallas kernels for 50%

profile of v4, /device:TPU:0, one launch (start us, length us, event | category | flops | bytes accessed | tf_op | source)
XLA Modules:
  0.0 98.5 jit_solution(13891576604062968770)
XLA Ops:
  0.6 2.9 %prep.1 = (s32[16,1,128]{2,1,0:T(1,128)S(1)}, s32[64]{0:T(128)S(1)}, f32[48,64,128]{2,1,0:T(8,128)S(1)}, f32[48,128]{1,0:T(8,128)S(1)}, f32[48,128]{1,0:T(8,128)S(1)}) custom-call(s32[4,16]{1,0:T(4,128)} %owner_ref.1, s32[4,16]{1,0:T(4,128)} %slot_ref.1, f32[48,64,128]{2,1,0:T(8,128)} %bitcast.6, bf16[48,192]{1,0:T(8,128)(2,1)} %bitcast.7), custom_call_target="tpu_custom_call" | custom-call | tf_op jit(solution)/shard_map/prep/pallas_call | solution.py:67
  3.5 15.5 %all_to_all.10.codes_ref = s32[16,1,128]{2,1,0:T(1,128)S(1)} all-to-all(s32[16,1,128]{2,1,0:T(1,128)S(1)} %get-tuple-element.23), channel_id=1, replica_groups=mesh['dp'=16,'mp'=8] {'dp'}, dimensions={0} | all-to-all | bytes 16384 | tf_op jit(solution)/shard_map/all_to_all | solution.py:674
  19.0 2.7 %pick.1 = f32[16,528,128]{2,1,0:T(8,128)} custom-call(s32[16,1,128]{2,1,0:T(1,128)S(1)} %all_to_all.10.codes_ref, f32[48,64,128]{2,1,0:T(8,128)S(1)} %get-tuple-element.24.cache_ref, f32[48,128]{1,0:T(8,128)S(1)} %get-tuple-element.25.wa_ref, f32[48,128]{1,0:T(8,128)S(1)} %get-tuple-element.26.wb_ref), custom_call_target="tpu_custom_call" | custom-call | bytes 8388608 | tf_op jit(solution)/shard_map/pick/pallas_call | solution.py:112
  21.8 0.0 copy-start.4
  21.8 0.0 copy-start.7
  21.8 0.0 copy-start.5
  21.8 4.7 %all-to-all-start.1 = ((f32[16,528,128]{2,1,0:T(8,128)}), f32[16,528,128]{2,1,0:T(8,128)}, u32[]{:S(2)}, u32[]{:S(2)}) async-start(f32[16,528,128]{2,1,0:T(8,128)} %pick.1), calls=%async_computation.1 | async-start | bytes 8650752 | tf_op jit(solution)/shard_map/all_to_all | solution.py:676
  26.5 0.0 copy-done.4
  26.5 1.4 %copy.18.wd_ref = bf16[4096,16]{1,0:T(8,128)(2,1)} copy(bf16[4096,16]{0,1:T(8,128)(2,1)S(1)} %copy-done.4) | data formatting | bytes 262144 | tf_op args[4]
  27.9 0.1 broadcast_in_dim.14
  27.9 0.1 broadcast_in_dim_reshape.3.skip_ref
  28.0 0.0 copy-done.5
  28.0 0.0 copy-start
  28.0 0.0 copy-start.1
  28.1 0.0 copy-start.2
  28.1 0.0 copy-start.3
  28.1 30.5 %project.1 = (bf16[1024,1024]{1,0:T(8,128)(2,1)}, bf16[1024,1024]{1,0:T(8,128)(2,1)}, bf16[1024,256]{1,0:T(8,128)(2,1)}, f32[1024,16]{1,0:T(8,128)}) custom-call(bf16[1024,4096]{1,0:T(8,128)(2,1)} %act_ref.1, bf16[4096,1024]{1,0:T(8,128)(2,1)} %wi_ref.1, bf16[4096,1024]{1,0:T(8,128)(2,1)} %wg_ref.1, bf16[4096,256]{1,0:T(8,128)(2,1)} %ws_ref.1, ...), custom_call_target="tpu_custom_call" | custom-call | flops 19461570560 | bytes 33554432 | tf_op jit(solution)/shard_map/project/pallas_call | solution.py:164
  58.6 0.0 copy-done
  58.6 0.0 copy-done.1
  58.7 17.3 %ssd.1 = (bf16[1024,1024]{1,0:T(8,128)(2,1)S(1)}, bf16[1024,1024]{1,0:T(8,128)(2,1)}, bf16[1024,256]{1,0:T(8,128)(2,1)S(1)}, f32[4,1024,128]{2,1,0:T(8,128)}, f3...) custom-call(bf16[1024,1024]{1,0:T(8,128)(2,1)} %get-tuple-element.27.inner_ref, ...), custom_call_target="tpu_custom_call" | custom-call | flops 1073741824 | bytes 14680064 | tf_op jit(solution)/shard_map/ssd/pallas_call | solution.py:341
  76.0 6.8 %all-to-all-done.1.back_ref = f32[16,528,128]{2,1,0:T(8,128)} async-done(((f32[16,528,128]{2,1,0:T(8,128)}), f32[16,528,128]{2,1,0:T(8,128)}, u32[]{:S(2)}, u32[]{:S(2)}) %all-to-all-start.1) | async-done | bytes 4325408 | tf_op jit(solution)/shard_map/all_to_all | solution.py:676
  82.7 5.1 %tail.1 = (bf16[1024,1024]{1,0:T(8,128)(2,1)S(1)}, f32[8,256]{1,0:T(8,128)S(1)}, bf16[1024,32]{1,0:T(8,128)(2,1)S(1)}, f32[64,64,128]{2,1,0:T(8,128)S(1)}, f32[4,1024,128]{2,1,0:T(8,128)S(1)}) custom-call(s32[64]{0:T(128)S(1)} %get-tuple-element.22.pos_ref, f32[16,528,128]{2,1,0:T(8,128)} %all-to-all-done.1.back_ref, ...), custom_call_target="tpu_custom_call" | custom-call | flops 268435456 | bytes 10485760 | tf_op jit(solution)/shard_map/tail/pallas_call | solution.py:537
  87.8 0.1 collective-permute-start
  87.9 1.2 %collective-permute-done = f32[8,256]{1,0:T(8,128)S(1)} collective-permute-done((f32[8,256]{1,0:T(8,128)S(1)}, f32[8,256]{1,0:T(8,128)S(1)}, u32[]{:S(2)}, u32[]{:S(2)}) %collective-permute-start) | collective-permute-done | bytes 8224 | tf_op jit(solution)/shard_map/ppermute | solution.py:694
  89.1 1.5 %collective-permute-start.1 = (f32[8,256]{1,0:T(8,128)S(1)}, f32[8,256]{1,0:T(8,128)S(1)}, u32[]{:S(2)}, u32[]{:S(2)}) collective-permute-start(f32[8,256]{1,0:T(8,128)S(1)} %add.3.s0_ref), channel_id=1, source_target_pairs={{0,2},{1,3},{2,4},{3,5},{4,6},{5,7},{6,0},{7,1},{8,10},{9,11},{10,... | collective-permute-start | bytes 24584 | tf_op jit(solution)/shard_map/ppermute | solution.py:696
  90.5 2.7 %collective-permute-start.2 = (f32[8,256]{1,0:T(8,128)S(1)}, f32[8,256]{1,0:T(8,128)S(1)}, u32[]{:S(2)}, u32[]{:S(2)}) collective-permute-start(f32[8,256]{1,0:T(8,128)S(1)} %add.3.s0_ref), channel_id=1, source_target_pairs={{0,4},{1,5},{2,6},{3,7},{4,0},{5,1},{6,2},{7,3},{8,12},{9,13},{10,... | collective-permute-start | bytes 24584 | tf_op jit(solution)/shard_map/ppermute | solution.py:696
  93.3 1.4 %collective-permute-start.3 = (f32[8,256]{1,0:T(8,128)S(1)}, f32[8,256]{1,0:T(8,128)S(1)}, u32[]{:S(2)}, u32[]{:S(2)}) collective-permute-start(f32[8,256]{1,0:T(8,128)S(1)} %add.3.s0_ref), channel_id=1, source_target_pairs={{0,6},{1,7},{2,0},{3,1},{4,2},{5,3},{6,4},{7,5},{8,14},{9,15},{10,... | collective-permute-start | bytes 24584 | tf_op jit(solution)/shard_map/ppermute | solution.py:696
  94.7 1.7 %finals.1 = f32[4,16,64,128]{3,2,1,0:T(8,128)} custom-call(f32[64,64,128]{2,1,0:T(8,128)S(1)} %get-tuple-element.39.held_ref, bf16[1024,32]{1,0:T(8,128)(2,1)S(1)} %get-tuple-element.40.grow_ref, f32[4,40,128]{2,1,0:T(8,128)S(1)} %get-tuple-element.35.small_ref, f32[4,1024,128]{2,1,0:T(8,128)S(1)} %get-tuple-element.41.f1_ref), custom_call_target="tpu_custom_call" | custom-call | flops 33554432 | bytes 6291456 | tf_op jit(solution)/shard_map/finals/pallas_call | solution.py:591
  96.4 0.0 collective-permute-done.1.s1_ref
  96.4 0.0 collective-permute-done.2.s2_ref
  96.4 0.5 collective-permute-done.3.s3_ref
  96.9 1.6 %normalise.1 = bf16[1024,1024]{1,0:T(8,128)(2,1)} custom-call(bf16[1024,1024]{1,0:T(8,128)(2,1)S(1)} %get-tuple-element.37.g_ref, f32[8,256]{1,0:T(8,128)S(1)} %add.3.s0_ref, f32[8,256]{1,0:T(8,128)S(1)} %collective-permute-done.1.s1_ref, f32[8,256]{1,0:T(8,128)S(1)} %collective-permute-done.2.s2_ref, f32[8,256]{1,0:T(8,128)S(1)} %collective-permute-done.3.s3_ref, ...), custom_call_target="tpu_custom_call" | custom-call | flops 2097152 | bytes 4194304 | tf_op jit(solution)/shard_map/normalise/pallas_call | solution.py:635
  (8 shorter events, 0.0 us)
Async XLA Ops:
  21.8 4.7 %copy-start.4 = (bf16[4096,16]{0,1:T(8,128)(2,1)S(1)}, bf16[4096,16]{0,1:T(8,128)(2,1)}, u32[]{:S(2)}) copy-start(bf16[4096,16]{0,1:T(8,128)(2,1)} %param.20) | copy-start | bytes 393220
  21.8 6.1 %copy-start.7 = (f32[16]{0:T(128)S(1)}, f32[16]{0:T(128)}, u32[]{:S(2)}) copy-start(f32[16]{0:T(128)} %param.25) | copy-start | bytes 196
  21.8 6.2 %copy-start.5 = (bf16[4,3,256]{2,0,1:T(4,128)(2,1)S(1)}, bf16[4,3,256]{2,0,1:T(4,128)(2,1)}, u32[]{:S(2)}) copy-start(bf16[4,3,256]{2,0,1:T(4,128)(2,1)} %param.29) | copy-start | bytes 18436
  21.8 60.9 %all-to-all-start.1 = ((f32[16,528,128]{2,1,0:T(8,128)}), f32[16,528,128]{2,1,0:T(8,128)}, u32[]{:S(2)}, u32[]{:S(2)}) async-start(f32[16,528,128]{2,1,0:T(8,128)} %pick.1), calls=%async_computation.1 | async-start | bytes 8650752 | tf_op jit(solution)/shard_map/all_to_all | solution.py:676
  28.0 30.6 %copy-start = (bf16[4,1024]{1,0:T(4,128)(2,1)S(1)}, bf16[4,1024]{1,0:T(4,128)(2,1)}, u32[]{:S(2)}) copy-start(bf16[4,1024]{1,0:T(4,128)(2,1)} %ik_ref.1) | copy-start | bytes 24580
  28.0 30.6 %copy-start.1 = (bf16[4,256]{1,0:T(4,128)(2,1)S(1)}, bf16[4,256]{1,0:T(4,128)(2,1)}, u32[]{:S(2)}) copy-start(bf16[4,256]{1,0:T(4,128)(2,1)} %sk_ref.1) | copy-start | bytes 6148
  28.1 30.6 %copy-start.2 = (f32[16]{0:T(128)S(1)}, f32[16]{0:T(128)}, u32[]{:S(2)}) copy-start(f32[16]{0:T(128)} %param.23) | copy-start | bytes 196
  28.1 30.6 %copy-start.3 = (f32[16]{0:T(128)S(1)}, f32[16]{0:T(128)}, u32[]{:S(2)}) copy-start(f32[16]{0:T(128)} %param.24) | copy-start | bytes 196
  82.7 12.0 %copy-start.6 = (bf16[1024]{0:T(1024)(128)(2,1)S(1)}, bf16[1024]{0:T(1024)(128)(2,1)}, u32[]{:S(2)}) copy-start(bf16[1024]{0:T(1024)(128)(2,1)} %param.26) | copy-start | bytes 6148
  87.8 1.3 %collective-permute-start = (f32[8,256]{1,0:T(8,128)S(1)}, f32[8,256]{1,0:T(8,128)S(1)}, u32[]{:S(2)}, u32[]{:S(2)}) collective-permute-start(f32[8,256]{1,0:T(8,128)S(1)} %get-tuple-element.38), channel_id=1, source_target_pairs={{0,1},{1,0},{2,3},{3,2},{4,5},{5,4},{6,7},{7,6},{8,9},{9,8},{10,11... | collective-permute-start | bytes 24584 | tf_op jit(solution)/shard_map/ppermute | solution.py:694
  89.1 7.4 %collective-permute-start.1 = (f32[8,256]{1,0:T(8,128)S(1)}, f32[8,256]{1,0:T(8,128)S(1)}, u32[]{:S(2)}, u32[]{:S(2)}) collective-permute-start(f32[8,256]{1,0:T(8,128)S(1)} %add.3.s0_ref), channel_id=1, source_target_pairs={{0,2},{1,3},{2,4},{3,5},{4,6},{5,7},{6,0},{7,1},{8,10},{9,11},{10,... | collective-permute-start | bytes 24584 | tf_op jit(solution)/shard_map/ppermute | solution.py:696
  90.5 5.9 %collective-permute-start.2 = (f32[8,256]{1,0:T(8,128)S(1)}, f32[8,256]{1,0:T(8,128)S(1)}, u32[]{:S(2)}, u32[]{:S(2)}) collective-permute-start(f32[8,256]{1,0:T(8,128)S(1)} %add.3.s0_ref), channel_id=1, source_target_pairs={{0,4},{1,5},{2,6},{3,7},{4,0},{5,1},{6,2},{7,3},{8,12},{9,13},{10,... | collective-permute-start | bytes 24584 | tf_op jit(solution)/shard_map/ppermute | solution.py:696
  93.3 3.7 %collective-permute-start.3 = (f32[8,256]{1,0:T(8,128)S(1)}, f32[8,256]{1,0:T(8,128)S(1)}, u32[]{:S(2)}, u32[]{:S(2)}) collective-permute-start(f32[8,256]{1,0:T(8,128)S(1)} %add.3.s0_ref), channel_id=1, source_target_pairs={{0,6},{1,7},{2,0},{3,1},{4,2},{5,3},{6,4},{7,5},{8,14},{9,15},{10,... | collective-permute-start | bytes 24584 | tf_op jit(solution)/shard_map/ppermute | solution.py:696

commit v5 on v4

--- a/solution.py
+++ b/solution.py
@@ -32,19 +32,27 @@
 
 
 def prep_kernel(
-    owner_ref, slot_ref, cache_hbm, window_ref, wanted_ref, pos_ref, cache_ref, wa_ref, wb_ref, count_ref, sem
+    owner_ref,
+    slot_ref,
+    cache_hbm,
+    window_hbm,
+    wanted_hbm,
+    pos_hbm,
+    cache_ref,
+    wa_ref,
+    wb_ref,
+    wanted_ref,
+    pos_ref,
+    count_ref,
+    window_ref,
+    sem,
 ):
     owners = wanted_ref.shape[0]
     requests, heads = owner_ref.shape
-    copy = pltpu.make_async_copy(cache_hbm, cache_ref, sem)
-    copy.start()
-    half = window_ref.shape[1] // 3
-    w = window_ref[...].astype(F32)
-    first = w[:, : 2 * half]
-    second = jnp.concatenate([w[:, 2 * half :], jnp.zeros((w.shape[0], half), F32)], axis=1)
-    odd = lax.broadcasted_iota(jnp.int32, first.shape, 0) % 2 == 1
-    wa_ref[...] = jnp.where(odd, pltpu.roll(first, half, 1), first)
-    wb_ref[...] = jnp.where(odd, pltpu.roll(second, half, 1), second)
+    window_copy = pltpu.make_async_copy(window_hbm, window_ref, sem.at[0])
+    window_copy.start()
+    cache_copy = pltpu.make_async_copy(cache_hbm, cache_ref, sem.at[1])
+    cache_copy.start()
     for o in range(owners):
         count_ref[o] = 0
         for k in range(CAP):
@@ -56,26 +64,47 @@
             count_ref[o] = k + 1
             wanted_ref[o, 0, k] = slot_ref[r, h] * heads + h
             pos_ref[r * heads + h] = o * CAP + k
-    copy.wait()
+    wanted_copy = pltpu.make_async_copy(wanted_ref, wanted_hbm, sem.at[2])
+    wanted_copy.start()
+    pos_copy = pltpu.make_async_copy(pos_ref, pos_hbm, sem.at[3])
+    pos_copy.start()
+    window_copy.wait()
+    half = window_ref.shape[1] // 3
+    w = window_ref[...].astype(F32)
+    first = w[:, : 2 * half]
+    second = jnp.concatenate([w[:, 2 * half :], jnp.zeros((w.shape[0], half), F32)], axis=1)
+    odd = lax.broadcasted_iota(jnp.int32, first.shape, 0) % 2 == 1
+    wa_ref[...] = jnp.where(odd, pltpu.roll(first, half, 1), first)
+    wb_ref[...] = jnp.where(odd, pltpu.roll(second, half, 1), second)
+    wanted_copy.wait()
+    pos_copy.wait()
+    cache_copy.wait()
 
 
 def prep(hit_owner, hit_slot, cache, window, owners):
     entries = hit_owner.size
     smem = pl.BlockSpec(memory_space=pltpu.SMEM)
     vmem = pl.BlockSpec(memory_space=pltpu.VMEM)
+    hbm = pl.BlockSpec(memory_space=pltpu.HBM)
     blocks, p, n = cache.shape
     return pl.pallas_call(
         prep_kernel,
         out_shape=(
-            jax.ShapeDtypeStruct((owners, 1, 128), jnp.int32),
-            jax.ShapeDtypeStruct((entries,), jnp.int32),
+            pltpu.HBM((owners, 1, 128), jnp.int32),
+            pltpu.HBM((entries,), jnp.int32),
             pltpu.VMEM((blocks, p, n), F32),
             pltpu.VMEM((blocks, n), F32),
             pltpu.VMEM((blocks, n), F32),
         ),
-        in_specs=[smem, smem, pl.BlockSpec(memory_space=pltpu.HBM), vmem],
-        out_specs=(smem, smem, vmem, vmem, vmem),
-        scratch_shapes=[pltpu.SMEM((owners,), jnp.int32), pltpu.SemaphoreType.DMA],
+        in_specs=[smem, smem, hbm, hbm],
+        out_specs=(hbm, hbm, vmem, vmem, vmem),
+        scratch_shapes=[
+            pltpu.SMEM((owners, 1, 128), jnp.int32),
+            pltpu.SMEM((entries,), jnp.int32),
+            pltpu.SMEM((owners,), jnp.int32),
+            pltpu.VMEM(window.shape, window.dtype),
+            pltpu.SemaphoreType.DMA((4,)),
+        ],
         compiler_params=pltpu.CompilerParams(vmem_limit_bytes=8 * MIB),
         name="prep",
     )(*in_hbm(hit_owner, hit_slot, cache, window))
@@ -423,25 +452,28 @@
     def rows_of(r):
         return slice(r * seq, r * seq + seq)
 
-    def ez_copy(r):
-        return pltpu.make_async_copy(ez_hbm.at[rows_of(r)], ez_ref.at[rows_of(r)], ez_sem.at[r])
-
-    def fetch(r):
-        for h in range(heads):
-            e = r * heads + h
+    batch = requests // 2
+
+    def ez_copy(i):
+        rows = slice(i * batch * seq, (i + 1) * batch * seq)
+        return pltpu.make_async_copy(ez_hbm.at[rows], ez_ref.at[rows], ez_sem.at[i])
+
+    def fetch(i):
+        ez_copy(i).start()
+        for e in range(i * batch * heads, (i + 1) * batch * heads):
             at = pos_ref[e]
             pltpu.make_async_copy(
                 back_ref.at[at // CAP, pl.ds(pl.multiple_of((at % CAP) * p, p), p)],
                 held_ref.at[e],
-                sem.at[r],
+                sem.at[i],
             ).start()
-        ez_copy(r).start()
 
     row_copy = pltpu.make_async_copy(back_ref.at[:, CAP * p :], rows_ref, once_sem.at[0])
     f1_copy = pltpu.make_async_copy(f1_hbm, f1_ref, once_sem.at[1])
     row_copy.start()
     fetch(0)
     fetch(1)
+    f1_copy.start()
     win_ref[...] = jnp.zeros_like(win_ref)
     x_ref[...] = jnp.zeros_like(x_ref)
     row_copy.wait()
@@ -481,23 +513,20 @@
     s_ref[0, :, n:] = grow
     s_ref[1, :, n:] = grow
 
-    for r in range(2, requests):
-        fetch(r)
-    f1_copy.start()
-
     row16 = lax.broadcasted_iota(jnp.int32, (16, 256), 0)
     nt = (((1,), (1,)), ((), ()))
     squares = []
     for r in range(requests):
         rows = rows_of(r)
-        part = held_ref.at[r * heads : r * heads + heads]
-        pltpu.make_async_copy(part, part, sem.at[r]).wait()
+        if r % batch == 0:
+            part = held_ref.at[r * heads : (r + batch) * heads]
+            pltpu.make_async_copy(part, part, sem.at[r // batch]).wait()
+            ez_copy(r // batch).wait()
         for h in range(heads):
             at = slice(h * p, h * p + p)
             block = held_ref[r * heads + h]
             raw_ref[r % 2, at] = block.astype(BF16)
             s_ref[r % 2, at, :n] = (small_ref[r, heads + h : heads + h + 1] * block).astype(BF16)
-        ez_copy(r).wait()
         c = c_ref[rows]
         total = jnp.zeros((seq - 16, 128), F32)
         total16 = jnp.zeros((16, 128), F32)
@@ -554,8 +583,8 @@
             pltpu.VMEM((requests * heads // 2, 128), F32),
             pltpu.VMEM((requests, 16, width), F32),
             pltpu.VMEM((requests, 8, width), F32),
-            pltpu.SemaphoreType.DMA((requests,)),
-            pltpu.SemaphoreType.DMA((requests,)),
+            pltpu.SemaphoreType.DMA((2,)),
+            pltpu.SemaphoreType.DMA((2,)),
             pltpu.SemaphoreType.DMA((2,)),
         ],
         compiler_params=pltpu.CompilerParams(vmem_limit_bytes=24 * MIB),

time: 98.9 us -> 97.7 us (0.988)
  Pallas kernels: 61.8 us -> 60.5 us
  transfers between devices with their start and end apart: 5 -> 5, of which waited for: 3 -> 3; matrix products, arithmetic and copies ran while one was open for 2% -> 2% of each run, Pallas kernels for 50% -> 51%
where the time goes in v5:
time: 97.7 us; the launch traced here: 97.4 us
  Pallas kernels  60.5 us (62%)
  blocking collectives  15.6 us (16%)
  starting transfers between devices  10.4 us (11%)
  waiting for transfers between devices  8.41 us (9%)
  local copies, waits for them, and re-layouts  1.59 us (2%)
    pallas_call x1, Pallas kernels, project(): pl.pallas_call(functools.partial(project_kernel, steps), out_shape=(jax.S...  30.5 us
    pallas_call x1, Pallas kernels, ssd(): pl.pallas_call(ssd_kernel, out_shape=(pltpu.VMEM((tokens, width), BF16),...  17.3 us
    all_to_all x1, blocking collectives, local(): lax.all_to_all(wanted, 'dp', split_axis=0, concat_axis=0, tiled=True)  15.6 us
    all_to_all x1, waiting for transfers between devices, local(): back = lax.all_to_all(sent, 'dp', split_axis=0, concat_axis=0, tiled=True)  6.75 us
    ppermute x3, starting transfers between devices, local(): lax.ppermute(square, 'mp', [(i, (i + 2 * s) % groups) for i in range(grou...  5.65 us
    all_to_all x1, starting transfers between devices, local(): back = lax.all_to_all(sent, 'dp', split_axis=0, concat_axis=0, tiled=True)  4.69 us
    pallas_call x1, Pallas kernels, tail(): pl.pallas_call(tail_kernel, out_shape=(pltpu.VMEM((tokens, width), BF16),...  4.53 us
    pallas_call x1, Pallas kernels, pick(): pl.pallas_call(pick_kernel, out_shape=pltpu.HBM((owners, CAP * p + 2 * CA...  2.71 us
  transfers between devices with their start and end apart: 5, of which 3 were waited for; matrix products, arithmetic and copies ran while one was open for 2% of the time, Pallas kernels for 51%

profile of v5, /device:TPU:0, one launch (start us, length us, event | category | flops | bytes accessed | tf_op | source)
XLA Modules:
  0.0 97.4 jit_solution(11351618106735684540)
XLA Ops:
  0.6 2.2 %prep.1 = (s32[16,1,128]{2,1,0:T(1,128)}, s32[64]{0:T(128)}, f32[48,64,128]{2,1,0:T(8,128)S(1)}, f32[48,128]{1,0:T(8,128)S(1)}, f32[48,128]{1,0:T(8,128)S(1)}) custom-call(s32[4,16]{1,0:T(4,128)} %owner_ref.1, s32[4,16]{1,0:T(4,128)} %slot_ref.1, f32[48,64,128]{2,1,0:T(8,128)} %bitcast.6, bf16[48,192]{1,0:T(8,128)(2,1)} %bitcast.7), custom_call_target="tpu_custom_call" | custom-call | tf_op jit(solution)/shard_map/prep/pallas_call | solution.py:90
  2.8 15.6 %all_to_all.10.codes_ref = s32[16,1,128]{2,1,0:T(1,128)S(1)} all-to-all(s32[16,1,128]{2,1,0:T(1,128)} %get-tuple-element.23), channel_id=1, replica_groups=mesh['dp'=16,'mp'=8] {'dp'}, dimensions={0} | all-to-all | bytes 16384 | tf_op jit(solution)/shard_map/all_to_all | solution.py:703
  18.5 2.7 %pick.1 = f32[16,528,128]{2,1,0:T(8,128)} custom-call(s32[16,1,128]{2,1,0:T(1,128)S(1)} %all_to_all.10.codes_ref, f32[48,64,128]{2,1,0:T(8,128)S(1)} %get-tuple-element.24.cache_ref, f32[48,128]{1,0:T(8,128)S(1)} %get-tuple-element.25.wa_ref, f32[48,128]{1,0:T(8,128)S(1)} %get-tuple-element.26.wb_ref), custom_call_target="tpu_custom_call" | custom-call | bytes 8388608 | tf_op jit(solution)/shard_map/pick/pallas_call | solution.py:141
  21.2 0.0 copy-start.5
  21.2 0.0 copy-start.8
  21.2 0.0 copy-start.6
  21.2 4.7 %all-to-all-start.1 = ((f32[16,528,128]{2,1,0:T(8,128)}), f32[16,528,128]{2,1,0:T(8,128)}, u32[]{:S(2)}, u32[]{:S(2)}) async-start(f32[16,528,128]{2,1,0:T(8,128)} %pick.1), calls=%async_computation.1 | async-start | bytes 8650752 | tf_op jit(solution)/shard_map/all_to_all | solution.py:705
  25.9 1.4 %copy.18.wd_ref = bf16[4096,16]{1,0:T(8,128)(2,1)} copy(bf16[4096,16]{0,1:T(8,128)(2,1)S(1)} %copy-done.5) | data formatting | bytes 262144 | tf_op args[4]
  27.3 0.1 broadcast_in_dim.14
  27.4 0.1 broadcast_in_dim_reshape.3.skip_ref
  27.5 0.0 copy-start.1
  27.5 0.0 copy-start.2
  27.5 0.0 copy-start.3
  27.5 0.0 copy-start.4
  27.5 30.5 %project.1 = (bf16[1024,1024]{1,0:T(8,128)(2,1)}, bf16[1024,1024]{1,0:T(8,128)(2,1)}, bf16[1024,256]{1,0:T(8,128)(2,1)}, f32[1024,16]{1,0:T(8,128)}) custom-call(bf16[1024,4096]{1,0:T(8,128)(2,1)} %act_ref.1, bf16[4096,1024]{1,0:T(8,128)(2,1)} %wi_ref.1, bf16[4096,1024]{1,0:T(8,128)(2,1)} %wg_ref.1, bf16[4096,256]{1,0:T(8,128)(2,1)} %ws_ref.1, ...), custom_call_target="tpu_custom_call" | custom-call | flops 19461570560 | bytes 33554432 | tf_op jit(solution)/shard_map/project/pallas_call | solution.py:193
  58.1 0.0 copy-done.1
  58.1 0.0 copy-done.2
  58.1 0.0 copy-done.3
  58.1 0.0 copy-done.4
  58.1 17.3 %ssd.1 = (bf16[1024,1024]{1,0:T(8,128)(2,1)S(1)}, bf16[1024,1024]{1,0:T(8,128)(2,1)}, bf16[1024,256]{1,0:T(8,128)(2,1)S(1)}, f32[4,1024,128]{2,1,0:T(8,128)}, f3...) custom-call(bf16[1024,1024]{1,0:T(8,128)(2,1)} %get-tuple-element.27.inner_ref, ...), custom_call_target="tpu_custom_call" | custom-call | flops 1073741824 | bytes 14680064 | tf_op jit(solution)/shard_map/ssd/pallas_call | solution.py:370
  75.4 6.8 %all-to-all-done.1.back_ref = f32[16,528,128]{2,1,0:T(8,128)} async-done(((f32[16,528,128]{2,1,0:T(8,128)}), f32[16,528,128]{2,1,0:T(8,128)}, u32[]{:S(2)}, u32[]{:S(2)}) %all-to-all-start.1) | async-done | bytes 4325408 | tf_op jit(solution)/shard_map/all_to_all | solution.py:705
  82.2 4.5 %tail.1 = (bf16[1024,1024]{1,0:T(8,128)(2,1)S(1)}, f32[8,256]{1,0:T(8,128)S(1)}, bf16[1024,32]{1,0:T(8,128)(2,1)S(1)}, f32[64,64,128]{2,1,0:T(8,128)S(1)}, f32[4,1024,128]{2,1,0:T(8,128)S(1)}) custom-call(s32[64]{0:T(128)S(1)} %copy-done, f32[16,528,128]{2,1,0:T(8,128)} %all-to-all-done.1.back_ref, bf16[1024,1024]{1,0:T(8,128)(2,1)} %get-tuple-element.31.ez_hbm, ...), custom_call_target="tpu_custom_call" | custom-call | flops 268435456 | bytes 10485760 | tf_op jit(solution)/shard_map/tail/pallas_call | solution.py:566
  86.7 0.1 collective-permute-start
  86.8 1.2 %collective-permute-done = f32[8,256]{1,0:T(8,128)S(1)} collective-permute-done((f32[8,256]{1,0:T(8,128)S(1)}, f32[8,256]{1,0:T(8,128)S(1)}, u32[]{:S(2)}, u32[]{:S(2)}) %collective-permute-start) | collective-permute-done | bytes 8224 | tf_op jit(solution)/shard_map/ppermute | solution.py:723
  88.0 1.5 %collective-permute-start.1 = (f32[8,256]{1,0:T(8,128)S(1)}, f32[8,256]{1,0:T(8,128)S(1)}, u32[]{:S(2)}, u32[]{:S(2)}) collective-permute-start(f32[8,256]{1,0:T(8,128)S(1)} %add.3.s0_ref), channel_id=1, source_target_pairs={{0,2},{1,3},{2,4},{3,5},{4,6},{5,7},{6,0},{7,1},{8,10},{9,11},{10,... | collective-permute-start | bytes 24584 | tf_op jit(solution)/shard_map/ppermute | solution.py:725
  89.5 2.7 %collective-permute-start.2 = (f32[8,256]{1,0:T(8,128)S(1)}, f32[8,256]{1,0:T(8,128)S(1)}, u32[]{:S(2)}, u32[]{:S(2)}) collective-permute-start(f32[8,256]{1,0:T(8,128)S(1)} %add.3.s0_ref), channel_id=1, source_target_pairs={{0,4},{1,5},{2,6},{3,7},{4,0},{5,1},{6,2},{7,3},{8,12},{9,13},{10,... | collective-permute-start | bytes 24584 | tf_op jit(solution)/shard_map/ppermute | solution.py:725
  92.2 1.4 %collective-permute-start.3 = (f32[8,256]{1,0:T(8,128)S(1)}, f32[8,256]{1,0:T(8,128)S(1)}, u32[]{:S(2)}, u32[]{:S(2)}) collective-permute-start(f32[8,256]{1,0:T(8,128)S(1)} %add.3.s0_ref), channel_id=1, source_target_pairs={{0,6},{1,7},{2,0},{3,1},{4,2},{5,3},{6,4},{7,5},{8,14},{9,15},{10,... | collective-permute-start | bytes 24584 | tf_op jit(solution)/shard_map/ppermute | solution.py:725
  93.6 1.7 %finals.1 = f32[4,16,64,128]{3,2,1,0:T(8,128)} custom-call(f32[64,64,128]{2,1,0:T(8,128)S(1)} %get-tuple-element.39.held_ref, bf16[1024,32]{1,0:T(8,128)(2,1)S(1)} %get-tuple-element.40.grow_ref, f32[4,40,128]{2,1,0:T(8,128)S(1)} %get-tuple-element.35.small_ref, f32[4,1024,128]{2,1,0:T(8,128)S(1)} %get-tuple-element.41.f1_ref), custom_call_target="tpu_custom_call" | custom-call | flops 33554432 | bytes 6291456 | tf_op jit(solution)/shard_map/finals/pallas_call | solution.py:620
  95.3 0.0 collective-permute-done.1.s1_ref
  95.3 0.0 collective-permute-done.2.s2_ref
  95.3 0.5 collective-permute-done.3.s3_ref
  95.8 1.6 %normalise.1 = bf16[1024,1024]{1,0:T(8,128)(2,1)} custom-call(bf16[1024,1024]{1,0:T(8,128)(2,1)S(1)} %get-tuple-element.37.g_ref, f32[8,256]{1,0:T(8,128)S(1)} %add.3.s0_ref, f32[8,256]{1,0:T(8,128)S(1)} %collective-permute-done.1.s1_ref, f32[8,256]{1,0:T(8,128)S(1)} %collective-permute-done.2.s2_ref, f32[8,256]{1,0:T(8,128)S(1)} %collective-permute-done.3.s3_ref, ...), custom_call_target="tpu_custom_call" | custom-call | flops 2097152 | bytes 4194304 | tf_op jit(solution)/shard_map/normalise/pallas_call | solution.py:664
  (10 shorter events, 0.0 us)
Async XLA Ops:
  21.2 4.7 %copy-start.5 = (bf16[4096,16]{0,1:T(8,128)(2,1)S(1)}, bf16[4096,16]{0,1:T(8,128)(2,1)}, u32[]{:S(2)}) copy-start(bf16[4096,16]{0,1:T(8,128)(2,1)} %param.20) | copy-start | bytes 393220
  21.2 6.1 %copy-start.8 = (f32[16]{0:T(128)S(1)}, f32[16]{0:T(128)}, u32[]{:S(2)}) copy-start(f32[16]{0:T(128)} %param.25) | copy-start | bytes 196
  21.2 6.3 %copy-start.6 = (bf16[4,3,256]{2,0,1:T(4,128)(2,1)S(1)}, bf16[4,3,256]{2,0,1:T(4,128)(2,1)}, u32[]{:S(2)}) copy-start(bf16[4,3,256]{2,0,1:T(4,128)(2,1)} %param.29) | copy-start | bytes 18436
  21.2 60.9 %all-to-all-start.1 = ((f32[16,528,128]{2,1,0:T(8,128)}), f32[16,528,128]{2,1,0:T(8,128)}, u32[]{:S(2)}, u32[]{:S(2)}) async-start(f32[16,528,128]{2,1,0:T(8,128)} %pick.1), calls=%async_computation.1 | async-start | bytes 8650752 | tf_op jit(solution)/shard_map/all_to_all | solution.py:705
  27.5 30.6 %copy-start.1 = (bf16[4,1024]{1,0:T(4,128)(2,1)S(1)}, bf16[4,1024]{1,0:T(4,128)(2,1)}, u32[]{:S(2)}) copy-start(bf16[4,1024]{1,0:T(4,128)(2,1)} %ik_ref.1) | copy-start | bytes 24580
  27.5 30.6 %copy-start.2 = (bf16[4,256]{1,0:T(4,128)(2,1)S(1)}, bf16[4,256]{1,0:T(4,128)(2,1)}, u32[]{:S(2)}) copy-start(bf16[4,256]{1,0:T(4,128)(2,1)} %sk_ref.1) | copy-start | bytes 6148
  27.5 30.6 %copy-start.3 = (f32[16]{0:T(128)S(1)}, f32[16]{0:T(128)}, u32[]{:S(2)}) copy-start(f32[16]{0:T(128)} %param.23) | copy-start | bytes 196
  27.5 30.6 %copy-start.4 = (f32[16]{0:T(128)S(1)}, f32[16]{0:T(128)}, u32[]{:S(2)}) copy-start(f32[16]{0:T(128)} %param.24) | copy-start | bytes 196
  58.1 24.1 %copy-start = (s32[64]{0:T(128)S(1)}, s32[64]{0:T(128)}, u32[]{:S(2)}) copy-start(s32[64]{0:T(128)} %get-tuple-element.22.pos_ref) | copy-start | bytes 772
  82.2 11.5 %copy-start.7 = (bf16[1024]{0:T(1024)(128)(2,1)S(1)}, bf16[1024]{0:T(1024)(128)(2,1)}, u32[]{:S(2)}) copy-start(bf16[1024]{0:T(1024)(128)(2,1)} %param.26) | copy-start | bytes 6148
  86.7 1.3 %collective-permute-start = (f32[8,256]{1,0:T(8,128)S(1)}, f32[8,256]{1,0:T(8,128)S(1)}, u32[]{:S(2)}, u32[]{:S(2)}) collective-permute-start(f32[8,256]{1,0:T(8,128)S(1)} %get-tuple-element.38), channel_id=1, source_target_pairs={{0,1},{1,0},{2,3},{3,2},{4,5},{5,4},{6,7},{7,6},{8,9},{9,8},{10,11... | collective-permute-start | bytes 24584 | tf_op jit(solution)/shard_map/ppermute | solution.py:723
  88.0 7.4 %collective-permute-start.1 = (f32[8,256]{1,0:T(8,128)S(1)}, f32[8,256]{1,0:T(8,128)S(1)}, u32[]{:S(2)}, u32[]{:S(2)}) collective-permute-start(f32[8,256]{1,0:T(8,128)S(1)} %add.3.s0_ref), channel_id=1, source_target_pairs={{0,2},{1,3},{2,4},{3,5},{4,6},{5,7},{6,0},{7,1},{8,10},{9,11},{10,... | collective-permute-start | bytes 24584 | tf_op jit(solution)/shard_map/ppermute | solution.py:725
  89.5 5.9 %collective-permute-start.2 = (f32[8,256]{1,0:T(8,128)S(1)}, f32[8,256]{1,0:T(8,128)S(1)}, u32[]{:S(2)}, u32[]{:S(2)}) collective-permute-start(f32[8,256]{1,0:T(8,128)S(1)} %add.3.s0_ref), channel_id=1, source_target_pairs={{0,4},{1,5},{2,6},{3,7},{4,0},{5,1},{6,2},{7,3},{8,12},{9,13},{10,... | collective-permute-start | bytes 24584 | tf_op jit(solution)/shard_map/ppermute | solution.py:725
  92.2 3.7 %collective-permute-start.3 = (f32[8,256]{1,0:T(8,128)S(1)}, f32[8,256]{1,0:T(8,128)S(1)}, u32[]{:S(2)}, u32[]{:S(2)}) collective-permute-start(f32[8,256]{1,0:T(8,128)S(1)} %add.3.s0_ref), channel_id=1, source_target_pairs={{0,6},{1,7},{2,0},{3,1},{4,2},{5,3},{6,4},{7,5},{8,14},{9,15},{10,... | collective-permute-start | bytes 24584 | tf_op jit(solution)/shard_map/ppermute | solution.py:725

commit v6 on v5

--- a/solution.py
+++ b/solution.py
@@ -32,8 +32,8 @@
 
 
 def prep_kernel(
-    owner_ref,
-    slot_ref,
+    owner_hbm,
+    slot_hbm,
     cache_hbm,
     window_hbm,
     wanted_hbm,
@@ -41,6 +41,8 @@
     cache_ref,
     wa_ref,
     wb_ref,
+    owner_ref,
+    slot_ref,
     wanted_ref,
     pos_ref,
     count_ref,
@@ -49,14 +51,22 @@
 ):
     owners = wanted_ref.shape[0]
     requests, heads = owner_ref.shape
+    tables = [
+        pltpu.make_async_copy(owner_hbm, owner_ref, sem.at[4]),
+        pltpu.make_async_copy(slot_hbm, slot_ref, sem.at[5]),
+    ]
+    for copy in tables:
+        copy.start()
+    cache_copy = pltpu.make_async_copy(cache_hbm, cache_ref, sem.at[1])
+    cache_copy.start()
     window_copy = pltpu.make_async_copy(window_hbm, window_ref, sem.at[0])
     window_copy.start()
-    cache_copy = pltpu.make_async_copy(cache_hbm, cache_ref, sem.at[1])
-    cache_copy.start()
     for o in range(owners):
         count_ref[o] = 0
         for k in range(CAP):
             wanted_ref[o, 0, k] = 0
+    for copy in tables:
+        copy.wait()
     for r in range(requests):
         for h in range(heads):
             o = owner_ref[r, h]
@@ -64,6 +74,8 @@
             count_ref[o] = k + 1
             wanted_ref[o, 0, k] = slot_ref[r, h] * heads + h
             pos_ref[r * heads + h] = o * CAP + k
+    for o in range(owners):
+        wanted_ref[o, 0, CAP] = count_ref[o]
     wanted_copy = pltpu.make_async_copy(wanted_ref, wanted_hbm, sem.at[2])
     wanted_copy.start()
     pos_copy = pltpu.make_async_copy(pos_ref, pos_hbm, sem.at[3])
@@ -83,7 +95,6 @@
 
 def prep(hit_owner, hit_slot, cache, window, owners):
     entries = hit_owner.size
-    smem = pl.BlockSpec(memory_space=pltpu.SMEM)
     vmem = pl.BlockSpec(memory_space=pltpu.VMEM)
     hbm = pl.BlockSpec(memory_space=pltpu.HBM)
     blocks, p, n = cache.shape
@@ -96,31 +107,48 @@
             pltpu.VMEM((blocks, n), F32),
             pltpu.VMEM((blocks, n), F32),
         ),
-        in_specs=[smem, smem, hbm, hbm],
+        in_specs=[hbm] * 4,
         out_specs=(hbm, hbm, vmem, vmem, vmem),
         scratch_shapes=[
+            pltpu.SMEM(hit_owner.shape, jnp.int32),
+            pltpu.SMEM(hit_slot.shape, jnp.int32),
             pltpu.SMEM((owners, 1, 128), jnp.int32),
             pltpu.SMEM((entries,), jnp.int32),
             pltpu.SMEM((owners,), jnp.int32),
             pltpu.VMEM(window.shape, window.dtype),
-            pltpu.SemaphoreType.DMA((4,)),
+            pltpu.SemaphoreType.DMA((6,)),
         ],
         compiler_params=pltpu.CompilerParams(vmem_limit_bytes=8 * MIB),
         name="prep",
     )(*in_hbm(hit_owner, hit_slot, cache, window))
 
 
-def pick_kernel(codes_ref, cache_ref, wa_ref, wb_ref, out_ref, rows_ref, sem):
+def pick_kernel(codes_ref, cache_ref, wa_ref, wb_ref, out_ref, rows_ref, extra_ref, sem, extra_sem):
     owners = out_ref.shape[0]
     p = cache_ref.shape[1]
     cached = CAP * p
+    always = CAP // 2
+    extra_ref[0] = 0
 
     @pl.loop(0, owners)
     def _(d):
-        for k in range(CAP):
+        for k in range(always):
             pltpu.make_async_copy(
                 cache_ref.at[codes_ref[d, 0, k]], out_ref.at[d, k * p : k * p + p], sem
             ).start()
+        count = codes_ref[d, 0, CAP]
+
+        @pl.when(count > always)
+        def _():
+            extra_ref[0] += count - always
+
+            @pl.loop(always, count)
+            def _(k):
+                pltpu.make_async_copy(
+                    cache_ref.at[codes_ref[d, 0, k]],
+                    out_ref.at[d, pl.ds(pl.multiple_of(k * p, p), p)],
+                    extra_sem,
+                ).start()
 
     @pl.loop(0, owners)
     def _(d):
@@ -130,7 +158,13 @@
             rows_ref[d, 2 * k + 1 : 2 * k + 2] = wb_ref[at]
 
     pltpu.make_async_copy(rows_ref, out_ref.at[:, cached:], sem).start()
-    pltpu.make_async_copy(out_ref, out_ref, sem).wait()
+
+    @pl.loop(0, extra_ref[0])
+    def _(_):
+        pltpu.make_async_copy(cache_ref.at[0], out_ref.at[0, :p], extra_sem).wait()
+
+    done = out_ref.at[:, : always * p + 2 * CAP]
+    pltpu.make_async_copy(done, done, sem).wait()
 
 
 def pick(codes, cache, wa, wb):
@@ -143,7 +177,12 @@
         out_shape=pltpu.HBM((owners, CAP * p + 2 * CAP, n), F32),
         in_specs=[pl.BlockSpec(memory_space=pltpu.SMEM), vmem, vmem, vmem],
         out_specs=hbm,
-        scratch_shapes=[pltpu.VMEM((owners, 2 * CAP, n), F32), pltpu.SemaphoreType.DMA],
+        scratch_shapes=[
+            pltpu.VMEM((owners, 2 * CAP, n), F32),
+            pltpu.SMEM((1,), jnp.int32),
+            pltpu.SemaphoreType.DMA,
+            pltpu.SemaphoreType.DMA,
+        ],
         compiler_params=pltpu.CompilerParams(vmem_limit_bytes=8 * MIB),
         cost_estimate=pl.CostEstimate(flops=0, bytes_accessed=8 * MIB, transcendentals=0),
         name="pick",

time: 97.7 us -> 96.8 us (level)
  no operation moved by 1% of the time
where the time goes in v6:
time: 96.8 us; the launch traced here: 96.4 us
  Pallas kernels  59.6 us (62%)
  blocking collectives  15.6 us (16%)
  starting transfers between devices  10.4 us (11%)
  waiting for transfers between devices  8.38 us (9%)
  local copies, waits for them, and re-layouts  1.59 us (2%)
    pallas_call x1, Pallas kernels, project(): pl.pallas_call(functools.partial(project_kernel, steps), out_shape=(jax.S...  30.6 us
    pallas_call x1, Pallas kernels, ssd(): pl.pallas_call(ssd_kernel, out_shape=(pltpu.VMEM((tokens, width), BF16),...  17.3 us
    all_to_all x1, blocking collectives, local(): lax.all_to_all(wanted, 'dp', split_axis=0, concat_axis=0, tiled=True)  15.6 us
    all_to_all x1, waiting for transfers between devices, local(): back = lax.all_to_all(sent, 'dp', split_axis=0, concat_axis=0, tiled=True)  6.78 us
    ppermute x3, starting transfers between devices, local(): lax.ppermute(square, 'mp', [(i, (i + 2 * s) % groups) for i in range(grou...  5.67 us
    all_to_all x1, starting transfers between devices, local(): back = lax.all_to_all(sent, 'dp', split_axis=0, concat_axis=0, tiled=True)  4.69 us
    pallas_call x1, Pallas kernels, tail(): pl.pallas_call(tail_kernel, out_shape=(pltpu.VMEM((tokens, width), BF16),...  4.53 us
    pallas_call x1, Pallas kernels, pick(): pl.pallas_call(pick_kernel, out_shape=pltpu.HBM((owners, CAP * p + 2 * CA...  2.16 us
  transfers between devices with their start and end apart: 5, of which 3 were waited for; matrix products, arithmetic and copies ran while one was open for 2% of the time, Pallas kernels for 51%

profile of v6, /device:TPU:0, one launch (start us, length us, event | category | flops | bytes accessed | tf_op | source)
XLA Modules:
  0.0 96.4 jit_solution(18840043872132394)
XLA Ops:
  0.6 1.8 %prep.1 = (s32[16,1,128]{2,1,0:T(1,128)}, s32[64]{0:T(128)}, f32[48,64,128]{2,1,0:T(8,128)S(1)}, f32[48,128]{1,0:T(8,128)S(1)}, f32[48,128]{1,0:T(8,128)S(1)}) custom-call(s32[4,16]{1,0:T(4,128)} %owner_hbm.1, s32[4,16]{1,0:T(4,128)} %slot_hbm.1, f32[48,64,128]{2,1,0:T(8,128)} %bitcast.6, bf16[48,192]{1,0:T(8,128)(2,1)} %bitcast.7), custom_call_target="tpu_custom_call" | custom-call | tf_op jit(solution)/shard_map/prep/pallas_call | solution.py:101
  2.4 15.6 %all_to_all.10.codes_ref = s32[16,1,128]{2,1,0:T(1,128)S(1)} all-to-all(s32[16,1,128]{2,1,0:T(1,128)} %get-tuple-element.23), channel_id=1, replica_groups=mesh['dp'=16,'mp'=8] {'dp'}, dimensions={0} | all-to-all | bytes 16384 | tf_op jit(solution)/shard_map/all_to_all | solution.py:742
  18.1 2.2 %pick.1 = f32[16,528,128]{2,1,0:T(8,128)} custom-call(s32[16,1,128]{2,1,0:T(1,128)S(1)} %all_to_all.10.codes_ref, f32[48,64,128]{2,1,0:T(8,128)S(1)} %get-tuple-element.24.cache_ref, f32[48,128]{1,0:T(8,128)S(1)} %get-tuple-element.25.wa_ref, f32[48,128]{1,0:T(8,128)S(1)} %get-tuple-element.26.wb_ref), custom_call_target="tpu_custom_call" | custom-call | bytes 8388608 | tf_op jit(solution)/shard_map/pick/pallas_call | solution.py:175
  20.2 0.0 copy-start.5
  20.2 0.0 copy-start.8
  20.3 0.0 copy-start.6
  20.3 4.7 %all-to-all-start.1 = ((f32[16,528,128]{2,1,0:T(8,128)}), f32[16,528,128]{2,1,0:T(8,128)}, u32[]{:S(2)}, u32[]{:S(2)}) async-start(f32[16,528,128]{2,1,0:T(8,128)} %pick.1), calls=%async_computation.1 | async-start | bytes 8650752 | tf_op jit(solution)/shard_map/all_to_all | solution.py:744
  25.0 0.0 copy-done.5
  25.0 1.4 %copy.18.wd_ref = bf16[4096,16]{1,0:T(8,128)(2,1)} copy(bf16[4096,16]{0,1:T(8,128)(2,1)S(1)} %copy-done.5) | data formatting | bytes 262144 | tf_op args[4]
  26.4 0.0 copy-done.8
  26.4 0.1 broadcast_in_dim.14
  26.4 0.1 broadcast_in_dim_reshape.3.skip_ref
  26.5 0.0 copy-done.6
  26.5 0.0 copy-start.1
  26.5 0.0 copy-start.2
  26.5 0.0 copy-start.3
  26.6 0.0 copy-start.4
  26.6 30.6 %project.1 = (bf16[1024,1024]{1,0:T(8,128)(2,1)}, bf16[1024,1024]{1,0:T(8,128)(2,1)}, bf16[1024,256]{1,0:T(8,128)(2,1)}, f32[1024,16]{1,0:T(8,128)}) custom-call(bf16[1024,4096]{1,0:T(8,128)(2,1)} %act_ref.1, bf16[4096,1024]{1,0:T(8,128)(2,1)} %wi_ref.1, bf16[4096,1024]{1,0:T(8,128)(2,1)} %wg_ref.1, bf16[4096,256]{1,0:T(8,128)(2,1)} %ws_ref.1, ...), custom_call_target="tpu_custom_call" | custom-call | flops 19461570560 | bytes 33554432 | tf_op jit(solution)/shard_map/project/pallas_call | solution.py:232
  57.1 0.0 copy-done.1
  57.2 17.3 %ssd.1 = (bf16[1024,1024]{1,0:T(8,128)(2,1)S(1)}, bf16[1024,1024]{1,0:T(8,128)(2,1)}, bf16[1024,256]{1,0:T(8,128)(2,1)S(1)}, f32[4,1024,128]{2,1,0:T(8,128)}, f3...) custom-call(bf16[1024,1024]{1,0:T(8,128)(2,1)} %get-tuple-element.27.inner_ref, ...), custom_call_target="tpu_custom_call" | custom-call | flops 1073741824 | bytes 14680064 | tf_op jit(solution)/shard_map/ssd/pallas_call | solution.py:409
  74.5 6.8 %all-to-all-done.1.back_ref = f32[16,528,128]{2,1,0:T(8,128)} async-done(((f32[16,528,128]{2,1,0:T(8,128)}), f32[16,528,128]{2,1,0:T(8,128)}, u32[]{:S(2)}, u32[]{:S(2)}) %all-to-all-start.1) | async-done | bytes 4325408 | tf_op jit(solution)/shard_map/all_to_all | solution.py:744
  81.2 4.5 %tail.1 = (bf16[1024,1024]{1,0:T(8,128)(2,1)S(1)}, f32[8,256]{1,0:T(8,128)S(1)}, bf16[1024,32]{1,0:T(8,128)(2,1)S(1)}, f32[64,64,128]{2,1,0:T(8,128)S(1)}, f32[4,1024,128]{2,1,0:T(8,128)S(1)}) custom-call(s32[64]{0:T(128)S(1)} %copy-done, f32[16,528,128]{2,1,0:T(8,128)} %all-to-all-done.1.back_ref, bf16[1024,1024]{1,0:T(8,128)(2,1)} %get-tuple-element.31.ez_hbm, ...), custom_call_target="tpu_custom_call" | custom-call | flops 268435456 | bytes 10485760 | tf_op jit(solution)/shard_map/tail/pallas_call | solution.py:605
  85.8 0.1 collective-permute-start
  85.9 1.2 %collective-permute-done = f32[8,256]{1,0:T(8,128)S(1)} collective-permute-done((f32[8,256]{1,0:T(8,128)S(1)}, f32[8,256]{1,0:T(8,128)S(1)}, u32[]{:S(2)}, u32[]{:S(2)}) %collective-permute-start) | collective-permute-done | bytes 8224 | tf_op jit(solution)/shard_map/ppermute | solution.py:762
  87.0 1.4 %collective-permute-start.1 = (f32[8,256]{1,0:T(8,128)S(1)}, f32[8,256]{1,0:T(8,128)S(1)}, u32[]{:S(2)}, u32[]{:S(2)}) collective-permute-start(f32[8,256]{1,0:T(8,128)S(1)} %add.3.s0_ref), channel_id=1, source_target_pairs={{0,2},{1,3},{2,4},{3,5},{4,6},{5,7},{6,0},{7,1},{8,10},{9,11},{10,... | collective-permute-start | bytes 24584 | tf_op jit(solution)/shard_map/ppermute | solution.py:764
  88.4 2.8 %collective-permute-start.2 = (f32[8,256]{1,0:T(8,128)S(1)}, f32[8,256]{1,0:T(8,128)S(1)}, u32[]{:S(2)}, u32[]{:S(2)}) collective-permute-start(f32[8,256]{1,0:T(8,128)S(1)} %add.3.s0_ref), channel_id=1, source_target_pairs={{0,4},{1,5},{2,6},{3,7},{4,0},{5,1},{6,2},{7,3},{8,12},{9,13},{10,... | collective-permute-start | bytes 24584 | tf_op jit(solution)/shard_map/ppermute | solution.py:764
  91.2 1.5 %collective-permute-start.3 = (f32[8,256]{1,0:T(8,128)S(1)}, f32[8,256]{1,0:T(8,128)S(1)}, u32[]{:S(2)}, u32[]{:S(2)}) collective-permute-start(f32[8,256]{1,0:T(8,128)S(1)} %add.3.s0_ref), channel_id=1, source_target_pairs={{0,6},{1,7},{2,0},{3,1},{4,2},{5,3},{6,4},{7,5},{8,14},{9,15},{10,... | collective-permute-start | bytes 24584 | tf_op jit(solution)/shard_map/ppermute | solution.py:764
  92.7 1.7 %finals.1 = f32[4,16,64,128]{3,2,1,0:T(8,128)} custom-call(f32[64,64,128]{2,1,0:T(8,128)S(1)} %get-tuple-element.39.held_ref, bf16[1024,32]{1,0:T(8,128)(2,1)S(1)} %get-tuple-element.40.grow_ref, f32[4,40,128]{2,1,0:T(8,128)S(1)} %get-tuple-element.35.small_ref, f32[4,1024,128]{2,1,0:T(8,128)S(1)} %get-tuple-element.41.f1_ref), custom_call_target="tpu_custom_call" | custom-call | flops 33554432 | bytes 6291456 | tf_op jit(solution)/shard_map/finals/pallas_call | solution.py:659
  94.4 0.0 collective-permute-done.1.s1_ref
  94.4 0.0 collective-permute-done.2.s2_ref
  94.4 0.4 collective-permute-done.3.s3_ref
  94.9 1.6 %normalise.1 = bf16[1024,1024]{1,0:T(8,128)(2,1)} custom-call(bf16[1024,1024]{1,0:T(8,128)(2,1)S(1)} %get-tuple-element.37.g_ref, f32[8,256]{1,0:T(8,128)S(1)} %add.3.s0_ref, f32[8,256]{1,0:T(8,128)S(1)} %collective-permute-done.1.s1_ref, f32[8,256]{1,0:T(8,128)S(1)} %collective-permute-done.2.s2_ref, f32[8,256]{1,0:T(8,128)S(1)} %collective-permute-done.3.s3_ref, ...), custom_call_target="tpu_custom_call" | custom-call | flops 2097152 | bytes 4194304 | tf_op jit(solution)/shard_map/normalise/pallas_call | solution.py:703
  (10 shorter events, 0.0 us)
Async XLA Ops:
  20.2 4.7 %copy-start.5 = (bf16[4096,16]{0,1:T(8,128)(2,1)S(1)}, bf16[4096,16]{0,1:T(8,128)(2,1)}, u32[]{:S(2)}) copy-start(bf16[4096,16]{0,1:T(8,128)(2,1)} %param.20) | copy-start | bytes 393220
  20.2 6.1 %copy-start.8 = (f32[16]{0:T(128)S(1)}, f32[16]{0:T(128)}, u32[]{:S(2)}) copy-start(f32[16]{0:T(128)} %param.25) | copy-start | bytes 196
  20.3 6.3 %copy-start.6 = (bf16[4,3,256]{2,0,1:T(4,128)(2,1)S(1)}, bf16[4,3,256]{2,0,1:T(4,128)(2,1)}, u32[]{:S(2)}) copy-start(bf16[4,3,256]{2,0,1:T(4,128)(2,1)} %param.29) | copy-start | bytes 18436
  20.3 61.0 %all-to-all-start.1 = ((f32[16,528,128]{2,1,0:T(8,128)}), f32[16,528,128]{2,1,0:T(8,128)}, u32[]{:S(2)}, u32[]{:S(2)}) async-start(f32[16,528,128]{2,1,0:T(8,128)} %pick.1), calls=%async_computation.1 | async-start | bytes 8650752 | tf_op jit(solution)/shard_map/all_to_all | solution.py:744
  26.5 30.6 %copy-start.1 = (bf16[4,1024]{1,0:T(4,128)(2,1)S(1)}, bf16[4,1024]{1,0:T(4,128)(2,1)}, u32[]{:S(2)}) copy-start(bf16[4,1024]{1,0:T(4,128)(2,1)} %ik_ref.1) | copy-start | bytes 24580
  26.5 30.6 %copy-start.2 = (bf16[4,256]{1,0:T(4,128)(2,1)S(1)}, bf16[4,256]{1,0:T(4,128)(2,1)}, u32[]{:S(2)}) copy-start(bf16[4,256]{1,0:T(4,128)(2,1)} %sk_ref.1) | copy-start | bytes 6148
  26.5 30.6 %copy-start.3 = (f32[16]{0:T(128)S(1)}, f32[16]{0:T(128)}, u32[]{:S(2)}) copy-start(f32[16]{0:T(128)} %param.23) | copy-start | bytes 196
  26.6 30.6 %copy-start.4 = (f32[16]{0:T(128)S(1)}, f32[16]{0:T(128)}, u32[]{:S(2)}) copy-start(f32[16]{0:T(128)} %param.24) | copy-start | bytes 196
  57.2 24.1 %copy-start = (s32[64]{0:T(128)S(1)}, s32[64]{0:T(128)}, u32[]{:S(2)}) copy-start(s32[64]{0:T(128)} %get-tuple-element.22.pos_ref) | copy-start | bytes 772
  81.2 11.5 %copy-start.7 = (bf16[1024]{0:T(1024)(128)(2,1)S(1)}, bf16[1024]{0:T(1024)(128)(2,1)}, u32[]{:S(2)}) copy-start(bf16[1024]{0:T(1024)(128)(2,1)} %param.26) | copy-start | bytes 6148
  85.8 1.3 %collective-permute-start = (f32[8,256]{1,0:T(8,128)S(1)}, f32[8,256]{1,0:T(8,128)S(1)}, u32[]{:S(2)}, u32[]{:S(2)}) collective-permute-start(f32[8,256]{1,0:T(8,128)S(1)} %get-tuple-element.38), channel_id=1, source_target_pairs={{0,1},{1,0},{2,3},{3,2},{4,5},{5,4},{6,7},{7,6},{8,9},{9,8},{10,11... | collective-permute-start | bytes 24584 | tf_op jit(solution)/shard_map/ppermute | solution.py:762
  87.0 7.4 %collective-permute-start.1 = (f32[8,256]{1,0:T(8,128)S(1)}, f32[8,256]{1,0:T(8,128)S(1)}, u32[]{:S(2)}, u32[]{:S(2)}) collective-permute-start(f32[8,256]{1,0:T(8,128)S(1)} %add.3.s0_ref), channel_id=1, source_target_pairs={{0,2},{1,3},{2,4},{3,5},{4,6},{5,7},{6,0},{7,1},{8,10},{9,11},{10,... | collective-permute-start | bytes 24584 | tf_op jit(solution)/shard_map/ppermute | solution.py:764
  88.4 6.0 %collective-permute-start.2 = (f32[8,256]{1,0:T(8,128)S(1)}, f32[8,256]{1,0:T(8,128)S(1)}, u32[]{:S(2)}, u32[]{:S(2)}) collective-permute-start(f32[8,256]{1,0:T(8,128)S(1)} %add.3.s0_ref), channel_id=1, source_target_pairs={{0,4},{1,5},{2,6},{3,7},{4,0},{5,1},{6,2},{7,3},{8,12},{9,13},{10,... | collective-permute-start | bytes 24584 | tf_op jit(solution)/shard_map/ppermute | solution.py:764
  91.2 3.7 %collective-permute-start.3 = (f32[8,256]{1,0:T(8,128)S(1)}, f32[8,256]{1,0:T(8,128)S(1)}, u32[]{:S(2)}, u32[]{:S(2)}) collective-permute-start(f32[8,256]{1,0:T(8,128)S(1)} %add.3.s0_ref), channel_id=1, source_target_pairs={{0,6},{1,7},{2,0},{3,1},{4,2},{5,3},{6,4},{7,5},{8,14},{9,15},{10,... | collective-permute-start | bytes 24584 | tf_op jit(solution)/shard_map/ppermute | solution.py:764

commit v7 on v6

--- a/solution.py
+++ b/solution.py
@@ -455,7 +455,7 @@
 
 
 def tail_kernel(
-    pos_ref,
+    pos_hbm,
     back_ref,
     ez_hbm,
     f1_hbm,
@@ -468,6 +468,7 @@
     grow_ref,
     held_ref,
     f1_ref,
+    pos_ref,
     ez_ref,
     rows_ref,
     s_ref,
@@ -498,7 +499,6 @@
         return pltpu.make_async_copy(ez_hbm.at[rows], ez_ref.at[rows], ez_sem.at[i])
 
     def fetch(i):
-        ez_copy(i).start()
         for e in range(i * batch * heads, (i + 1) * batch * heads):
             at = pos_ref[e]
             pltpu.make_async_copy(
@@ -509,12 +509,17 @@
 
     row_copy = pltpu.make_async_copy(back_ref.at[:, CAP * p :], rows_ref, once_sem.at[0])
     f1_copy = pltpu.make_async_copy(f1_hbm, f1_ref, once_sem.at[1])
+    pos_copy = pltpu.make_async_copy(pos_hbm, pos_ref, once_sem.at[2])
+    pos_copy.start()
     row_copy.start()
+    ez_copy(0).start()
+    win_ref[...] = jnp.zeros_like(win_ref)
+    x_ref[...] = jnp.zeros_like(x_ref)
+    pos_copy.wait()
     fetch(0)
+    ez_copy(1).start()
     fetch(1)
     f1_copy.start()
-    win_ref[...] = jnp.zeros_like(win_ref)
-    x_ref[...] = jnp.zeros_like(x_ref)
     row_copy.wait()
 
     low = lax.broadcasted_iota(jnp.int32, (1, 128), 1) < p
@@ -611,9 +616,10 @@
             pltpu.VMEM((requests * heads, p, n), F32),
             pltpu.VMEM(f1.shape, F32),
         ),
-        in_specs=[pl.BlockSpec(memory_space=pltpu.SMEM)] + [hbm] * 3 + [vmem] * 4,
+        in_specs=[hbm] * 4 + [vmem] * 4,
         out_specs=(vmem,) * 5,
         scratch_shapes=[
+            pltpu.SMEM(pos.shape, jnp.int32),
             pltpu.VMEM((tokens, width), BF16),
             pltpu.VMEM((owners, 2 * CAP, n), F32),
             pltpu.VMEM((2, width, 2 * n), BF16),
@@ -624,14 +630,14 @@
             pltpu.VMEM((requests, 8, width), F32),
             pltpu.SemaphoreType.DMA((2,)),
             pltpu.SemaphoreType.DMA((2,)),
-            pltpu.SemaphoreType.DMA((2,)),
+            pltpu.SemaphoreType.DMA((3,)),
         ],
         compiler_params=pltpu.CompilerParams(vmem_limit_bytes=24 * MIB),
         cost_estimate=pl.CostEstimate(
             flops=2 * tokens * width * n, bytes_accessed=10 * MIB, transcendentals=0
         ),
         name="tail",
-    )(pos, *in_hbm(back, ez, f1), *in_vmem(az, c, small, first))
+    )(*in_hbm(pos, back, ez, f1), *in_vmem(az, c, small, first))
 
 
 def final_kernel(held_ref, grow_ref, small_ref, f1_ref, out_ref, made_ref, sem):

time: 96.8 us -> 96.3 us (level)
  transfers between devices with their start and end apart: 5 -> 5, of which waited for: 3 -> 3; matrix products, arithmetic and copies ran while one was open for 2% -> 2% of each run, Pallas kernels for 51% -> 52%
where the time goes in v7:
time: 96.3 us; the launch traced here: 96 us
  Pallas kernels  59.1 us (61%)
  blocking collectives  15.6 us (16%)
  starting transfers between devices  10.7 us (11%)
  waiting for transfers between devices  8.1 us (8%)
  local copies, waits for them, and re-layouts  1.58 us (2%)
    pallas_call x1, Pallas kernels, project(): pl.pallas_call(functools.partial(project_kernel, steps), out_shape=(jax.S...  30.5 us
    pallas_call x1, Pallas kernels, ssd(): pl.pallas_call(ssd_kernel, out_shape=(pltpu.VMEM((tokens, width), BF16),...  17.3 us
    all_to_all x1, blocking collectives, local(): lax.all_to_all(wanted, 'dp', split_axis=0, concat_axis=0, tiled=True)  15.6 us
    all_to_all x1, waiting for transfers between devices, local(): back = lax.all_to_all(sent, 'dp', split_axis=0, concat_axis=0, tiled=True)  6.68 us
    ppermute x3, starting transfers between devices, local(): lax.ppermute(square, 'mp', [(i, (i + 2 * s) % groups) for i in range(grou...  5.95 us
    all_to_all x1, starting transfers between devices, local(): back = lax.all_to_all(sent, 'dp', split_axis=0, concat_axis=0, tiled=True)  4.68 us
    pallas_call x1, Pallas kernels, tail(): pl.pallas_call(tail_kernel, out_shape=(pltpu.VMEM((tokens, width), BF16),...  4.19 us
    pallas_call x1, Pallas kernels, pick(): pl.pallas_call(pick_kernel, out_shape=pltpu.HBM((owners, CAP * p + 2 * CA...  2.03 us
  transfers between devices with their start and end apart: 5, of which 3 were waited for; matrix products, arithmetic and copies ran while one was open for 2% of the time, Pallas kernels for 52%

profile of v7, /device:TPU:0, one launch (start us, length us, event | category | flops | bytes accessed | tf_op | source)
XLA Modules:
  0.0 96.0 jit_solution(12333292333679080477)
XLA Ops:
  0.6 1.8 %prep.1 = (s32[16,1,128]{2,1,0:T(1,128)}, s32[64]{0:T(128)}, f32[48,64,128]{2,1,0:T(8,128)S(1)}, f32[48,128]{1,0:T(8,128)S(1)}, f32[48,128]{1,0:T(8,128)S(1)}) custom-call(s32[4,16]{1,0:T(4,128)} %owner_hbm.1, s32[4,16]{1,0:T(4,128)} %slot_hbm.1, f32[48,64,128]{2,1,0:T(8,128)} %bitcast.6, bf16[48,192]{1,0:T(8,128)(2,1)} %bitcast.7), custom_call_target="tpu_custom_call" | custom-call | tf_op jit(solution)/shard_map/prep/pallas_call | solution.py:101
  2.4 15.6 %all_to_all.10.codes_ref = s32[16,1,128]{2,1,0:T(1,128)S(1)} all-to-all(s32[16,1,128]{2,1,0:T(1,128)} %get-tuple-element.23), channel_id=1, replica_groups=mesh['dp'=16,'mp'=8] {'dp'}, dimensions={0} | all-to-all | bytes 16384 | tf_op jit(solution)/shard_map/all_to_all | solution.py:748
  18.1 2.0 %pick.1 = f32[16,528,128]{2,1,0:T(8,128)} custom-call(s32[16,1,128]{2,1,0:T(1,128)S(1)} %all_to_all.10.codes_ref, f32[48,64,128]{2,1,0:T(8,128)S(1)} %get-tuple-element.24.cache_ref, f32[48,128]{1,0:T(8,128)S(1)} %get-tuple-element.25.wa_ref, f32[48,128]{1,0:T(8,128)S(1)} %get-tuple-element.26.wb_ref), custom_call_target="tpu_custom_call" | custom-call | bytes 8388608 | tf_op jit(solution)/shard_map/pick/pallas_call | solution.py:175
  20.1 0.0 copy-start.4
  20.1 0.0 copy-start.7
  20.1 0.0 copy-start.5
  20.1 4.7 %all-to-all-start.1 = ((f32[16,528,128]{2,1,0:T(8,128)}), f32[16,528,128]{2,1,0:T(8,128)}, u32[]{:S(2)}, u32[]{:S(2)}) async-start(f32[16,528,128]{2,1,0:T(8,128)} %pick.1), calls=%async_computation.1 | async-start | bytes 8650752 | tf_op jit(solution)/shard_map/all_to_all | solution.py:750
  24.8 0.0 copy-done.4
  24.8 1.4 %copy.18.wd_ref = bf16[4096,16]{1,0:T(8,128)(2,1)} copy(bf16[4096,16]{0,1:T(8,128)(2,1)S(1)} %copy-done.4) | data formatting | bytes 262144 | tf_op args[4]
  26.2 0.0 copy-done.7
  26.2 0.1 broadcast_in_dim.14
  26.3 0.1 broadcast_in_dim_reshape.3.skip_ref
  26.4 0.0 copy-done.5
  26.4 0.0 copy-start
  26.4 0.0 copy-start.1
  26.4 0.0 copy-start.2
  26.4 0.0 copy-start.3
  26.4 30.5 %project.1 = (bf16[1024,1024]{1,0:T(8,128)(2,1)}, bf16[1024,1024]{1,0:T(8,128)(2,1)}, bf16[1024,256]{1,0:T(8,128)(2,1)}, f32[1024,16]{1,0:T(8,128)}) custom-call(bf16[1024,4096]{1,0:T(8,128)(2,1)} %act_ref.1, bf16[4096,1024]{1,0:T(8,128)(2,1)} %wi_ref.1, bf16[4096,1024]{1,0:T(8,128)(2,1)} %wg_ref.1, bf16[4096,256]{1,0:T(8,128)(2,1)} %ws_ref.1, ...), custom_call_target="tpu_custom_call" | custom-call | flops 19461570560 | bytes 33554432 | tf_op jit(solution)/shard_map/project/pallas_call | solution.py:232
  57.0 17.3 %ssd.1 = (bf16[1024,1024]{1,0:T(8,128)(2,1)S(1)}, bf16[1024,1024]{1,0:T(8,128)(2,1)}, bf16[1024,256]{1,0:T(8,128)(2,1)S(1)}, f32[4,1024,128]{2,1,0:T(8,128)}, f3...) custom-call(bf16[1024,1024]{1,0:T(8,128)(2,1)} %get-tuple-element.27.inner_ref, ...), custom_call_target="tpu_custom_call" | custom-call | flops 1073741824 | bytes 14680064 | tf_op jit(solution)/shard_map/ssd/pallas_call | solution.py:409
  74.3 6.7 %all-to-all-done.1.back_ref = f32[16,528,128]{2,1,0:T(8,128)} async-done(((f32[16,528,128]{2,1,0:T(8,128)}), f32[16,528,128]{2,1,0:T(8,128)}, u32[]{:S(2)}, u32[]{:S(2)}) %all-to-all-start.1) | async-done | bytes 4325408 | tf_op jit(solution)/shard_map/all_to_all | solution.py:750
  81.0 4.2 %tail.1 = (bf16[1024,1024]{1,0:T(8,128)(2,1)S(1)}, f32[8,256]{1,0:T(8,128)S(1)}, bf16[1024,32]{1,0:T(8,128)(2,1)S(1)}, f32[64,64,128]{2,1,0:T(8,128)S(1)}, f32[4,1024,128]{2,1,0:T(8,128)S(1)}) custom-call(s32[64]{0:T(128)} %get-tuple-element.22.pos_hbm, f32[16,528,128]{2,1,0:T(8,128)} %all-to-all-done.1.back_ref, ...), custom_call_target="tpu_custom_call" | custom-call | flops 268435456 | bytes 10485760 | tf_op jit(solution)/shard_map/tail/pallas_call | solution.py:610
  85.2 0.1 collective-permute-start
  85.3 1.2 %collective-permute-done = f32[8,256]{1,0:T(8,128)S(1)} collective-permute-done((f32[8,256]{1,0:T(8,128)S(1)}, f32[8,256]{1,0:T(8,128)S(1)}, u32[]{:S(2)}, u32[]{:S(2)}) %collective-permute-start) | collective-permute-done | bytes 8224 | tf_op jit(solution)/shard_map/ppermute | solution.py:768
  86.4 1.7 %collective-permute-start.1 = (f32[8,256]{1,0:T(8,128)S(1)}, f32[8,256]{1,0:T(8,128)S(1)}, u32[]{:S(2)}, u32[]{:S(2)}) collective-permute-start(f32[8,256]{1,0:T(8,128)S(1)} %add.3.s0_ref), channel_id=1, source_target_pairs={{0,2},{1,3},{2,4},{3,5},{4,6},{5,7},{6,0},{7,1},{8,10},{9,11},{10,... | collective-permute-start | bytes 24584 | tf_op jit(solution)/shard_map/ppermute | solution.py:770
  88.1 2.6 %collective-permute-start.2 = (f32[8,256]{1,0:T(8,128)S(1)}, f32[8,256]{1,0:T(8,128)S(1)}, u32[]{:S(2)}, u32[]{:S(2)}) collective-permute-start(f32[8,256]{1,0:T(8,128)S(1)} %add.3.s0_ref), channel_id=1, source_target_pairs={{0,4},{1,5},{2,6},{3,7},{4,0},{5,1},{6,2},{7,3},{8,12},{9,13},{10,... | collective-permute-start | bytes 24584 | tf_op jit(solution)/shard_map/ppermute | solution.py:770
  90.7 1.7 %collective-permute-start.3 = (f32[8,256]{1,0:T(8,128)S(1)}, f32[8,256]{1,0:T(8,128)S(1)}, u32[]{:S(2)}, u32[]{:S(2)}) collective-permute-start(f32[8,256]{1,0:T(8,128)S(1)} %add.3.s0_ref), channel_id=1, source_target_pairs={{0,6},{1,7},{2,0},{3,1},{4,2},{5,3},{6,4},{7,5},{8,14},{9,15},{10,... | collective-permute-start | bytes 24584 | tf_op jit(solution)/shard_map/ppermute | solution.py:770
  92.4 0.0 copy-done.6
  92.4 1.7 %finals.1 = f32[4,16,64,128]{3,2,1,0:T(8,128)} custom-call(f32[64,64,128]{2,1,0:T(8,128)S(1)} %get-tuple-element.39.held_ref, bf16[1024,32]{1,0:T(8,128)(2,1)S(1)} %get-tuple-element.40.grow_ref, f32[4,40,128]{2,1,0:T(8,128)S(1)} %get-tuple-element.35.small_ref, f32[4,1024,128]{2,1,0:T(8,128)S(1)} %get-tuple-element.41.f1_ref), custom_call_target="tpu_custom_call" | custom-call | flops 33554432 | bytes 6291456 | tf_op jit(solution)/shard_map/finals/pallas_call | solution.py:665
  94.1 0.0 collective-permute-done.1.s1_ref
  94.1 0.0 collective-permute-done.2.s2_ref
  94.1 0.3 collective-permute-done.3.s3_ref
  94.4 1.6 %normalise.1 = bf16[1024,1024]{1,0:T(8,128)(2,1)} custom-call(bf16[1024,1024]{1,0:T(8,128)(2,1)S(1)} %get-tuple-element.37.g_ref, f32[8,256]{1,0:T(8,128)S(1)} %add.3.s0_ref, f32[8,256]{1,0:T(8,128)S(1)} %collective-permute-done.1.s1_ref, f32[8,256]{1,0:T(8,128)S(1)} %collective-permute-done.2.s2_ref, f32[8,256]{1,0:T(8,128)S(1)} %collective-permute-done.3.s3_ref, ...), custom_call_target="tpu_custom_call" | custom-call | flops 2097152 | bytes 4194304 | tf_op jit(solution)/shard_map/normalise/pallas_call | solution.py:709
  (8 shorter events, 0.0 us)
Async XLA Ops:
  20.1 4.7 %copy-start.4 = (bf16[4096,16]{0,1:T(8,128)(2,1)S(1)}, bf16[4096,16]{0,1:T(8,128)(2,1)}, u32[]{:S(2)}) copy-start(bf16[4096,16]{0,1:T(8,128)(2,1)} %param.20) | copy-start | bytes 393220
  20.1 6.1 %copy-start.7 = (f32[16]{0:T(128)S(1)}, f32[16]{0:T(128)}, u32[]{:S(2)}) copy-start(f32[16]{0:T(128)} %param.25) | copy-start | bytes 196
  20.1 6.2 %copy-start.5 = (bf16[4,3,256]{2,0,1:T(4,128)(2,1)S(1)}, bf16[4,3,256]{2,0,1:T(4,128)(2,1)}, u32[]{:S(2)}) copy-start(bf16[4,3,256]{2,0,1:T(4,128)(2,1)} %param.29) | copy-start | bytes 18436
  20.1 60.8 %all-to-all-start.1 = ((f32[16,528,128]{2,1,0:T(8,128)}), f32[16,528,128]{2,1,0:T(8,128)}, u32[]{:S(2)}, u32[]{:S(2)}) async-start(f32[16,528,128]{2,1,0:T(8,128)} %pick.1), calls=%async_computation.1 | async-start | bytes 8650752 | tf_op jit(solution)/shard_map/all_to_all | solution.py:750
  26.4 30.6 %copy-start = (bf16[4,1024]{1,0:T(4,128)(2,1)S(1)}, bf16[4,1024]{1,0:T(4,128)(2,1)}, u32[]{:S(2)}) copy-start(bf16[4,1024]{1,0:T(4,128)(2,1)} %ik_ref.1) | copy-start | bytes 24580
  26.4 30.6 %copy-start.1 = (bf16[4,256]{1,0:T(4,128)(2,1)S(1)}, bf16[4,256]{1,0:T(4,128)(2,1)}, u32[]{:S(2)}) copy-start(bf16[4,256]{1,0:T(4,128)(2,1)} %sk_ref.1) | copy-start | bytes 6148
  26.4 30.6 %copy-start.2 = (f32[16]{0:T(128)S(1)}, f32[16]{0:T(128)}, u32[]{:S(2)}) copy-start(f32[16]{0:T(128)} %param.23) | copy-start | bytes 196
  26.4 30.6 %copy-start.3 = (f32[16]{0:T(128)S(1)}, f32[16]{0:T(128)}, u32[]{:S(2)}) copy-start(f32[16]{0:T(128)} %param.24) | copy-start | bytes 196
  81.0 11.4 %copy-start.6 = (bf16[1024]{0:T(1024)(128)(2,1)S(1)}, bf16[1024]{0:T(1024)(128)(2,1)}, u32[]{:S(2)}) copy-start(bf16[1024]{0:T(1024)(128)(2,1)} %param.26) | copy-start | bytes 6148
  85.2 1.3 %collective-permute-start = (f32[8,256]{1,0:T(8,128)S(1)}, f32[8,256]{1,0:T(8,128)S(1)}, u32[]{:S(2)}, u32[]{:S(2)}) collective-permute-start(f32[8,256]{1,0:T(8,128)S(1)} %get-tuple-element.38), channel_id=1, source_target_pairs={{0,1},{1,0},{2,3},{3,2},{4,5},{5,4},{6,7},{7,6},{8,9},{9,8},{10,11... | collective-permute-start | bytes 24584 | tf_op jit(solution)/shard_map/ppermute | solution.py:768
  86.4 7.7 %collective-permute-start.1 = (f32[8,256]{1,0:T(8,128)S(1)}, f32[8,256]{1,0:T(8,128)S(1)}, u32[]{:S(2)}, u32[]{:S(2)}) collective-permute-start(f32[8,256]{1,0:T(8,128)S(1)} %add.3.s0_ref), channel_id=1, source_target_pairs={{0,2},{1,3},{2,4},{3,5},{4,6},{5,7},{6,0},{7,1},{8,10},{9,11},{10,... | collective-permute-start | bytes 24584 | tf_op jit(solution)/shard_map/ppermute | solution.py:770
  88.1 6.0 %collective-permute-start.2 = (f32[8,256]{1,0:T(8,128)S(1)}, f32[8,256]{1,0:T(8,128)S(1)}, u32[]{:S(2)}, u32[]{:S(2)}) collective-permute-start(f32[8,256]{1,0:T(8,128)S(1)} %add.3.s0_ref), channel_id=1, source_target_pairs={{0,4},{1,5},{2,6},{3,7},{4,0},{5,1},{6,2},{7,3},{8,12},{9,13},{10,... | collective-permute-start | bytes 24584 | tf_op jit(solution)/shard_map/ppermute | solution.py:770
  90.7 3.7 %collective-permute-start.3 = (f32[8,256]{1,0:T(8,128)S(1)}, f32[8,256]{1,0:T(8,128)S(1)}, u32[]{:S(2)}, u32[]{:S(2)}) collective-permute-start(f32[8,256]{1,0:T(8,128)S(1)} %add.3.s0_ref), channel_id=1, source_target_pairs={{0,6},{1,7},{2,0},{3,1},{4,2},{5,3},{6,4},{7,5},{8,14},{9,15},{10,... | collective-permute-start | bytes 24584 | tf_op jit(solution)/shard_map/ppermute | solution.py:770

commit v8 on v7

--- a/solution.py
+++ b/solution.py
@@ -130,7 +130,7 @@
     always = CAP // 2
     extra_ref[0] = 0
 
-    @pl.loop(0, owners)
+    @pl.loop(0, owners, unroll=4)
     def _(d):
         for k in range(always):
             pltpu.make_async_copy(
@@ -150,7 +150,7 @@
                     extra_sem,
                 ).start()
 
-    @pl.loop(0, owners)
+    @pl.loop(0, owners, unroll=4)
     def _(d):
         for k in range(CAP):
             at = pl.ds(codes_ref[d, 0, k], 1)

time: 96.3 us -> 96.4 us (level)
  no operation moved by 1% of the time
where the time goes in v8:
time: 96.4 us; the launch traced here: 96.1 us
  Pallas kernels  59.2 us (61%)
  blocking collectives  15.6 us (16%)
  starting transfers between devices  10.5 us (11%)
  waiting for transfers between devices  8.33 us (9%)
  local copies, waits for them, and re-layouts  1.58 us (2%)
    pallas_call x1, Pallas kernels, project(): pl.pallas_call(functools.partial(project_kernel, steps), out_shape=(jax.S...  30.5 us
    pallas_call x1, Pallas kernels, ssd(): pl.pallas_call(ssd_kernel, out_shape=(pltpu.VMEM((tokens, width), BF16),...  17.3 us
    all_to_all x1, blocking collectives, local(): lax.all_to_all(wanted, 'dp', split_axis=0, concat_axis=0, tiled=True)  15.6 us
    all_to_all x1, waiting for transfers between devices, local(): back = lax.all_to_all(sent, 'dp', split_axis=0, concat_axis=0, tiled=True)  6.7 us
    ppermute x3, starting transfers between devices, local(): lax.ppermute(square, 'mp', [(i, (i + 2 * s) % groups) for i in range(grou...  5.71 us
    all_to_all x1, starting transfers between devices, local(): back = lax.all_to_all(sent, 'dp', split_axis=0, concat_axis=0, tiled=True)  4.68 us
    pallas_call x1, Pallas kernels, tail(): pl.pallas_call(tail_kernel, out_shape=(pltpu.VMEM((tokens, width), BF16),...  4.19 us
    pallas_call x1, Pallas kernels, pick(): pl.pallas_call(pick_kernel, out_shape=pltpu.HBM((owners, CAP * p + 2 * CA...  2.15 us
  transfers between devices with their start and end apart: 5, of which 3 were waited for; matrix products, arithmetic and copies ran while one was open for 2% of the time, Pallas kernels for 52%

profile of v8, /device:TPU:0, one launch (start us, length us, event | category | flops | bytes accessed | tf_op | source)
XLA Modules:
  0.0 96.1 jit_solution(13568566259590644797)
XLA Ops:
  0.6 1.8 %prep.1 = (s32[16,1,128]{2,1,0:T(1,128)}, s32[64]{0:T(128)}, f32[48,64,128]{2,1,0:T(8,128)S(1)}, f32[48,128]{1,0:T(8,128)S(1)}, f32[48,128]{1,0:T(8,128)S(1)}) custom-call(s32[4,16]{1,0:T(4,128)} %owner_hbm.1, s32[4,16]{1,0:T(4,128)} %slot_hbm.1, f32[48,64,128]{2,1,0:T(8,128)} %bitcast.6, bf16[48,192]{1,0:T(8,128)(2,1)} %bitcast.7), custom_call_target="tpu_custom_call" | custom-call | tf_op jit(solution)/shard_map/prep/pallas_call | solution.py:101
  2.4 15.6 %all_to_all.10.codes_ref = s32[16,1,128]{2,1,0:T(1,128)S(1)} all-to-all(s32[16,1,128]{2,1,0:T(1,128)} %get-tuple-element.23), channel_id=1, replica_groups=mesh['dp'=16,'mp'=8] {'dp'}, dimensions={0} | all-to-all | bytes 16384 | tf_op jit(solution)/shard_map/all_to_all | solution.py:748
  18.1 2.1 %pick.1 = f32[16,528,128]{2,1,0:T(8,128)} custom-call(s32[16,1,128]{2,1,0:T(1,128)S(1)} %all_to_all.10.codes_ref, f32[48,64,128]{2,1,0:T(8,128)S(1)} %get-tuple-element.24.cache_ref, f32[48,128]{1,0:T(8,128)S(1)} %get-tuple-element.25.wa_ref, f32[48,128]{1,0:T(8,128)S(1)} %get-tuple-element.26.wb_ref), custom_call_target="tpu_custom_call" | custom-call | bytes 8388608 | tf_op jit(solution)/shard_map/pick/pallas_call | solution.py:175
  20.2 0.0 copy-start.4
  20.2 0.0 copy-start.7
  20.2 0.0 copy-start.5
  20.3 4.7 %all-to-all-start.1 = ((f32[16,528,128]{2,1,0:T(8,128)}), f32[16,528,128]{2,1,0:T(8,128)}, u32[]{:S(2)}, u32[]{:S(2)}) async-start(f32[16,528,128]{2,1,0:T(8,128)} %pick.1), calls=%async_computation.1 | async-start | bytes 8650752 | tf_op jit(solution)/shard_map/all_to_all | solution.py:750
  24.9 0.0 copy-done.4
  24.9 1.4 %copy.18.wd_ref = bf16[4096,16]{1,0:T(8,128)(2,1)} copy(bf16[4096,16]{0,1:T(8,128)(2,1)S(1)} %copy-done.4) | data formatting | bytes 262144 | tf_op args[4]
  26.3 0.0 copy-done.7
  26.3 0.1 broadcast_in_dim.14
  26.4 0.1 broadcast_in_dim_reshape.3.skip_ref
  26.5 0.0 copy-done.5
  26.5 0.0 copy-start
  26.5 0.0 copy-start.1
  26.5 0.0 copy-start.2
  26.5 0.0 copy-start.3
  26.5 30.5 %project.1 = (bf16[1024,1024]{1,0:T(8,128)(2,1)}, bf16[1024,1024]{1,0:T(8,128)(2,1)}, bf16[1024,256]{1,0:T(8,128)(2,1)}, f32[1024,16]{1,0:T(8,128)}) custom-call(bf16[1024,4096]{1,0:T(8,128)(2,1)} %act_ref.1, bf16[4096,1024]{1,0:T(8,128)(2,1)} %wi_ref.1, bf16[4096,1024]{1,0:T(8,128)(2,1)} %wg_ref.1, bf16[4096,256]{1,0:T(8,128)(2,1)} %ws_ref.1, ...), custom_call_target="tpu_custom_call" | custom-call | flops 19461570560 | bytes 33554432 | tf_op jit(solution)/shard_map/project/pallas_call | solution.py:232
  57.1 0.0 copy-done
  57.1 17.3 %ssd.1 = (bf16[1024,1024]{1,0:T(8,128)(2,1)S(1)}, bf16[1024,1024]{1,0:T(8,128)(2,1)}, bf16[1024,256]{1,0:T(8,128)(2,1)S(1)}, f32[4,1024,128]{2,1,0:T(8,128)}, f3...) custom-call(bf16[1024,1024]{1,0:T(8,128)(2,1)} %get-tuple-element.27.inner_ref, ...), custom_call_target="tpu_custom_call" | custom-call | flops 1073741824 | bytes 14680064 | tf_op jit(solution)/shard_map/ssd/pallas_call | solution.py:409
  74.4 6.7 %all-to-all-done.1.back_ref = f32[16,528,128]{2,1,0:T(8,128)} async-done(((f32[16,528,128]{2,1,0:T(8,128)}), f32[16,528,128]{2,1,0:T(8,128)}, u32[]{:S(2)}, u32[]{:S(2)}) %all-to-all-start.1) | async-done | bytes 4325408 | tf_op jit(solution)/shard_map/all_to_all | solution.py:750
  81.1 4.2 %tail.1 = (bf16[1024,1024]{1,0:T(8,128)(2,1)S(1)}, f32[8,256]{1,0:T(8,128)S(1)}, bf16[1024,32]{1,0:T(8,128)(2,1)S(1)}, f32[64,64,128]{2,1,0:T(8,128)S(1)}, f32[4,1024,128]{2,1,0:T(8,128)S(1)}) custom-call(s32[64]{0:T(128)} %get-tuple-element.22.pos_hbm, f32[16,528,128]{2,1,0:T(8,128)} %all-to-all-done.1.back_ref, ...), custom_call_target="tpu_custom_call" | custom-call | flops 268435456 | bytes 10485760 | tf_op jit(solution)/shard_map/tail/pallas_call | solution.py:610
  85.3 0.1 collective-permute-start
  85.4 1.2 %collective-permute-done = f32[8,256]{1,0:T(8,128)S(1)} collective-permute-done((f32[8,256]{1,0:T(8,128)S(1)}, f32[8,256]{1,0:T(8,128)S(1)}, u32[]{:S(2)}, u32[]{:S(2)}) %collective-permute-start) | collective-permute-done | bytes 8224 | tf_op jit(solution)/shard_map/ppermute | solution.py:768
  86.6 1.4 %collective-permute-start.1 = (f32[8,256]{1,0:T(8,128)S(1)}, f32[8,256]{1,0:T(8,128)S(1)}, u32[]{:S(2)}, u32[]{:S(2)}) collective-permute-start(f32[8,256]{1,0:T(8,128)S(1)} %add.3.s0_ref), channel_id=1, source_target_pairs={{0,2},{1,3},{2,4},{3,5},{4,6},{5,7},{6,0},{7,1},{8,10},{9,11},{10,... | collective-permute-start | bytes 24584 | tf_op jit(solution)/shard_map/ppermute | solution.py:770
  88.0 2.9 %collective-permute-start.2 = (f32[8,256]{1,0:T(8,128)S(1)}, f32[8,256]{1,0:T(8,128)S(1)}, u32[]{:S(2)}, u32[]{:S(2)}) collective-permute-start(f32[8,256]{1,0:T(8,128)S(1)} %add.3.s0_ref), channel_id=1, source_target_pairs={{0,4},{1,5},{2,6},{3,7},{4,0},{5,1},{6,2},{7,3},{8,12},{9,13},{10,... | collective-permute-start | bytes 24584 | tf_op jit(solution)/shard_map/ppermute | solution.py:770
  90.8 1.5 %collective-permute-start.3 = (f32[8,256]{1,0:T(8,128)S(1)}, f32[8,256]{1,0:T(8,128)S(1)}, u32[]{:S(2)}, u32[]{:S(2)}) collective-permute-start(f32[8,256]{1,0:T(8,128)S(1)} %add.3.s0_ref), channel_id=1, source_target_pairs={{0,6},{1,7},{2,0},{3,1},{4,2},{5,3},{6,4},{7,5},{8,14},{9,15},{10,... | collective-permute-start | bytes 24584 | tf_op jit(solution)/shard_map/ppermute | solution.py:770
  92.3 1.7 %finals.1 = f32[4,16,64,128]{3,2,1,0:T(8,128)} custom-call(f32[64,64,128]{2,1,0:T(8,128)S(1)} %get-tuple-element.39.held_ref, bf16[1024,32]{1,0:T(8,128)(2,1)S(1)} %get-tuple-element.40.grow_ref, f32[4,40,128]{2,1,0:T(8,128)S(1)} %get-tuple-element.35.small_ref, f32[4,1024,128]{2,1,0:T(8,128)S(1)} %get-tuple-element.41.f1_ref), custom_call_target="tpu_custom_call" | custom-call | flops 33554432 | bytes 6291456 | tf_op jit(solution)/shard_map/finals/pallas_call | solution.py:665
  94.0 0.0 collective-permute-done.1.s1_ref
  94.0 0.0 collective-permute-done.2.s2_ref
  94.0 0.5 collective-permute-done.3.s3_ref
  94.5 1.6 %normalise.1 = bf16[1024,1024]{1,0:T(8,128)(2,1)} custom-call(bf16[1024,1024]{1,0:T(8,128)(2,1)S(1)} %get-tuple-element.37.g_ref, f32[8,256]{1,0:T(8,128)S(1)} %add.3.s0_ref, f32[8,256]{1,0:T(8,128)S(1)} %collective-permute-done.1.s1_ref, f32[8,256]{1,0:T(8,128)S(1)} %collective-permute-done.2.s2_ref, f32[8,256]{1,0:T(8,128)S(1)} %collective-permute-done.3.s3_ref, ...), custom_call_target="tpu_custom_call" | custom-call | flops 2097152 | bytes 4194304 | tf_op jit(solution)/shard_map/normalise/pallas_call | solution.py:709
  (8 shorter events, 0.0 us)
Async XLA Ops:
  20.2 4.7 %copy-start.4 = (bf16[4096,16]{0,1:T(8,128)(2,1)S(1)}, bf16[4096,16]{0,1:T(8,128)(2,1)}, u32[]{:S(2)}) copy-start(bf16[4096,16]{0,1:T(8,128)(2,1)} %param.20) | copy-start | bytes 393220
  20.2 6.1 %copy-start.7 = (f32[16]{0:T(128)S(1)}, f32[16]{0:T(128)}, u32[]{:S(2)}) copy-start(f32[16]{0:T(128)} %param.25) | copy-start | bytes 196
  20.2 6.2 %copy-start.5 = (bf16[4,3,256]{2,0,1:T(4,128)(2,1)S(1)}, bf16[4,3,256]{2,0,1:T(4,128)(2,1)}, u32[]{:S(2)}) copy-start(bf16[4,3,256]{2,0,1:T(4,128)(2,1)} %param.29) | copy-start | bytes 18436
  20.3 60.9 %all-to-all-start.1 = ((f32[16,528,128]{2,1,0:T(8,128)}), f32[16,528,128]{2,1,0:T(8,128)}, u32[]{:S(2)}, u32[]{:S(2)}) async-start(f32[16,528,128]{2,1,0:T(8,128)} %pick.1), calls=%async_computation.1 | async-start | bytes 8650752 | tf_op jit(solution)/shard_map/all_to_all | solution.py:750
  26.5 30.6 %copy-start = (bf16[4,1024]{1,0:T(4,128)(2,1)S(1)}, bf16[4,1024]{1,0:T(4,128)(2,1)}, u32[]{:S(2)}) copy-start(bf16[4,1024]{1,0:T(4,128)(2,1)} %ik_ref.1) | copy-start | bytes 24580
  26.5 30.6 %copy-start.1 = (bf16[4,256]{1,0:T(4,128)(2,1)S(1)}, bf16[4,256]{1,0:T(4,128)(2,1)}, u32[]{:S(2)}) copy-start(bf16[4,256]{1,0:T(4,128)(2,1)} %sk_ref.1) | copy-start | bytes 6148
  26.5 30.6 %copy-start.2 = (f32[16]{0:T(128)S(1)}, f32[16]{0:T(128)}, u32[]{:S(2)}) copy-start(f32[16]{0:T(128)} %param.23) | copy-start | bytes 196
  26.5 30.6 %copy-start.3 = (f32[16]{0:T(128)S(1)}, f32[16]{0:T(128)}, u32[]{:S(2)}) copy-start(f32[16]{0:T(128)} %param.24) | copy-start | bytes 196
  81.1 11.2 %copy-start.6 = (bf16[1024]{0:T(1024)(128)(2,1)S(1)}, bf16[1024]{0:T(1024)(128)(2,1)}, u32[]{:S(2)}) copy-start(bf16[1024]{0:T(1024)(128)(2,1)} %param.26) | copy-start | bytes 6148
  85.3 1.3 %collective-permute-start = (f32[8,256]{1,0:T(8,128)S(1)}, f32[8,256]{1,0:T(8,128)S(1)}, u32[]{:S(2)}, u32[]{:S(2)}) collective-permute-start(f32[8,256]{1,0:T(8,128)S(1)} %get-tuple-element.38), channel_id=1, source_target_pairs={{0,1},{1,0},{2,3},{3,2},{4,5},{5,4},{6,7},{7,6},{8,9},{9,8},{10,11... | collective-permute-start | bytes 24584 | tf_op jit(solution)/shard_map/ppermute | solution.py:768
  86.6 7.4 %collective-permute-start.1 = (f32[8,256]{1,0:T(8,128)S(1)}, f32[8,256]{1,0:T(8,128)S(1)}, u32[]{:S(2)}, u32[]{:S(2)}) collective-permute-start(f32[8,256]{1,0:T(8,128)S(1)} %add.3.s0_ref), channel_id=1, source_target_pairs={{0,2},{1,3},{2,4},{3,5},{4,6},{5,7},{6,0},{7,1},{8,10},{9,11},{10,... | collective-permute-start | bytes 24584 | tf_op jit(solution)/shard_map/ppermute | solution.py:770
  88.0 6.0 %collective-permute-start.2 = (f32[8,256]{1,0:T(8,128)S(1)}, f32[8,256]{1,0:T(8,128)S(1)}, u32[]{:S(2)}, u32[]{:S(2)}) collective-permute-start(f32[8,256]{1,0:T(8,128)S(1)} %add.3.s0_ref), channel_id=1, source_target_pairs={{0,4},{1,5},{2,6},{3,7},{4,0},{5,1},{6,2},{7,3},{8,12},{9,13},{10,... | collective-permute-start | bytes 24584 | tf_op jit(solution)/shard_map/ppermute | solution.py:770
  90.8 3.7 %collective-permute-start.3 = (f32[8,256]{1,0:T(8,128)S(1)}, f32[8,256]{1,0:T(8,128)S(1)}, u32[]{:S(2)}, u32[]{:S(2)}) collective-permute-start(f32[8,256]{1,0:T(8,128)S(1)} %add.3.s0_ref), channel_id=1, source_target_pairs={{0,6},{1,7},{2,0},{3,1},{4,2},{5,3},{6,4},{7,5},{8,14},{9,15},{10,... | collective-permute-start | bytes 24584 | tf_op jit(solution)/shard_map/ppermute | solution.py:770
